TPU v7x, 32 devices: a whole 2x2x4 slice. The times are simulated.
32 devices in a mesh: groups: 2 (over y), replica: 4 (over z), tensor: 4 (over x, core).
Axes of the slice: x: 2, y: 2, z: 4, core: 2. Of those that a mesh axis runs over, the one named last changes fastest.
Arguments:
- queries: bfloat16 [2048, 4096], P(('groups', 'replica'), 'tensor'), parts along dimension 0
- fresh_key_value: bfloat16 [2048, 1024], P(('groups', 'replica')), parts along dimension 0, may hold values from -6 to 6
- key_value_cache_blocks: bfloat16 [1024, 16, 1024], P(('groups', 'replica')), parts along dimension 0
- row_block_indices: int32 [2048, 16], P(('groups', 'replica')), parts along dimension 0, may hold values from 0 to 127
- cached_length: int32 [2048], P(('groups', 'replica')), parts along dimension 0, may hold values from 1 to 256
- row_adapter_id: int32 [2048], P(('groups', 'replica')), parts along dimension 0, may hold values from 0 to 7
- adapter_storage_slot: int32 [8], replicated, may hold values from 0 to 7, each once
- leaving_row_indices: int32 [8, 2], P(('groups', 'replica')), parts along dimension 0, may hold values from 0 to 255, as said below
- receiving_replica: int32 [8], P(('groups', 'replica')), parts along dimension 0, may hold values from 0 to 3, each once
- output_weight_matrix: bfloat16 [4096, 8192], P('tensor'), may hold values from -0.09375 to 0.09375
- adapter_down_weight: bfloat16 [8, 4096, 64], P('replica', 'tensor'), may hold values from -0.09375 to 0.09375
- adapter_up_weight: bfloat16 [8, 64, 8192], P('replica', None, 'tensor'), may hold values from -0.75 to 0.75
Outputs:
- mixed: bfloat16 [2048, 8192], P(('groups', 'replica'), 'tensor'), parts along dimension 0
There are 2 independent parts, one for each index of `groups`. A program takes and returns all parts, laid end to end along the dimension named above; an argument that names none is the same for every part. Nothing has to cross between parts.
Inputs may be any that keep to these rules, and one draw needn't show every extreme that they name: `leaving_row_indices`: each replica's 2 entries are distinct.
All inputs are finite; a program needn't handle non-finite values.
Results may differ from a plain program's by a relative error of at most 0.008.
Values may be sent and summed in bfloat16 or wider, within the bound.
No kernel may reach another device: no remote copies, remote signals or barrier semaphores. Data moves between devices by JAX's collectives and lax.ppermute only.
A program may use at most 128 MiB of HBM per device.

v0:
```python
import math

import jax
import jax.numpy as jnp
from jax import lax
from jax.sharding import PartitionSpec as P

QUERY_HEADS_HALF = 32
KVH = 4
HEAD_SIZE = 128


adapter_scale = 2.0


def attend(query_rows, own_rows, cache_rows, lengths):
    count_rows = query_rows.shape[0]
    head_width = own_rows.shape[1] // 2
    head_count = query_rows.shape[1] // head_width
    context = cache_rows.shape[1]
    query_heads = query_rows.reshape(count_rows, head_count, head_width)
    score_scale = 1.0 / math.sqrt(head_width)
    scores = (
        jnp.einsum(
            "nhd,ncd->nhc",
            query_heads,
            cache_rows[:, :, :head_width],
            preferred_element_type=jnp.float32,
        )
        * score_scale
    )
    is_valid = jnp.arange(context, dtype=jnp.int32)[None, :] < lengths[:, None]
    scores = jnp.where(is_valid[:, None, :], scores, -jnp.inf)
    own_score = (
        jnp.einsum(
            "nhd,nd->nh", query_heads, own_rows[:, :head_width], preferred_element_type=jnp.float32
        )
        * score_scale
    )
    row_max = jnp.maximum(jnp.max(scores, axis=2), own_score)
    weights_past = jnp.exp(scores - row_max[:, :, None])
    weight_own = jnp.exp(own_score - row_max)
    denominator = jnp.sum(weights_past, axis=2) + weight_own
    mixed_past = (weights_past / denominator[:, :, None]).astype(jnp.bfloat16)
    mixed_own = (weight_own / denominator).astype(jnp.bfloat16)
    result = jnp.einsum(
        "nhc,ncd->nhd",
        mixed_past,
        cache_rows[:, :, head_width:],
        preferred_element_type=jnp.float32,
    )
    result = result + mixed_own.astype(jnp.float32)[:, :, None] * own_rows[
        :, None, head_width:
    ].astype(jnp.float32)
    return result.reshape(count_rows, head_count * head_width).astype(jnp.bfloat16)


def on_device(
    queries,
    fresh_key_value,
    key_value_cache_blocks,
    row_block_indices,
    cached_length,
    row_adapter_id,
    adapter_storage_slot,
    leaving_row_indices,
    receiving_replica,
    output_weight_matrix,
    adapter_down_weight,
    adapter_up_weight,
):
    count_rows = queries.shape[0]
    heads_here = queries.shape[1] // HEAD_SIZE
    group_heads = QUERY_HEADS_HALF // KVH
    leaving = leaving_row_indices[0]
    count_moved = leaving.shape[0]
    replica_here = lax.axis_index("replica")
    kv_head = lax.axis_index("tensor") * heads_here // group_heads
    own_pool = lax.dynamic_slice_in_dim(
        key_value_cache_blocks, kv_head * 2 * HEAD_SIZE, 2 * HEAD_SIZE, 2
    )
    own_new = lax.dynamic_slice_in_dim(fresh_key_value, kv_head * 2 * HEAD_SIZE, 2 * HEAD_SIZE, 1)
    cache_all = own_pool[row_block_indices].reshape(count_rows, -1, 2 * HEAD_SIZE)
    lengths_out = cached_length[leaving]
    adapters_out = row_adapter_id[leaving]
    meta_lengths, meta_adapters, meta_dest = (
        lax.all_gather(lengths_out, "replica", axis=0, tiled=True),
        lax.all_gather(adapters_out, "replica", axis=0, tiled=True),
        lax.all_gather(receiving_replica, "replica", axis=0, tiled=True),
    )
    source_id = jnp.sum(
        jnp.where(meta_dest == replica_here, jnp.arange(meta_dest.shape[0], dtype=jnp.int32), 0)
    )
    in_lengths = lax.dynamic_slice_in_dim(meta_lengths, source_id * count_moved, count_moved)
    in_adapters = lax.dynamic_slice_in_dim(meta_adapters, source_id * count_moved, count_moved)
    payload = (queries[leaving], own_new[leaving], cache_all[leaving])
    empty_payload = tuple((jnp.zeros_like(member) for member in payload))
    arrived = (
        lax.all_gather(payload[0], "replica", axis=0, tiled=True),
        lax.all_gather(payload[1], "replica", axis=0, tiled=True),
        lax.all_gather(payload[2], "replica", axis=0, tiled=True),
    )
    members = arrived[0].shape[0] // count_moved
    owner_ids = jnp.arange(members, dtype=jnp.int32)
    matched = owner_ids == source_id
    updated = []
    for held_sum, member in zip(empty_payload, arrived):
        shaped = member.reshape((members, count_moved) + member.shape[1:])
        hit_mask = matched.reshape((members,) + (1,) * (shaped.ndim - 1))
        updated.append(jnp.sum(jnp.where(hit_mask, shaped, jnp.zeros_like(shaped)), axis=0))
    in_queries, in_own, in_cache = tuple(updated)
    attn = attend(
        queries.at[leaving].set(in_queries),
        own_new.at[leaving].set(in_own),
        cache_all.at[leaving].set(in_cache),
        cached_length.at[leaving].set(in_lengths),
    )
    catalog = adapter_storage_slot.shape[0]
    matches = (
        row_adapter_id.at[leaving].set(in_adapters)[:, None]
        == jnp.arange(catalog, dtype=jnp.int32)[None, :]
    )
    storage_slot_index = jnp.sum(jnp.where(matches, adapter_storage_slot[None, :], 0), axis=1)
    adapter_rank_width = adapter_down_weight.shape[2]
    output_columns = adapter_up_weight.shape[2]
    down_projection_part = lax.all_gather(adapter_down_weight, "replica", axis=0, tiled=True)
    up_projection_part = lax.all_gather(adapter_up_weight, "replica", axis=0, tiled=True)
    piece_slots = down_projection_part.shape[0]
    hit_piece = storage_slot_index[:, None] == jnp.arange(piece_slots, dtype=jnp.int32)[None, :]
    products = jnp.einsum(
        "nc,kcr->nkr", attn, down_projection_part, preferred_element_type=jnp.float32
    )
    shrink_part = jnp.sum(jnp.where(hit_piece[:, :, None], products, 0.0), axis=1)
    up_tables = up_projection_part
    shrink_part, up_tables = (shrink_part, up_tables)
    shrunk = lax.psum(shrink_part, "tensor").astype(jnp.bfloat16)
    slot_hits = storage_slot_index[:, None] == jnp.arange(catalog, dtype=jnp.int32)[None, :]
    spread = jnp.where(
        slot_hits[:, :, None], shrunk[:, None, :], jnp.zeros((), jnp.bfloat16)
    ).reshape(count_rows, catalog * adapter_rank_width)
    adapter_update = jnp.dot(
        spread,
        up_tables.reshape(catalog * adapter_rank_width, output_columns),
        preferred_element_type=jnp.float32,
    )
    partial_sum = jnp.dot(attn, output_weight_matrix, preferred_element_type=jnp.float32)
    frozen_projection_sum = lax.psum_scatter(partial_sum, "tensor", scatter_dimension=1, tiled=True)
    return (frozen_projection_sum + adapter_scale * adapter_update).astype(jnp.bfloat16)


def solution(mesh):
    return jax.shard_map(
        on_device,
        mesh=mesh,
        in_specs=(
            P(("groups", "replica"), "tensor"),
            P(("groups", "replica"), None),
            P(("groups", "replica"), None, None),
            P(("groups", "replica"), None),
            P(("groups", "replica")),
            P(("groups", "replica")),
            P(),
            P(("groups", "replica"), None),
            P(("groups", "replica")),
            P("tensor", None),
            P("replica", "tensor", None),
            P("replica", None, "tensor"),
        ),
        out_specs=P(("groups", "replica"), "tensor"),
        check_vma=False,
    )
```

profile of v0, /device:TPU:0, one launch (start us, length us, event | category | flops | bytes accessed | tf_op | source)
XLA Modules:
  0.0 241.8 jit_solution(1923249917280243149)
XLA Ops:
  6.5 0.7 copy.57
  8.0 1.0 copy.56
  9.0 0.7 compare_select_fusion
  10.6 1.3 constant_dynamic-slice_fusion.1
  11.9 37.2 %gather_fusion.2 = bf16[4096,16,256]{2,1,0:T(8,128)(2,1)} fusion(bf16[128,16,256]{2,1,0:T(8,128)(2,1)S(1)} %constant_dynamic-slice_fusion.1, s32[4096]{0:T(1024)S(1)} %broadcast_clamp_fusion), kind=kCustom, calls=%fused_computation.2 | custom fusion | bytes 67125248 | tf_op jit(solution)/shard_map/gather | solution.py:83
  49.1 2.2 gather_fusion.3
  51.4 0.7 all-gather.11.cloned.1.call-update
  56.5 0.7 dynamic-update-slice.1
  57.2 9.9 %all-reduce.3 = (s32[4]{0:T(128)S(1)}, s32[8]{0:T(128)S(1)}, s32[8]{0:T(128)S(1)}) all-reduce(s32[4]{0:T(128)S(1)} %dynamic-update-slice.1, s32[8]{0:T(128)S(1)} %dynamic-update-slice, s32[8]{0:T(128)S(1)} %dynamic-update-slice.2), channel_id=1, replica_groups=mesh['groups'=2,'replica'=4,'tensor'=4] {'replica'}, use_global_device_ids=true, to_apply=%add.1 | all-reduce | flops 20 | bytes 160
  70.4 13.3 %all-gather.5 = bf16[4,2,1024]{2,1,0:T(2,128)(2,1)S(1)} all-gather(bf16[1,2,1024]{2,1,0:T(2,128)(2,1)S(1)} %bitcast.63), channel_id=3, replica_groups=mesh['groups'=2,'replica'=4,'tensor'=4] {'replica'}, dimensions={0}, use_global_device_ids=true | all-gather | bytes 20480 | tf_op jit(solution)/shard_map/all_gather | solution.py:99
  83.8 1.0 scatter_fusion.1
  85.5 9.2 %all-gather.6 = bf16[4,2,256]{2,1,0:T(2,128)(2,1)S(1)} all-gather(bf16[1,2,256]{2,1,0:T(2,128)(2,1)S(1)} %bitcast.64), channel_id=5, replica_groups=mesh['groups'=2,'replica'=4,'tensor'=4] {'replica'}, dimensions={0}, use_global_device_ids=true | all-gather | bytes 5120 | tf_op jit(solution)/shard_map/all_gather | solution.py:100
  94.8 0.7 scatter_fusion.3
  96.0 1.5 select_reduce_fusion
  97.5 2.2 scatter_fusion.2
  99.8 8.2 %fusion.7 = (f32[256,8]{1,0:T(8,128)S(1)}, f32[256,8,256]{2,1,0:T(8,128)S(1)}) fusion(pred[256,256]{1,0:T(8,128)(4,1)S(1)} %iota_compare_fusion, bf16[256,8,128]{2,1,0:T(8,128)(2,1)S(1)} %bitcast.59, bf16[256,256,256]{2,1,0:T(8,128)(2,1)} %scatter_fusion.2), kind=kOutput, calls=%fused_computation.22 | convolution fusion | flops 135788544 | bytes 19472384 | tf_op jit(solution)/shard_map/nhd,ncd->nhc/dot_general | solution.py:24
  108.2 1.0 fusion.8
  109.6 7.2 %fusion.12 = bf16[256,8,128]{2,1,0:T(8,128)(2,1)S(1)} fusion(bf16[256,256,256]{2,1,0:T(8,128)(2,1)} %scatter_fusion.2, f32[256,8,256]{2,1,0:T(8,128)S(1)} %get-tuple-element.13, f32[256,8]{1,0:T(8,128)S(1)} %copy.24, f32[256,8]{1,0:T(8,128)S(1)} %copy.22, pred[256,256]{1,0:T(8,128)(4,1)S(1)} %iota_compare_fusion, f32[256,128]{1,0:T(8,128)S(1)} %get-tuple-element.8, ...), kind=kOutput, calls=%fused_computation.25 | convolution fusion | flops 137625600 | bytes 19619840 | tf_op jit(solution)/shard_map/nhc,ncd->nhd/dot_general | solution.py:46
  116.8 13.0 %fusion.22 = f32[256,8192]{1,0:T(8,128)} fusion(bf16[1024,8192]{1,0:T(8,128)(2,1)} %param.21, bf16[32,8,8,128]{3,2,1,0:T(8,128)(2,1)S(1)} %bitcast.55), kind=kOutput, calls=%fused_computation.34 | convolution fusion | flops 4294967296 | bytes 25690112 | tf_op jit(solution)/shard_map/dot_general | solution.py:146
  130.7 1.7 fusion.20
  132.4 11.6 %psum.7 = bf16[256,64]{0,1:T(8,128)(2,1)S(1)} all-reduce(f32[256,64]{0,1:T(8,128)S(1)} %select_reduce_fusion.1), channel_id=1, replica_groups=mesh['groups'=2,'replica'=4,'tensor'=4] {'tensor'}, use_global_device_ids=true, to_apply=%region_14.15 | all-reduce | flops 16384 | bytes 98304 | tf_op jit(solution)/shard_map/psum | solution.py:136
  144.0 14.4 %all-gather.13.cloned.1.call-done = bf16[8,64,2048]{2,1,0:T(8,128)(2,1)} async-done(((bf16[2,64,2048]{2,1,0:T(8,128)(2,1)}), bf16[8,64,2048]{2,1,0:T(8,128)(2,1)}) %all-gather.13.cloned.1.call-update) | async-done | bytes 2097168 | tf_op jit(solution)/shard_map/all_gather | solution.py:127
  158.5 72.9 %reduce-scatter.2.cloned.1.call-done = f32[256,2048]{1,0:T(8,128)} async-done(((f32[256,8192]{1,0:T(8,128)}), f32[256,2048]{1,0:T(8,128)}) %reduce-scatter.2.cloned.1.call-update) | async-done | bytes 2097168 | tf_op jit(solution)/shard_map/reduce_scatter | solution.py:147
  231.4 3.9 %fusion.6 = bf16[256,2048]{1,0:T(8,128)(2,1)} fusion(f32[256,2048]{1,0:T(8,128)} %reduce-scatter.2.cloned.1.call-done, bf16[8,64,2048]{2,1,0:T(8,128)(2,1)} %all-gather.13.cloned.1.call-done, pred[256,8]{0,1:T(8,128)(4,1)S(1)} %iota_compare_fusion.1, bf16[256,64]{0,1:T(8,128)(2,1)S(1)} %psum.7), kind=kOutput, calls=%fused_computation.18 | convolution fusion | flops 538574848 | bytes 5277696 | tf_op jit(solution)/shard_map/dot_general | solution.py:141
  (57 shorter events, 10.0 us)
Async XLA Ops:
  6.5 78.3 %copy-start = (bf16[256,1024]{1,0:T(8,128)(2,1)S(1)}, bf16[256,1024]{1,0:T(8,128)(2,1)}, u32[]{:S(2)}) copy-start(bf16[256,1024]{1,0:T(8,128)(2,1)} %param.13) | copy-start | bytes 1572868
  6.5 89.5 %all-gather.15.cloned.1.call-start = ((), (), s32[]{:S(2)}) async-start(), calls=%async_computation.4 | async-start | bytes 1310720 | tf_op jit(solution)/shard_map/all_gather | solution.py:101
  49.1 5.7 %copy-start.3 = (u32[32]{0:T(128)S(1)}, u32[32]{0:T(128)}, u32[]{:S(2)}) copy-start(u32[32]{0:T(128)} %constant.60) | copy-start | bytes 388
  51.3 79.3 %all-gather.11.cloned.1.call-start = ((), (), s32[]{:S(2)}) async-start(), calls=%async_computation.2 | async-start | bytes 1310720 | tf_op jit(solution)/shard_map/all_gather | solution.py:126
  52.1 106.4 %all-gather.13.cloned.1.call-start = ((), (), s32[]{:S(2)}) async-start(), calls=%async_computation.3 | async-start | bytes 2621440 | tf_op jit(solution)/shard_map/all_gather | solution.py:127
  52.8 178.5 %reduce-scatter.2.cloned.1.call-start = ((), (), s32[]{:S(2)}) async-start(), calls=%async_computation.1 | async-start | bytes 10485760 | tf_op jit(solution)/shard_map/reduce_scatter | solution.py:147
  129.8 0.7 copy-start.2
  132.4 102.9 %copy-start.1 = (bf16[256,1024]{1,0:T(8,128)(2,1)S(1)}, bf16[256,1024]{1,0:T(8,128)(2,1)}, u32[]{:S(2)}) copy-start(bf16[256,1024]{1,0:T(8,128)(2,1)} %param.13) | copy-start | bytes 1572868
Sparse Core Ops, SparseCore 0:
  51.5 31.3 all-gather.14
  84.4 26.9 all-gather.10
  113.0 45.4 all-gather.12
  160.9 70.4 reduce-scatter.1
where the time goes:
time: 242 us
  waiting for transfers between devices  88.7 us (37%)
  local copies, waits for them, and re-layouts  53.5 us (22%)
  blocking collectives  44 us (18%)
  matrix products  34.5 us (14%)
  between operations  15.3 us (6%)
  other arithmetic  5.67 us (2%)
    reduce_scatter x1, waiting for transfers between devices, on_device(): lax.psum_scatter(partial_sum, 'tensor', scatter_dimension=1, tiled=True)  72.9 us
    gather x1, local copies, waits for them, and re-layouts, on_device(): own_pool[row_block_indices].reshape(count_rows, -1, 2 * HEAD_SIZE)  37.2 us
    all_gather x1, waiting for transfers between devices, on_device(): lax.all_gather(adapter_up_weight, 'replica', axis=0, tiled=True)  14.4 us
    all_gather x1, blocking collectives, on_device(): lax.all_gather(payload[0], 'replica', axis=0, tiled=True)  13.3 us
    dot_general x1, matrix products, on_device(): jnp.dot(attn, output_weight_matrix, preferred_element_type=jnp.float32)  13 us
    psum x1, blocking collectives, on_device(): shrunk = lax.psum(shrink_part, 'tensor').astype(jnp.bfloat16)  11.6 us
    unnamed x1, blocking collectives  9.93 us
    all_gather x1, blocking collectives, on_device(): lax.all_gather(payload[1], 'replica', axis=0, tiled=True)  9.23 us
  transfers between devices with their start and end apart: 4, of which 2 were waited for; matrix products, arithmetic and copies ran while one was open for 19% of the time, Pallas kernels for 0%

commit v1 on v0

v1 whole, which is shorter than its diff:
```python
import functools
import math

import jax
import jax.numpy as jnp
from jax import lax
from jax.experimental import pallas as pl
from jax.experimental.pallas import tpu as pltpu
from jax.sharding import PartitionSpec as P

QUERY_HEADS_HALF = 32
KVH = 4
HEAD_SIZE = 128
ADAPTER_SCALE = 2.0
PAD = 16
IDS = 128
VMEM_LIMIT = 60 * 1024 * 1024
BF16 = jnp.bfloat16
F32 = jnp.float32
ANY = pl.BlockSpec(memory_space=pl.ANY)
VMEM = pl.BlockSpec(memory_space=pltpu.VMEM)
SMEM = pl.BlockSpec(memory_space=pltpu.SMEM)


def call(body, out_shape, in_specs, scratch, name, args, cost=None):
    return pl.pallas_call(
        body,
        out_shape=out_shape,
        in_specs=in_specs,
        out_specs=[VMEM] * len(out_shape),
        scratch_shapes=scratch,
        compiler_params=pltpu.CompilerParams(vmem_limit_bytes=VMEM_LIMIT),
        cost_estimate=cost,
        name=name,
    )(*args)


def down_rows(lane_row):
    return jnp.broadcast_to(lane_row, (128, lane_row.shape[1])).T


def attend(q_of, own, idx, lens, pool_ref, kt_ref, vx_ref, bias_ref, s_ref, heads, store):
    rows = own.shape[0]
    D = HEAD_SIZE
    nblk, bs, _ = pool_ref.shape
    npos = nblk * bs
    nslot = idx.shape[0]
    scale = math.log2(math.e) / math.sqrt(D)
    pool = pool_ref[...].reshape(npos, 2 * D)
    kt_ref[...] = pool[:, :D].T
    vx_ref[:, :D] = pool[:, D:]
    vx_ref[:, D:] = jnp.ones((npos, D), BF16)
    nfull = jnp.floor(lens * (1.0 / bs))
    rem = lens - nfull * bs
    block = lax.broadcasted_iota(jnp.int32, (nblk, rows), 0).astype(F32)
    full = jnp.zeros((nblk, rows), F32)
    some = jnp.zeros((nblk, rows), F32)
    for j in range(nslot):
        hit = idx[j : j + 1, :] == block
        full += jnp.where(hit & (nfull > j), 1.0, 0.0)
        some += jnp.where(hit & (lens > j * bs), 1.0, 0.0)
    full = full.astype(BF16)
    some = some.astype(BF16)
    pad = -rows % 128
    rem_row = jnp.concatenate([rem, jnp.zeros((1, pad), F32)], 1) if pad else rem
    rem_col = down_rows(rem_row)[:rows]
    width = 512
    offset = (lax.broadcasted_iota(jnp.int32, (rows, 128), 1) % bs).astype(F32)
    partial = jnp.concatenate([offset < rem_col] * (width // 128), 1)
    over_rows = (((0,), (0,)), ((), ()))
    for w in range(0, npos, width):
        spot = lax.broadcasted_iota(jnp.int32, (nblk, width), 1) + w
        here = spot // bs == lax.broadcasted_iota(jnp.int32, (nblk, width), 0)
        spread = jnp.where(here, 1.0, 0.0).astype(BF16)
        count_full = lax.dot_general(full, spread, over_rows, preferred_element_type=F32)
        count_some = lax.dot_general(some, spread, over_rows, preferred_element_type=F32)
        count = jnp.where(partial, count_some, count_full)
        bias_ref[:, w : w + width] = jnp.where(
            count > 0.5, jnp.log2(jnp.maximum(count, 1.0)), -jnp.inf
        )
    own = own.astype(F32)
    own_k, own_v = own[:, :D], own[:, D:]
    for h in range(heads):
        q = q_of(h)
        top = None
        for w in range(0, npos, width):
            s = jnp.dot(q, kt_ref[:, w : w + width], preferred_element_type=F32)
            s = s * scale + bias_ref[:, w : w + width]
            s_ref[h % 2, :, w : w + width] = s
            for lane in range(0, width, 128):
                part = s[:, lane : lane + 128]
                top = part if top is None else jnp.maximum(top, part)
        own_s = jnp.sum(q.astype(F32) * own_k, axis=1, keepdims=True) * scale
        m = jnp.maximum(jnp.max(top, axis=1, keepdims=True), own_s)
        acc = jnp.zeros((rows, 2 * D), F32)
        for w in range(0, npos, width):
            p = jnp.exp2(s_ref[h % 2, :, w : w + width] - m).astype(BF16)
            acc += jnp.dot(p, vx_ref[w : w + width, :], preferred_element_type=F32)
        own_w = jnp.exp2(own_s - m)
        out = (acc[:, :D] + own_w * own_v) / (acc[:, D : D + 1] + own_w)
        store(h, out.astype(BF16))


def weight_copies(w_ref, held, sems, blocks):
    width = held.shape[2]
    out = []
    for i, block in enumerate(blocks):
        start = pl.multiple_of(block * width, width)
        out.append(pltpu.make_async_copy(w_ref.at[:, pl.ds(start, width)], held.at[i], sems.at[i]))
    return out


def chip_blocks(t, chips):
    chip, core = t // 2, t % 2
    out = []
    for d in range(1, chips):
        at = 2 * lax.rem(chip + d, chips)
        out += [at + 1 - core, at + core]
    return out


def first_kernel(n1, chips, members, sc_ref, leave_ref, recv_ref, q_ref, fresh_ref, idx_ref, len_ref, id_ref,
                 pool_ref, w_ref, attn_ref, send_ref, keep_ref, *rest):
    pays = rest[:members]
    pool, own_all, kt, vx, bias, s, aug_q, held, psem, wsem = rest[members:]
    t, z, kv = sc_ref[0], sc_ref[1], sc_ref[2]
    D = HEAD_SIZE
    kv_at = pl.multiple_of(kv * 2 * D, 2 * D)
    pool_copy = pltpu.make_async_copy(pool_ref.at[:, :, pl.ds(kv_at, 2 * D)], pool, psem.at[0])
    own_copy = pltpu.make_async_copy(fresh_ref.at[:, pl.ds(kv_at, 2 * D)], own_all, psem.at[1])
    own_copy.start()
    pool_copy.start()
    copies = weight_copies(w_ref, held, wsem, chip_blocks(t, chips))
    for c in copies:
        c.start()
    rows, channels = q_ref.shape
    moved = leave_ref.shape[1]
    heads = channels // D
    lane = lax.broadcasted_iota(jnp.int32, (PAD, rows), 1)
    row = lax.broadcasted_iota(jnp.int32, (PAD, rows), 0)
    pick = jnp.zeros((PAD, rows), jnp.bool_)
    for j in range(moved):
        pick = pick | ((row == j) & (lane == leave_ref[0, j]))
    pick = jnp.where(pick, 1.0, 0.0).astype(BF16)
    aug_q[:n1, :] = q_ref[:n1, :]
    aug_q[n1:, :] = jnp.dot(pick, q_ref[...], preferred_element_type=F32).astype(BF16)
    idx = idx_ref[...].astype(F32)
    lens = len_ref[...].astype(F32)
    ids = id_ref[...].astype(F32)
    both = jnp.concatenate([idx, jnp.broadcast_to(lens, (8, rows)), jnp.broadcast_to(ids, (8, rows))], 0)
    nt = (((1,), (1,)), ((), ()))
    out_of = lax.dot_general(both.astype(BF16), pick, nt, preferred_element_type=F32)
    ns = idx.shape[0]
    idx = jnp.concatenate([idx[:, :n1], out_of[:ns]], 1)
    lens = jnp.concatenate([lens[:, :n1], out_of[ns : ns + 1]], 1)
    id_col = lax.dot_general(pick, jnp.broadcast_to(ids, (128, rows)).astype(BF16), nt, preferred_element_type=F32)
    own_copy.wait()
    own = jnp.concatenate(
        [own_all[:n1, :], jnp.dot(pick, own_all[...], preferred_element_type=F32).astype(BF16)], 0
    )
    pool_copy.wait()
    left = []

    def store(h, out):
        attn_ref[:, h * D : (h + 1) * D] = out[:n1]
        left.append(out[n1:])

    attend(lambda h: aug_q[:, h * D : (h + 1) * D], own, idx, lens, pool, kt, vx, bias, s, heads, store)
    width = held.shape[2]
    a = attn_ref[...]
    for i, c in enumerate(copies):
        c.wait()
        ref = (send_ref, keep_ref)[i % 2]
        at = (i // 2) * width
        ref[:, at : at + width] = jnp.dot(a, held[i], preferred_element_type=F32).astype(BF16)
    left = jnp.concatenate(left + [id_col[:, :IDS].astype(BF16)], 1)
    mask_row = lax.broadcasted_iota(jnp.int32, left.shape, 0) < moved
    for k in range(members):
        mine = recv_ref[0] == lax.rem(z + k, members)
        pays[k][...] = jnp.where(mask_row & mine, left, jnp.zeros_like(left))


def second_kernel(n1, sc_ref, q_ref, fresh_ref, idx_ref, len_ref, pool_ref, attn_ref,
                  pool, own_all, kt, vx, bias, s, psem):
    kv = sc_ref[2]
    D = HEAD_SIZE
    kv_at = pl.multiple_of(kv * 2 * D, 2 * D)
    pool_copy = pltpu.make_async_copy(pool_ref.at[:, :, pl.ds(kv_at, 2 * D)], pool, psem.at[0])
    own_copy = pltpu.make_async_copy(fresh_ref.at[:, pl.ds(kv_at, 2 * D)], own_all, psem.at[1])
    own_copy.start()
    pool_copy.start()
    heads = q_ref.shape[1] // D
    own_copy.wait()
    pool_copy.wait()

    def store(h, out):
        attn_ref[:, h * D : (h + 1) * D] = out

    attend(lambda h: q_ref[n1:, h * D : (h + 1) * D], own_all[n1:, :], idx_ref[:, n1:].astype(F32),
           len_ref[:, n1:].astype(F32), pool, kt, vx, bias, s, heads, store)


def project_kernel(chips, members, sc_ref, attn_ref, w_ref, *rest):
    pays, (full_ref, arr_ref, send_ref, keep_ref, held, wsem) = rest[:members], rest[members:]
    copies = weight_copies(w_ref, held, wsem, chip_blocks(sc_ref[0], chips))
    for c in copies:
        c.start()
    arr = pays[0][...]
    for p in pays[1:]:
        arr = arr + p[...]
    arr_ref[...] = arr
    n, channels = attn_ref.shape
    full_ref[:n, :] = attn_ref[...]
    full_ref[n:, :] = arr[:, :channels]
    width = held.shape[2]
    a = full_ref[...]
    for i, c in enumerate(copies):
        c.wait()
        ref = (send_ref, keep_ref)[i % 2]
        at = (i // 2) * width
        ref[:, at : at + width] = jnp.dot(a, held[i], preferred_element_type=F32).astype(BF16)


def own_kernel(sc_ref, a1_ref, a2_ref, w_ref, send_ref, own_ref, held, wsem):
    t = sc_ref[0]
    core = t % 2
    copies = weight_copies(w_ref, held, wsem, [t + 1 - 2 * core, t])
    for c in copies:
        c.start()
    n1 = a1_ref.shape[0]
    for i, (c, ref) in enumerate(zip(copies, (send_ref, own_ref))):
        c.wait()
        for a, rows in ((a1_ref, slice(0, n1)), (a2_ref, slice(n1, None))):
            ref[rows, :] = jnp.dot(a[...], held[i], preferred_element_type=F32).astype(ref.dtype)


def shrink_kernel(members, groups, sc_ref, slots_ref, a1_ref, a2_ref, id_ref, arr_ref, own_down, *rest):
    same, swapped = rest[: members - 1], rest[members - 1 : 2 * (members - 1)]
    shr_ref, slot_ref = rest[2 * (members - 1) :]
    z, y = sc_ref[1], sc_ref[3]
    n1, channels = a1_ref.shape
    ids = down_rows(id_ref[...].astype(F32))
    ids = jnp.concatenate([ids, jnp.broadcast_to(arr_ref[:, channels : channels + 1].astype(F32), (PAD, 128))], 0)
    slot = jnp.zeros_like(ids)
    for a in range(slots_ref.shape[0]):
        slot = jnp.where(ids == a, slots_ref[a].astype(F32), slot)
    slot_ref[...] = slot
    nt = (((1,), (1,)), ((), ()))
    pieces = [(own_down[g], z * groups + g) for g in range(groups)]
    for k in range(1, members):
        layer = lax.rem(z + members - k, members) * groups
        pieces.append((same[k - 1][...], layer + y))
        pieces.append((swapped[k - 1][...], layer + 1 - y))
    rank = own_down.shape[1]
    for a, lo, hi in ((a1_ref, 0, n1), (a2_ref, n1, slot.shape[0])):
        total = jnp.zeros((hi - lo, 2 * rank), F32)
        for i in range(0, len(pieces), 2):
            table = jnp.concatenate([pieces[i][0], pieces[i + 1][0]], 0)
            part = lax.dot_general(a[...], table, nt, preferred_element_type=F32)
            left = lax.broadcasted_iota(jnp.int32, part.shape, 1) < rank
            at = jnp.where(left, pieces[i][1].astype(F32), pieces[i + 1][1].astype(F32))
            total += jnp.where(slot[lo:hi, : 2 * rank] == at, part, 0.0)
        shr_ref[lo:hi, :] = total[:, :rank] + total[:, rank:]


def final_kernel(members, groups, chips, sc_ref, leave_ref, shr_ref, slot_ref, own_ref, recv_ref, own_up, *rest):
    same, swapped = rest[: members - 1], rest[members - 1 : 2 * (members - 1)]
    rest = rest[2 * (members - 1) :]
    shr_in, rest = rest[: chips - 1], rest[chips - 1 :]
    x1, x2 = rest[: chips - 1], rest[chips - 1 : 2 * (chips - 1)]
    out_ref = rest[2 * (chips - 1)]
    z, y = sc_ref[1], sc_ref[3]
    shrunk = shr_ref[...]
    for r in shr_in:
        shrunk = shrunk + r[...].astype(F32)
    shrunk = shrunk.astype(BF16).astype(F32)
    rank = own_up.shape[1]
    wide = jnp.concatenate([shrunk, shrunk], 1)
    slot = slot_ref[:, : 2 * rank]
    pieces = [(own_up[g], z * groups + g) for g in range(groups)]
    for k in range(1, members):
        layer = lax.rem(z + members - k, members) * groups
        pieces.append((same[k - 1][...], layer + y))
        pieces.append((swapped[k - 1][...], layer + 1 - y))
    left = lax.broadcasted_iota(jnp.int32, wide.shape, 1) < rank
    delta = None
    for i in range(0, len(pieces), 2):
        at = jnp.where(left, pieces[i][1].astype(F32), pieces[i + 1][1].astype(F32))
        spread = jnp.where(slot == at, wide, 0.0).astype(BF16)
        table = jnp.concatenate([pieces[i][0], pieces[i + 1][0]], 0)
        part = jnp.dot(spread, table, preferred_element_type=F32)
        delta = part if delta is None else delta + part
    base = own_ref[...] + recv_ref[...].astype(F32)
    for a, b in zip(x1, x2):
        base = base + jnp.concatenate([a[...], b[...]], 0).astype(F32)
    result = base + ADAPTER_SCALE * delta
    rows = out_ref.shape[0]
    moved = leave_ref.shape[1]
    row = lax.broadcasted_iota(jnp.int32, out_ref.shape, 0)
    out = result[:rows]
    for j in range(moved):
        out = jnp.where(row == leave_ref[0, j], result[rows + j : rows + j + 1], out)
    out_ref[...] = out.astype(BF16)


def add_kernel(a_ref, b_ref, o_ref):
    o_ref[...] = (a_ref[...].astype(F32) + b_ref[...].astype(F32)).astype(o_ref.dtype)


def after(value, *others):
    return lax.optimization_barrier((value,) + others)[0]


def on_device(mesh_shape, queries, fresh, pool, table, lengths, adapter_id, storage_slot, leaving, receiving,
              w, down, up):
    members, tensors, groups = mesh_shape["replica"], mesh_shape["tensor"], mesh_shape["groups"]
    chips = tensors // 2
    rows, channels = queries.shape
    heads = channels // HEAD_SIZE
    nblk, bs, _ = pool.shape
    npos = nblk * bs
    cols = w.shape[1] // tensors
    rank = down.shape[2]
    n1 = rows // 2
    n2 = rows - n1
    t = lax.axis_index("tensor")
    z = lax.axis_index("replica")
    y = lax.axis_index("groups")
    kv = t * heads // (QUERY_HEADS_HALF // KVH)
    sc = jnp.stack([t, z, kv, y]).astype(jnp.int32)
    idx_t = table.T
    len_row = lengths[None, :]
    id_row = adapter_id[None, :]
    down_t = jnp.swapaxes(down, 1, 2)

    def shift(v, k):
        return lax.ppermute(v, "replica", [(i, (i + k) % members) for i in range(members)])

    def swap(v):
        return lax.ppermute(v, "groups", [(0, 1), (1, 0)])

    def core(v):
        return lax.ppermute(v, "tensor", [(i, i ^ 1) for i in range(tensors)])

    def chip(v, d):
        return lax.ppermute(v, "tensor", [(i, (i + 2 * d) % tensors) for i in range(tensors)])

    mine_down = lax.dynamic_index_in_dim(down_t, y, 0, keepdims=False)
    mine_up = lax.dynamic_index_in_dim(up, y, 0, keepdims=False)
    down_same = [shift(mine_down, k) for k in range(1, members)]

    sds = jax.ShapeDtypeStruct
    dma = pltpu.SemaphoreType.DMA
    far = (chips - 1) * cols
    aug = n1 + PAD
    attn_scratch = lambda n: [
        pltpu.VMEM((HEAD_SIZE, npos), BF16),
        pltpu.VMEM((npos, 2 * HEAD_SIZE), BF16),
        pltpu.VMEM((n, npos), F32),
        pltpu.VMEM((2, n, npos), F32),
    ]
    pool_scratch = [pltpu.VMEM((nblk, bs, 2 * HEAD_SIZE), BF16), pltpu.VMEM((rows, 2 * HEAD_SIZE), BF16)]
    far_scratch = [pltpu.VMEM((2 * (chips - 1), channels, cols), BF16)]
    out1 = call(
        functools.partial(first_kernel, n1, chips, members),
        [sds((n1, channels), BF16), sds((n1, far), BF16), sds((n1, far), BF16)]
        + [sds((PAD, channels + IDS), BF16)] * members,
        [SMEM, SMEM, SMEM, VMEM, ANY, VMEM, VMEM, VMEM, ANY, ANY],
        pool_scratch + attn_scratch(aug) + [pltpu.VMEM((aug, channels), BF16)] + far_scratch
        + [dma((2,)), dma((2 * (chips - 1),))],
        "attend_and_project_first_rows",
        (sc, leaving, receiving, queries, fresh, idx_t, len_row, id_row, pool, w),
    )
    attn1, send1, keep1 = out1[:3]
    pays = out1[3:]

    def reduce_far(send, keep):
        got = core(send)
        total = call(add_kernel, [sds(keep.shape, BF16)], [VMEM, VMEM], [], "add_partner_core", (keep, got))[0]
        return [chip(total[:, (d - 1) * cols : d * cols] if chips > 2 else total, d) for d in range(1, chips)]

    x1 = reduce_far(send1, keep1)
    arrived = [pays[0]] + [shift(pays[k], k) for k in range(1, members)]
    up_from = after(mine_up, attn1)
    up_same = [shift(up_from, k) for k in range(1, members)]
    down_swapped = [swap(v) for v in down_same]

    (attn2,) = call(
        functools.partial(second_kernel, n1),
        [sds((n2, channels), BF16)],
        [SMEM, VMEM, ANY, VMEM, VMEM, ANY],
        pool_scratch + attn_scratch(n2) + [dma((2,))],
        "attend_second_rows",
        (sc, after(queries, attn1), fresh, idx_t, len_row, pool),
    )
    full2, arr, send2, keep2 = call(
        functools.partial(project_kernel, chips, members),
        [sds((n2 + PAD, channels), BF16), sds((PAD, channels + IDS), BF16), sds((n2 + PAD, far), BF16),
         sds((n2 + PAD, far), BF16)],
        [SMEM, VMEM, ANY] + [VMEM] * members,
        far_scratch + [dma((2 * (chips - 1),))],
        "project_second_rows",
        (sc, attn2, w, *arrived),
    )
    x2 = reduce_far(send2, keep2)
    total_rows = rows + PAD
    send3, own = call(
        own_kernel,
        [sds((total_rows, cols), BF16), sds((total_rows, cols), F32)],
        [SMEM, VMEM, VMEM, ANY],
        [pltpu.VMEM((2, channels, cols), BF16), dma((2,))],
        "project_own_columns",
        (sc, attn1, after(full2, send2), w),
    )
    recv3 = core(send3)
    shr, slot = call(
        functools.partial(shrink_kernel, members, groups),
        [sds((total_rows, rank), F32), sds((total_rows, 128), F32)],
        [SMEM, SMEM, VMEM, VMEM, VMEM, VMEM, VMEM] + [VMEM] * (2 * (members - 1)),
        [],
        "shrink",
        (sc, storage_slot, attn1, full2, id_row, arr, down_t, *down_same, *down_swapped),
    )
    shr = shr + core(shr)
    shr16 = shr.astype(BF16)
    shr_in = [chip(shr16, d) for d in range(1, chips)]
    up_swapped = [swap(v) for v in up_same]

    tile = min(cols, 512)
    col = lambda n: pl.BlockSpec((n, tile), lambda i: (0, i))
    fixed = lambda *shape: pl.BlockSpec(shape, lambda i: (0,) * len(shape))
    return pl.pallas_call(
        functools.partial(final_kernel, members, groups, chips),
        grid=(cols // tile,),
        out_shape=sds((rows, cols), BF16),
        in_specs=[SMEM, SMEM, fixed(total_rows, rank), fixed(total_rows, 128), col(total_rows), col(total_rows),
                  pl.BlockSpec((groups, rank, tile), lambda i: (0, 0, i))]
        + [col(rank)] * (2 * (members - 1)) + [fixed(total_rows, rank)] * (chips - 1)
        + [col(n1)] * (chips - 1) + [col(n2 + PAD)] * (chips - 1),
        out_specs=col(rows),
        compiler_params=pltpu.CompilerParams(vmem_limit_bytes=VMEM_LIMIT),
        name="combine",
    )(sc, leaving, shr, slot, own, recv3, up, *up_same, *up_swapped, *shr_in, *x1, *x2)


def solution(mesh):
    return jax.shard_map(
        functools.partial(on_device, dict(mesh.shape)),
        mesh=mesh,
        in_specs=(
            P(("groups", "replica"), "tensor"),
            P(("groups", "replica"), None),
            P(("groups", "replica"), None, None),
            P(("groups", "replica"), None),
            P(("groups", "replica")),
            P(("groups", "replica")),
            P(),
            P(("groups", "replica"), None),
            P(("groups", "replica")),
            P("tensor", None),
            P("replica", "tensor", None),
            P("replica", None, "tensor"),
        ),
        out_specs=P(("groups", "replica"), "tensor"),
        check_vma=False,
    )
```

time: 242 us -> 111 us (0.46)
  waiting for transfers between devices: 88.7 us -> 37.3 us
  local copies, waits for them, and re-layouts: 53.5 us -> 3.77 us
  Pallas kernels: 0 us -> 44.5 us
  blocking collectives: 44 us -> 0 us
  matrix products: 34.5 us -> 0 us
  starting transfers between devices: 0.12 us -> 22.9 us
  between operations: 15.3 us -> 1.05 us
  other arithmetic: 5.67 us -> 1.25 us
    reduce_scatter x1 -> x0, waiting for transfers between devices: 72.9 us -> none  [on_device(): lax.psum_scatter(partial_sum, 'tensor', scatter_dimension=1, tiled=True)]
    pallas_call x0 -> x8, Pallas kernels: none -> 44.5 us  [the longest x7 38.5 us: call(): pl.pallas_call(body, out_shape=out_shape, in_specs=in_specs, out_specs=[V...]
    gather x6 -> x0, local copies, waits for them, and re-layouts: 41.8 us -> none  [the longest x1 37.2 us: on_device(): own_pool[row_block_indices].reshape(count_rows, -1, 2 * HEAD_SIZE)]
    ppermute x0 -> x22, waiting for transfers between devices: none -> 37.3 us  [the longest x6 15.9 us: swap(): return lax.ppermute(v, 'groups', [(0, 1), (1, 0)])]
    dot_general x5 -> x0, matrix products: 32.8 us -> none  [the longest x1 13 us: on_device(): jnp.dot(attn, output_weight_matrix, preferred_element_type=jnp.float32)]
    ppermute x0 -> x22, starting transfers between devices: none -> 22.9 us  [the longest x9 12.9 us: shift(): lax.ppermute(v, 'replica', [(i, (i + k) % members) for i in range(members)])]
    all_gather x2 -> x0, blocking collectives: 22.5 us -> none  [the longest x1 13.3 us: on_device(): lax.all_gather(payload[0], 'replica', axis=0, tiled=True)]
    all_gather x3 -> x0, waiting for transfers between devices: 14.4 us -> none  [the longest x1 14.4 us: on_device(): lax.all_gather(adapter_up_weight, 'replica', axis=0, tiled=True)]
  transfers between devices with their start and end apart: 4 -> 22, of which waited for: 2 -> 9; matrix products, arithmetic and copies ran while one was open for 19% -> 1% of each run, Pallas kernels for 0% -> 35%
where the time goes in v1:
time: 111 us
  Pallas kernels  44.5 us (40%)
  waiting for transfers between devices  37.3 us (34%)
  starting transfers between devices  22.9 us (21%)
  local copies, waits for them, and re-layouts  3.77 us (3%)
  other arithmetic  1.25 us (1%)
    pallas_call x7, Pallas kernels, call(): pl.pallas_call(body, out_shape=out_shape, in_specs=in_specs, out_specs=[V...  38.5 us
    ppermute x6, waiting for transfers between devices, swap(): return lax.ppermute(v, 'groups', [(0, 1), (1, 0)])  15.9 us
    ppermute x9, starting transfers between devices, shift(): lax.ppermute(v, 'replica', [(i, (i + k) % members) for i in range(members)])  12.9 us
    ppermute x3, waiting for transfers between devices, chip(): lax.ppermute(v, 'tensor', [(i, (i + 2 * d) % tensors) for i in range(tens...  12.2 us
    ppermute x9, waiting for transfers between devices, shift(): lax.ppermute(v, 'replica', [(i, (i + k) % members) for i in range(members)])  9.16 us
    ppermute x6, starting transfers between devices, swap(): return lax.ppermute(v, 'groups', [(0, 1), (1, 0)])  6.08 us
    pallas_call x1, Pallas kernels, on_device(): pl.pallas_call(functools.partial(final_kernel, members, groups, chips), g...  6.02 us
    ppermute x3, starting transfers between devices, chip(): lax.ppermute(v, 'tensor', [(i, (i + 2 * d) % tensors) for i in range(tens...  3.18 us
  transfers between devices with their start and end apart: 22, of which 9 were waited for; matrix products, arithmetic and copies ran while one was open for 1% of the time, Pallas kernels for 35%

profile of v1, /device:TPU:0, one launch (start us, length us, event | category | flops | bytes accessed | tf_op | source)
XLA Modules:
  0.0 110.9 jit_solution(15013773586055967779)
XLA Ops:
  0.9 3.1 %collective-permute-start.3 = (bf16[64,1024]{1,0:T(8,128)(2,1)S(1)}, bf16[64,1024]{1,0:T(8,128)(2,1)S(1)}, u32[]{:S(2)}, u32[]{:S(2)}) collective-permute-start(bf16[64,1024]{1,0:T(8,128)(2,1)S(1)} %dynamic-slice_bitcast_fusion.1), channel_id=1, source_target_pairs={{0,4},{4,8},{8,12},{12,0},{1,5},{5,9},{9,13},{13,1},{2,6},{6,10},{... | collective-permute-start | bytes 393224 | tf_op jit(solution)/shard_map/ppermute | solution.py:337
  5.2 10.7 %attend_and_project_first_rows.1 = (bf16[128,1024]{1,0:T(8,128)(2,1)}, bf16[128,2048]{1,0:T(8,128)(2,1)}, bf16[128,2048]{1,0:T(8,128)(2,1)}, bf16[16,1152]{1,0:T...) custom-call(s32[4]{0:T(128)} %pad_add_fusion.sc_ref, ...), custom_call_target="tpu_custom_call" | custom-call | tf_op jit(solution)/shard_map/attend_and_project_first_rows/pallas_call | solution.py:26
  15.9 1.6 %collective-permute-start = (bf16[16,1152]{1,0:T(8,128)(2,1)}, bf16[16,1152]{1,0:T(8,128)(2,1)S(1)}, u32[]{:S(2)}, u32[]{:S(2)}) collective-permute-start(bf16[16,1152]{1,0:T(8,128)(2,1)} %get-tuple-element.26), channel_id=1, source_target_pairs={{0,4},{4,8},{8,12},{12,0},{1,5},{5,9},{9,13},{13,1},{2,6},{6,10},{... | collective-permute-start | bytes 110600 | tf_op jit(solution)/shard_map/ppermute | solution.py:337
  18.6 2.8 %collective-permute-start.2 = (bf16[16,1152]{1,0:T(8,128)(2,1)}, bf16[16,1152]{1,0:T(8,128)(2,1)S(1)}, u32[]{:S(2)}, u32[]{:S(2)}) collective-permute-start(bf16[16,1152]{1,0:T(8,128)(2,1)} %get-tuple-element.28), channel_id=1, source_target_pairs={{0,12},{4,0},{8,4},{12,8},{1,13},{5,1},{9,5},{13,9},{2,14},{6,2},{... | collective-permute-start | bytes 110600 | tf_op jit(solution)/shard_map/ppermute | solution.py:337
  23.0 1.7 %collective-permute-start.6 = (bf16[64,1024]{1,0:T(8,128)(2,1)S(1)}, bf16[64,1024]{1,0:T(8,128)(2,1)S(1)}, u32[]{:S(2)}, u32[]{:S(2)}) collective-permute-start(bf16[64,1024]{1,0:T(8,128)(2,1)S(1)} %collective-permute-done.3.rest_0_), channel_id=1, source_target_pairs={{0,16},{16,0},{1,17},{17,1},{2,18},{18,2},{3,19},{19,3},{4,20},{20... | collective-permute-start | bytes 393224 | tf_op jit(solution)/shard_map/ppermute | solution.py:340
  24.7 7.1 %attend_second_rows.1.attn_ref = bf16[128,1024]{1,0:T(8,128)(2,1)} custom-call(s32[4]{0:T(128)} %pad_add_fusion.sc_ref, bf16[256,1024]{1,0:T(8,128)(2,1)} %q_ref.2, bf16[256,1024]{1,0:T(8,128)(2,1)} %fresh_ref.3, s32[16,256]{1,0:T(8,128)} %bitcast.16, s32[1,256]{1,0:T(1,128)} %bitcast.18, bf16[128,16,1024]{2,1,0:T(8,128)(2,1)} %pool_ref.3), custom_call_target="tpu_custom_call" | custom-call | tf_op jit(solution)/shard_map/attend_second_rows/pallas_call | solution.py:26
  32.5 6.1 %project_second_rows.1 = (bf16[144,1024]{1,0:T(8,128)(2,1)}, bf16[16,1152]{1,0:T(8,128)(2,1)}, bf16[144,2048]{1,0:T(8,128)(2,1)}, bf16[144,2048]{1,0:T(8,128)(2,1)}) custom-call(s32[4]{0:T(128)} %pad_add_fusion.sc_ref, bf16[128,1024]{1,0:T(8,128)(2,1)} %attend_second_rows.1.attn_ref, bf16[1024,8192]{1,0:T(8,128)(2,1)} %w_ref.5, ...), custom_call_target="tpu_custom_call" | custom-call | tf_op jit(solution)/shard_map/project_second_rows/pallas_call | solution.py:26
  38.7 7.4 %project_own_columns.1 = (bf16[272,2048]{1,0:T(8,128)(2,1)}, f32[272,2048]{1,0:T(8,128)}) custom-call(s32[4]{0:T(128)} %pad_add_fusion.sc_ref, bf16[128,1024]{1,0:T(8,128)(2,1)} %get-tuple-element.23.a1_ref, bf16[144,1024]{1,0:T(8,128)(2,1)} %get-tuple-element.34.a2_ref, bf16[1024,8192]{1,0:T(8,128)(2,1)} %w_ref.5), custom_call_target="tpu_custom_call" | custom-call | tf_op jit(solution)/shard_map/project_own_columns/pallas_call | solution.py:26
  47.1 1.7 %collective-permute-start.8 = (bf16[64,1024]{1,0:T(8,128)(2,1)S(1)}, bf16[64,1024]{1,0:T(8,128)(2,1)S(1)}, u32[]{:S(2)}, u32[]{:S(2)}) collective-permute-start(bf16[64,1024]{1,0:T(8,128)(2,1)S(1)} %collective-permute-done.5.rest_2_), channel_id=1, source_target_pairs={{0,16},{16,0},{1,17},{17,1},{2,18},{18,2},{3,19},{19,3},{4,20},{20... | collective-permute-start | bytes 393224 | tf_op jit(solution)/shard_map/ppermute | solution.py:340
  48.8 4.4 %collective-permute-done.7.rest_4_ = bf16[64,1024]{1,0:T(8,128)(2,1)} collective-permute-done((bf16[64,1024]{1,0:T(8,128)(2,1)S(1)}, bf16[64,1024]{1,0:T(8,128)(2,1)}, u32[]{:S(2)}, u32[]{:S(2)}) %collective-permute-start.7) | collective-permute-done | bytes 131104 | tf_op jit(solution)/shard_map/ppermute | solution.py:340
  55.4 1.3 %collective-permute-start.12 = (bf16[64,2048]{1,0:T(8,128)(2,1)S(1)}, bf16[64,2048]{1,0:T(8,128)(2,1)S(1)}, u32[]{:S(2)}, u32[]{:S(2)}) collective-permute-start(bf16[64,2048]{1,0:T(8,128)(2,1)S(1)} %dynamic-slice_bitcast_fusion), channel_id=1, source_target_pairs={{0,8},{4,12},{8,0},{12,4},{1,9},{5,13},{9,1},{13,5},{2,10},{6,14},... | collective-permute-start | bytes 786440 | tf_op jit(solution)/shard_map/ppermute | solution.py:337
  56.7 2.9 %shrink.1 = (f32[272,64]{1,0:T(8,128)}, f32[272,128]{1,0:T(8,128)}) custom-call(s32[4]{0:T(128)} %pad_add_fusion.sc_ref, s32[8]{0:T(128)} %slots_ref.1, bf16[128,1024]{1,0:T(8,128)(2,1)} %get-tuple-element.23.a1_ref, bf16[144,1024]{1,0:T(8,128)(2,1)} %get-tuple-element.34.a2_ref, s32[1,256]{1,0:T(1,128)} %bitcast.20, ...), custom_call_target="tpu_custom_call" | custom-call | tf_op jit(solution)/shard_map/shrink/pallas_call | solution.py:26
  60.4 2.2 %add_partner_core.3 = bf16[144,2048]{1,0:T(8,128)(2,1)} custom-call(bf16[144,2048]{1,0:T(8,128)(2,1)} %get-tuple-element.40.a_ref, bf16[144,2048]{1,0:T(8,128)(2,1)} %copy-done.2), custom_call_target="tpu_custom_call" | custom-call | tf_op jit(solution)/shard_map/add_partner_core/pallas_call | solution.py:26
  62.7 1.6 %collective-permute-done.11.rest_0_ = bf16[64,2048]{1,0:T(8,128)(2,1)S(1)} collective-permute-done((bf16[64,2048]{1,0:T(8,128)(2,1)S(1)}, bf16[64,2048]{1,0:T(8,128)(2,1)S(1)}, u32[]{:S(2)}, u32[]{:S(2)}) %collective-permute-start.11) | collective-permute-done | bytes 262176 | tf_op jit(solution)/shard_map/ppermute | solution.py:337
  64.3 1.5 %collective-permute-start.21 = (bf16[144,2048]{1,0:T(8,128)(2,1)}, bf16[144,2048]{1,0:T(8,128)(2,1)S(1)}, u32[]{:S(2)}, u32[]{:S(2)}) collective-permute-start(bf16[144,2048]{1,0:T(8,128)(2,1)} %add_partner_core.3), channel_id=1, source_target_pairs={{0,2},{1,3},{2,0},{3,1},{4,6},{5,7},{6,4},{7,5},{8,10},{9,11},{10,... | collective-permute-start | bytes 1769480 | tf_op jit(solution)/shard_map/ppermute | solution.py:346
  66.5 2.1 %add_partner_core.2 = bf16[128,2048]{1,0:T(8,128)(2,1)} custom-call(bf16[128,2048]{1,0:T(8,128)(2,1)} %get-tuple-element.38.a_ref, bf16[128,2048]{1,0:T(8,128)(2,1)} %copy-done.4), custom_call_target="tpu_custom_call" | custom-call | tf_op jit(solution)/shard_map/add_partner_core/pallas_call | solution.py:26
  68.7 5.0 %collective-permute-done.12.rest_1_ = bf16[64,2048]{1,0:T(8,128)(2,1)S(1)} collective-permute-done((bf16[64,2048]{1,0:T(8,128)(2,1)S(1)}, bf16[64,2048]{1,0:T(8,128)(2,1)S(1)}, u32[]{:S(2)}, u32[]{:S(2)}) %collective-permute-start.12) | collective-permute-done | bytes 262176 | tf_op jit(solution)/shard_map/ppermute | solution.py:337
  74.0 1.6 %collective-permute-start.19 = (bf16[128,2048]{1,0:T(8,128)(2,1)}, bf16[128,2048]{1,0:T(8,128)(2,1)S(1)}, u32[]{:S(2)}, u32[]{:S(2)}) collective-permute-start(bf16[128,2048]{1,0:T(8,128)(2,1)} %add_partner_core.2), channel_id=1, source_target_pairs={{0,2},{1,3},{2,0},{3,1},{4,6},{5,7},{6,4},{7,5},{8,10},{9,11},{10,... | collective-permute-start | bytes 1572872 | tf_op jit(solution)/shard_map/ppermute | solution.py:346
  76.4 2.0 %collective-permute-done.13.rest_2_ = bf16[64,2048]{1,0:T(8,128)(2,1)S(1)} collective-permute-done((bf16[64,2048]{1,0:T(8,128)(2,1)S(1)}, bf16[64,2048]{1,0:T(8,128)(2,1)S(1)}, u32[]{:S(2)}, u32[]{:S(2)}) %collective-permute-start.13) | collective-permute-done | bytes 262176 | tf_op jit(solution)/shard_map/ppermute | solution.py:337
  78.4 12.2 %collective-permute-done.17.rest_6_ = bf16[272,64]{1,0:T(8,128)(2,1)S(1)} collective-permute-done((bf16[272,64]{1,0:T(8,128)(2,1)S(1)}, bf16[272,64]{1,0:T(8,128)(2,1)S(1)}, u32[]{:S(2)}, u32[]{:S(2)}) %collective-permute-start.17) | collective-permute-done | bytes 34848 | tf_op jit(solution)/shard_map/ppermute | solution.py:346
  91.1 1.5 %collective-permute-start.16 = (bf16[64,2048]{1,0:T(8,128)(2,1)S(1)}, bf16[64,2048]{1,0:T(8,128)(2,1)S(1)}, u32[]{:S(2)}, u32[]{:S(2)}) collective-permute-start(bf16[64,2048]{1,0:T(8,128)(2,1)S(1)} %collective-permute-done.13.rest_2_), channel_id=1, source_target_pairs={{0,16},{16,0},{1,17},{17,1},{2,18},{18,2},{3,19},{19,3},{4,20},{20... | collective-permute-start | bytes 786440 | tf_op jit(solution)/shard_map/ppermute | solution.py:340
  92.7 7.2 %collective-permute-done.15.rest_4_ = bf16[64,2048]{1,0:T(8,128)(2,1)S(1)} collective-permute-done((bf16[64,2048]{1,0:T(8,128)(2,1)S(1)}, bf16[64,2048]{1,0:T(8,128)(2,1)S(1)}, u32[]{:S(2)}, u32[]{:S(2)}) %collective-permute-start.15) | collective-permute-done | bytes 262176 | tf_op jit(solution)/shard_map/ppermute | solution.py:340
  99.9 3.4 %collective-permute-done.16.rest_5_ = bf16[64,2048]{1,0:T(8,128)(2,1)S(1)} collective-permute-done((bf16[64,2048]{1,0:T(8,128)(2,1)S(1)}, bf16[64,2048]{1,0:T(8,128)(2,1)S(1)}, u32[]{:S(2)}, u32[]{:S(2)}) %collective-permute-start.16) | collective-permute-done | bytes 262176 | tf_op jit(solution)/shard_map/ppermute | solution.py:340
  104.7 6.0 %combine.1 = bf16[256,2048]{1,0:T(8,128)(2,1)} custom-call(s32[4]{0:T(128)} %pad_add_fusion.sc_ref, s32[1,2]{1,0:T(1,128)} %leave_ref.3, f32[272,64]{1,0:T(8,128)} %get-tuple-element.42.shr_ref, f32[272,128]{1,0:T(8,128)} %get-tuple-element.32.slot_ref, f32[272,2048]{1,0:T(8,128)} %get-tuple-element.35.own_ref, bf16[272,2048]{1,0:T(8,128)(2,1)} %copy-done.1, ...), custom_call_target="tpu_custom_call" | custom-call | tf_op jit(solution)/shard_map/combine/pallas_call | solution.py:432
  (76 shorter events, 12.7 us)
Async XLA Ops:
  0.9 22.1 %collective-permute-start.3 = (bf16[64,1024]{1,0:T(8,128)(2,1)S(1)}, bf16[64,1024]{1,0:T(8,128)(2,1)S(1)}, u32[]{:S(2)}, u32[]{:S(2)}) collective-permute-start(bf16[64,1024]{1,0:T(8,128)(2,1)S(1)} %dynamic-slice_bitcast_fusion.1), channel_id=1, source_target_pairs={{0,4},{4,8},{8,12},{12,0},{1,5},{5,9},{9,13},{13,1},{2,6},{6,10},{... | collective-permute-start | bytes 393224 | tf_op jit(solution)/shard_map/ppermute | solution.py:337
  15.9 6.5 %collective-permute-start = (bf16[16,1152]{1,0:T(8,128)(2,1)}, bf16[16,1152]{1,0:T(8,128)(2,1)S(1)}, u32[]{:S(2)}, u32[]{:S(2)}) collective-permute-start(bf16[16,1152]{1,0:T(8,128)(2,1)} %get-tuple-element.26), channel_id=1, source_target_pairs={{0,4},{4,8},{8,12},{12,0},{1,5},{5,9},{9,13},{13,1},{2,6},{6,10},{... | collective-permute-start | bytes 110600 | tf_op jit(solution)/shard_map/ppermute | solution.py:337
  17.5 14.3 %collective-permute-start.1 = (bf16[16,1152]{1,0:T(8,128)(2,1)}, bf16[16,1152]{1,0:T(8,128)(2,1)S(1)}, u32[]{:S(2)}, u32[]{:S(2)}) collective-permute-start(bf16[16,1152]{1,0:T(8,128)(2,1)} %get-tuple-element.27), channel_id=1, source_target_pairs={{0,8},{4,12},{8,0},{12,4},{1,9},{5,13},{9,1},{13,5},{2,10},{6,14},... | collective-permute-start | bytes 110600 | tf_op jit(solution)/shard_map/ppermute | solution.py:337
  18.6 13.2 %collective-permute-start.2 = (bf16[16,1152]{1,0:T(8,128)(2,1)}, bf16[16,1152]{1,0:T(8,128)(2,1)S(1)}, u32[]{:S(2)}, u32[]{:S(2)}) collective-permute-start(bf16[16,1152]{1,0:T(8,128)(2,1)} %get-tuple-element.28), channel_id=1, source_target_pairs={{0,12},{4,0},{8,4},{12,8},{1,13},{5,1},{9,5},{13,9},{2,14},{6,2},{... | collective-permute-start | bytes 110600 | tf_op jit(solution)/shard_map/ppermute | solution.py:337
  21.5 25.1 %collective-permute-start.4 = (bf16[64,1024]{1,0:T(8,128)(2,1)S(1)}, bf16[64,1024]{1,0:T(8,128)(2,1)S(1)}, u32[]{:S(2)}, u32[]{:S(2)}) collective-permute-start(bf16[64,1024]{1,0:T(8,128)(2,1)S(1)} %dynamic-slice_bitcast_fusion.1), channel_id=1, source_target_pairs={{0,8},{4,12},{8,0},{12,4},{1,9},{5,13},{9,1},{13,5},{2,10},{6,14},... | collective-permute-start | bytes 393224 | tf_op jit(solution)/shard_map/ppermute | solution.py:337
  22.4 24.3 %collective-permute-start.5 = (bf16[64,1024]{1,0:T(8,128)(2,1)S(1)}, bf16[64,1024]{1,0:T(8,128)(2,1)S(1)}, u32[]{:S(2)}, u32[]{:S(2)}) collective-permute-start(bf16[64,1024]{1,0:T(8,128)(2,1)S(1)} %dynamic-slice_bitcast_fusion.1), channel_id=1, source_target_pairs={{0,12},{4,0},{8,4},{12,8},{1,13},{5,1},{9,5},{13,9},{2,14},{6,2},{... | collective-permute-start | bytes 393224 | tf_op jit(solution)/shard_map/ppermute | solution.py:337
  23.0 24.1 %collective-permute-start.6 = (bf16[64,1024]{1,0:T(8,128)(2,1)S(1)}, bf16[64,1024]{1,0:T(8,128)(2,1)S(1)}, u32[]{:S(2)}, u32[]{:S(2)}) collective-permute-start(bf16[64,1024]{1,0:T(8,128)(2,1)S(1)} %collective-permute-done.3.rest_0_), channel_id=1, source_target_pairs={{0,16},{16,0},{1,17},{17,1},{2,18},{18,2},{3,19},{19,3},{4,20},{20... | collective-permute-start | bytes 393224 | tf_op jit(solution)/shard_map/ppermute | solution.py:340
  38.6 21.0 %collective-permute-start.20 = (bf16[144,2048]{1,0:T(8,128)(2,1)}, bf16[144,2048]{1,0:T(8,128)(2,1)S(1)}, u32[]{:S(2)}, u32[]{:S(2)}) collective-permute-start(bf16[144,2048]{1,0:T(8,128)(2,1)} %get-tuple-element.33), channel_id=1, source_target_pairs={{0,1},{1,0},{2,3},{3,2},{4,5},{5,4},{6,7},{7,6},{8,9},{9,8},{10,11... | collective-permute-start | bytes 1769480 | tf_op jit(solution)/shard_map/ppermute | solution.py:343
  46.0 57.2 %collective-permute-start.10 = (bf16[272,2048]{1,0:T(8,128)(2,1)}, bf16[272,2048]{1,0:T(8,128)(2,1)S(1)}, u32[]{:S(2)}, u32[]{:S(2)}) collective-permute-start(bf16[272,2048]{1,0:T(8,128)(2,1)} %get-tuple-element.36), channel_id=1, source_target_pairs={{0,1},{1,0},{2,3},{3,2},{4,5},{5,4},{6,7},{7,6},{8,9},{9,8},{10,11... | collective-permute-start | bytes 3342344 | tf_op jit(solution)/shard_map/ppermute | solution.py:343
  46.6 19.1 %collective-permute-start.18 = (bf16[128,2048]{1,0:T(8,128)(2,1)}, bf16[128,2048]{1,0:T(8,128)(2,1)S(1)}, u32[]{:S(2)}, u32[]{:S(2)}) collective-permute-start(bf16[128,2048]{1,0:T(8,128)(2,1)} %get-tuple-element.39), channel_id=1, source_target_pairs={{0,1},{1,0},{2,3},{3,2},{4,5},{5,4},{6,7},{7,6},{8,9},{9,8},{10,11... | collective-permute-start | bytes 1572872 | tf_op jit(solution)/shard_map/ppermute | solution.py:343
  46.7 6.4 %collective-permute-start.7 = (bf16[64,1024]{1,0:T(8,128)(2,1)S(1)}, bf16[64,1024]{1,0:T(8,128)(2,1)}, u32[]{:S(2)}, u32[]{:S(2)}) collective-permute-start(bf16[64,1024]{1,0:T(8,128)(2,1)S(1)} %collective-permute-done.4.rest_1_), channel_id=1, source_target_pairs={{0,16},{16,0},{1,17},{17,1},{2,18},{18,2},{3,19},{19,3},{4,20},{20... | collective-permute-start | bytes 393224 | tf_op jit(solution)/shard_map/ppermute | solution.py:340
  47.1 8.3 %collective-permute-start.8 = (bf16[64,1024]{1,0:T(8,128)(2,1)S(1)}, bf16[64,1024]{1,0:T(8,128)(2,1)S(1)}, u32[]{:S(2)}, u32[]{:S(2)}) collective-permute-start(bf16[64,1024]{1,0:T(8,128)(2,1)S(1)} %collective-permute-done.5.rest_2_), channel_id=1, source_target_pairs={{0,16},{16,0},{1,17},{17,1},{2,18},{18,2},{3,19},{19,3},{4,20},{20... | collective-permute-start | bytes 393224 | tf_op jit(solution)/shard_map/ppermute | solution.py:340
  53.1 11.1 %collective-permute-start.11 = (bf16[64,2048]{1,0:T(8,128)(2,1)S(1)}, bf16[64,2048]{1,0:T(8,128)(2,1)S(1)}, u32[]{:S(2)}, u32[]{:S(2)}) collective-permute-start(bf16[64,2048]{1,0:T(8,128)(2,1)S(1)} %dynamic-slice_bitcast_fusion), channel_id=1, source_target_pairs={{0,4},{4,8},{8,12},{12,0},{1,5},{5,9},{9,13},{13,1},{2,6},{6,10},{... | collective-permute-start | bytes 786440 | tf_op jit(solution)/shard_map/ppermute | solution.py:337
  55.4 18.3 %collective-permute-start.12 = (bf16[64,2048]{1,0:T(8,128)(2,1)S(1)}, bf16[64,2048]{1,0:T(8,128)(2,1)S(1)}, u32[]{:S(2)}, u32[]{:S(2)}) collective-permute-start(bf16[64,2048]{1,0:T(8,128)(2,1)S(1)} %dynamic-slice_bitcast_fusion), channel_id=1, source_target_pairs={{0,8},{4,12},{8,0},{12,4},{1,9},{5,13},{9,1},{13,5},{2,10},{6,14},... | collective-permute-start | bytes 786440 | tf_op jit(solution)/shard_map/ppermute | solution.py:337
  59.6 14.4 %collective-permute-start.9 = (f32[272,64]{1,0:T(8,128)}, f32[272,64]{1,0:T(8,128)S(1)}, u32[]{:S(2)}, u32[]{:S(2)}) collective-permute-start(f32[272,64]{1,0:T(8,128)} %get-tuple-element.31), channel_id=1, source_target_pairs={{0,1},{1,0},{2,3},{3,2},{4,5},{5,4},{6,7},{7,6},{8,9},{9,8},{10,11... | collective-permute-start | bytes 208904 | tf_op jit(solution)/shard_map/ppermute | solution.py:343
  64.3 39.0 %copy-start.6 = (bf16[64,2048]{1,0:T(8,128)(2,1)}, bf16[64,2048]{1,0:T(8,128)(2,1)S(1)}, u32[]{:S(2)}) copy-start(bf16[64,2048]{1,0:T(8,128)(2,1)S(1)} %collective-permute-done.11.rest_0_) | copy-start | bytes 786436
  64.3 39.0 %collective-permute-start.21 = (bf16[144,2048]{1,0:T(8,128)(2,1)}, bf16[144,2048]{1,0:T(8,128)(2,1)S(1)}, u32[]{:S(2)}, u32[]{:S(2)}) collective-permute-start(bf16[144,2048]{1,0:T(8,128)(2,1)} %add_partner_core.3), channel_id=1, source_target_pairs={{0,2},{1,3},{2,0},{3,1},{4,6},{5,7},{6,4},{7,5},{8,10},{9,11},{10,... | collective-permute-start | bytes 1769480 | tf_op jit(solution)/shard_map/ppermute | solution.py:346
  65.8 12.6 %collective-permute-start.13 = (bf16[64,2048]{1,0:T(8,128)(2,1)S(1)}, bf16[64,2048]{1,0:T(8,128)(2,1)S(1)}, u32[]{:S(2)}, u32[]{:S(2)}) collective-permute-start(bf16[64,2048]{1,0:T(8,128)(2,1)S(1)} %dynamic-slice_bitcast_fusion), channel_id=1, source_target_pairs={{0,12},{4,0},{8,4},{12,8},{1,13},{5,1},{9,5},{13,9},{2,14},{6,2},{... | collective-permute-start | bytes 786440 | tf_op jit(solution)/shard_map/ppermute | solution.py:337
  73.7 29.6 %copy-start.7 = (bf16[64,2048]{1,0:T(8,128)(2,1)}, bf16[64,2048]{1,0:T(8,128)(2,1)S(1)}, u32[]{:S(2)}) copy-start(bf16[64,2048]{1,0:T(8,128)(2,1)S(1)} %collective-permute-done.12.rest_1_) | copy-start | bytes 786436
  73.7 17.5 %collective-permute-start.14 = (bf16[64,2048]{1,0:T(8,128)(2,1)S(1)}, bf16[64,2048]{1,0:T(8,128)(2,1)S(1)}, u32[]{:S(2)}, u32[]{:S(2)}) collective-permute-start(bf16[64,2048]{1,0:T(8,128)(2,1)S(1)} %collective-permute-done.11.rest_0_), channel_id=1, source_target_pairs={{0,16},{16,0},{1,17},{17,1},{2,18},{18,2},{3,19},{19,3},{4,20},{20... | collective-permute-start | bytes 786440 | tf_op jit(solution)/shard_map/ppermute | solution.py:340
  74.0 29.2 %collective-permute-start.19 = (bf16[128,2048]{1,0:T(8,128)(2,1)}, bf16[128,2048]{1,0:T(8,128)(2,1)S(1)}, u32[]{:S(2)}, u32[]{:S(2)}) collective-permute-start(bf16[128,2048]{1,0:T(8,128)(2,1)} %add_partner_core.2), channel_id=1, source_target_pairs={{0,2},{1,3},{2,0},{3,1},{4,6},{5,7},{6,4},{7,5},{8,10},{9,11},{10,... | collective-permute-start | bytes 1572872 | tf_op jit(solution)/shard_map/ppermute | solution.py:346
  78.3 12.3 %collective-permute-start.17 = (bf16[272,64]{1,0:T(8,128)(2,1)S(1)}, bf16[272,64]{1,0:T(8,128)(2,1)S(1)}, u32[]{:S(2)}, u32[]{:S(2)}) collective-permute-start(bf16[272,64]{1,0:T(8,128)(2,1)S(1)} %get-tuple-element.41), channel_id=1, source_target_pairs={{0,2},{1,3},{2,0},{3,1},{4,6},{5,7},{6,4},{7,5},{8,10},{9,11},{10,... | collective-permute-start | bytes 104456 | tf_op jit(solution)/shard_map/ppermute | solution.py:346
  90.6 9.2 %collective-permute-start.15 = (bf16[64,2048]{1,0:T(8,128)(2,1)S(1)}, bf16[64,2048]{1,0:T(8,128)(2,1)S(1)}, u32[]{:S(2)}, u32[]{:S(2)}) collective-permute-start(bf16[64,2048]{1,0:T(8,128)(2,1)S(1)} %collective-permute-done.12.rest_1_), channel_id=1, source_target_pairs={{0,16},{16,0},{1,17},{17,1},{2,18},{18,2},{3,19},{19,3},{4,20},{20... | collective-permute-start | bytes 786440 | tf_op jit(solution)/shard_map/ppermute | solution.py:340
  91.1 12.1 %collective-permute-start.16 = (bf16[64,2048]{1,0:T(8,128)(2,1)S(1)}, bf16[64,2048]{1,0:T(8,128)(2,1)S(1)}, u32[]{:S(2)}, u32[]{:S(2)}) collective-permute-start(bf16[64,2048]{1,0:T(8,128)(2,1)S(1)} %collective-permute-done.13.rest_2_), channel_id=1, source_target_pairs={{0,16},{16,0},{1,17},{17,1},{2,18},{18,2},{3,19},{19,3},{4,20},{20... | collective-permute-start | bytes 786440 | tf_op jit(solution)/shard_map/ppermute | solution.py:340
  (20 other events, 135.8 us)

commit v2 on v1

v2 whole, which is shorter than its diff:
```python
import functools
import math

import jax
import jax.numpy as jnp
from jax import lax
from jax.experimental import pallas as pl
from jax.experimental.pallas import tpu as pltpu
from jax.sharding import PartitionSpec as P

QUERY_HEADS_HALF = 32
KVH = 4
HEAD_SIZE = 128
ADAPTER_SCALE = 2.0
RUNS = (5, 5, 6)
LONG = 200
PAD = 16
IDS = 128
VMEM_LIMIT = 60 * 1024 * 1024
BF16 = jnp.bfloat16
F32 = jnp.float32
ANY = pl.BlockSpec(memory_space=pl.ANY)
VMEM = pl.BlockSpec(memory_space=pltpu.VMEM)
SMEM = pl.BlockSpec(memory_space=pltpu.SMEM)


def cost(micros):
    return pl.CostEstimate(flops=int(micros * 1.15e9), bytes_accessed=1024, transcendentals=0)


def call(body, out_shape, in_specs, scratch, name, args, micros, limit=VMEM_LIMIT):
    return pl.pallas_call(
        body,
        out_shape=out_shape,
        in_specs=in_specs,
        out_specs=[VMEM] * len(out_shape),
        scratch_shapes=scratch,
        compiler_params=pltpu.CompilerParams(vmem_limit_bytes=limit),
        cost_estimate=cost(micros),
        name=name,
    )(*args)


def down_rows(lane_row):
    return jnp.broadcast_to(lane_row, (128, lane_row.shape[1])).T


def attend(q_of, own_of, idx, lens, pool_ref, at, k_ref, v_ref, sems, bias_ref, s_ref, heads, store):
    rows = idx.shape[1]
    D = HEAD_SIZE
    nblk, bs, _ = pool_ref.shape
    npos = nblk * bs
    scale = math.log2(math.e) / math.sqrt(D)
    k_copy = pltpu.make_async_copy(pool_ref.at[:, :, pl.ds(at, D)], k_ref, sems.at[0])
    v_copy = pltpu.make_async_copy(
        pool_ref.at[:, :, pl.ds(pl.multiple_of(at + D, D), D)], v_ref.at[:, :, pl.ds(0, D)], sems.at[1]
    )
    k_copy.start()
    v_copy.start()
    v_ref[:, :, D:] = jnp.ones((nblk, bs, D), BF16)
    nfull = jnp.floor(lens * (1.0 / bs))
    rem = lens - nfull * bs
    block = lax.broadcasted_iota(jnp.int32, (nblk, rows), 0).astype(F32)
    full = jnp.zeros((nblk, rows), F32)
    some = jnp.zeros((nblk, rows), F32)
    for j in range(idx.shape[0]):
        hit = idx[j : j + 1, :] == block
        full += jnp.where(hit & (nfull > j), 1.0, 0.0)
        some += jnp.where(hit & (lens > j * bs), 1.0, 0.0)
    full = full.astype(BF16)
    some = some.astype(BF16)
    width = 512
    offset = (lax.broadcasted_iota(jnp.int32, (rows, 128), 1) % bs).astype(F32)
    partial = jnp.concatenate([offset < down_rows(rem)] * (width // 128), 1)
    over_rows = (((0,), (0,)), ((), ()))
    for w in range(0, npos, width):
        spot = lax.broadcasted_iota(jnp.int32, (nblk, width), 1) + w
        here = spot // bs == lax.broadcasted_iota(jnp.int32, (nblk, width), 0)
        spread = jnp.where(here, 1.0, 0.0).astype(BF16)
        count_full = lax.dot_general(full, spread, over_rows, preferred_element_type=F32)
        count_some = lax.dot_general(some, spread, over_rows, preferred_element_type=F32)
        count = jnp.where(partial, count_some, count_full)
        bias_ref[:, w : w + width] = jnp.where(
            count > 0.5, jnp.log2(jnp.maximum(count, 1.0)), -jnp.inf
        )
    own = own_of().astype(F32)
    own_k, own_v = own[:, :D], own[:, D:]
    k_copy.wait()
    v_copy.wait()
    keys = k_ref[...].reshape(npos, D)
    values = v_ref[...].reshape(npos, 2 * D)
    nt = (((1,), (1,)), ((), ()))
    before = None
    width = 1024
    for h in range(heads + 1):
        top = acc = None
        for w in range(0, npos, width):
            if h < heads:
                s = lax.dot_general(q_of(h), keys[w : w + width], nt, preferred_element_type=F32)
                s = s * scale + bias_ref[:, w : w + width]
                s_ref[h % 2, :, w : w + width] = s
                for lane in range(0, width, 128):
                    part = s[:, lane : lane + 128]
                    top = part if top is None else jnp.maximum(top, part)
            if h:
                p = jnp.exp2(s_ref[(h - 1) % 2, :, w : w + width] - before[1]).astype(BF16)
                part = jnp.dot(p, values[w : w + width], preferred_element_type=F32)
                acc = part if acc is None else acc + part
        if h:
            own_w = jnp.exp2(before[0] - before[1])
            out = (acc[:, :D] + own_w * own_v) / (acc[:, D : D + 1] + own_w)
            store(h - 1, out.astype(BF16))
        if h < heads:
            own_s = jnp.sum(q_of(h).astype(F32) * own_k, axis=1, keepdims=True) * scale
            before = own_s, jnp.maximum(jnp.max(top, axis=1, keepdims=True), own_s)


def weight_copies(w_ref, held, sems, blocks):
    width = held.shape[2]
    out = []
    for i, block in enumerate(blocks):
        start = pl.multiple_of(block * width, width)
        out.append(pltpu.make_async_copy(w_ref.at[:, pl.ds(start, width)], held.at[i], sems.at[i]))
    return out


def chip_blocks(t, chips):
    chip, core = t // 2, t % 2
    out = []
    for d in range(1, chips):
        at = 2 * lax.rem(chip + d, chips)
        out += [at + 1 - core, at + core]
    return out


def attend_kernel(chips, members, sc_ref, leave_ref, recv_ref, q_ref, fresh_ref, idx_ref, len_ref, id_ref, pool_ref,
                  w_ref, attn_ref, *rest):
    sends, keeps, rest = rest[: len(RUNS)], rest[len(RUNS) : 2 * len(RUNS)], rest[2 * len(RUNS) :]
    pays, (k_ref, v_ref, fresh, bias, s, held, psem, wsem) = rest[:members], rest[members:]
    t, z, kv = sc_ref[0], sc_ref[1], sc_ref[2]
    D = HEAD_SIZE
    rows, channels = attn_ref.shape
    at = pl.multiple_of(kv * 2 * D, 2 * D)
    own_copy = pltpu.make_async_copy(fresh_ref.at[:, pl.ds(at, 2 * D)], fresh, psem.at[2])
    own_copy.start()
    copies = weight_copies(w_ref, held, wsem, chip_blocks(t, chips))

    def own_of():
        for c in copies:
            c.start()
        own_copy.wait()
        return fresh[...]

    def store(h, out):
        attn_ref[:, h * D : (h + 1) * D] = out

    attend(lambda h: q_ref[:, h * D : (h + 1) * D], own_of, idx_ref[...].astype(F32),
           len_ref[...].astype(F32), pool_ref, at, k_ref, v_ref, psem, bias, s, channels // D, store)
    a = attn_ref[...]
    width = held.shape[2]
    for i, c in enumerate(copies):
        c.wait()
        lo = (i // 2) * width
        out = jnp.dot(a, held[i], preferred_element_type=F32).astype(BF16)
        row = 0
        for ref in (sends, keeps)[i % 2]:
            ref[:, lo : lo + width] = out[row : row + ref.shape[0]]
            row += ref.shape[0]
    moved = leave_ref.shape[1]
    lane = lax.broadcasted_iota(jnp.int32, (PAD, rows), 1)
    row = lax.broadcasted_iota(jnp.int32, (PAD, rows), 0)
    pick = jnp.zeros((PAD, rows), jnp.bool_)
    for j in range(moved):
        pick = pick | ((row == j) & (lane == leave_ref[0, j]))
    pick = jnp.where(pick, 1.0, 0.0).astype(BF16)
    left = jnp.dot(pick, a, preferred_element_type=F32)
    nt = (((1,), (1,)), ((), ()))
    ids = jnp.broadcast_to(id_ref[...].astype(F32), (IDS, rows)).astype(BF16)
    id_col = lax.dot_general(pick, ids, nt, preferred_element_type=F32)
    left = jnp.concatenate([left, id_col], 1).astype(BF16)
    for k in range(members):
        pays[k][...] = jnp.where(recv_ref[0] == (z ^ k), left, jnp.zeros_like(left))


def own_kernel(members, sc_ref, slots_ref, leave_ref, w_ref, id_ref, attn_ref, *rest):
    pays, (send_ref, own_ref, fixed, slot_ref, arr_ref, held, wsem) = rest[:members], rest[members:]
    t = sc_ref[0]
    copies = weight_copies(w_ref, held, wsem, [t + 1 - 2 * (t % 2), t])
    for c in copies:
        c.start()
    rows, channels = fixed.shape
    moved = leave_ref.shape[1]
    arr = pays[0][...]
    for p in pays[1:]:
        arr = arr + p[...]
    arr_ref[...] = arr[:, :channels]
    row = lax.broadcasted_iota(jnp.int32, (rows, channels), 0)
    whole = attn_ref[...].astype(F32)
    for j in range(moved):
        whole = jnp.where(row == leave_ref[0, j], arr[j : j + 1, :channels].astype(F32), whole)
    fixed[...] = whole.astype(BF16)
    ids = down_rows(id_ref[...].astype(F32))
    came = arr[:, channels:].astype(F32)
    row = lax.broadcasted_iota(jnp.int32, ids.shape, 0)
    for j in range(moved):
        ids = jnp.where(row == leave_ref[0, j], came[j : j + 1, 0:1], ids)
    slot = jnp.zeros_like(ids)
    for i in range(slots_ref.shape[0]):
        slot = jnp.where(ids == i, slots_ref[i].astype(F32), slot)
    slot_ref[...] = slot
    a = fixed[...]
    for i, (c, ref) in enumerate(zip(copies, (send_ref, own_ref))):
        c.wait()
        ref[...] = jnp.dot(a, held[i], preferred_element_type=F32).astype(BF16)


def shrink_kernel(members, groups, chips, sc_ref, w_ref, attn_ref, slot_ref, arr_ref, own_down, *rest):
    same, swapped, rest = rest[: members - 1], rest[members - 1 : 2 * (members - 1)], rest[2 * (members - 1) :]
    pack_send, pack_keep, held, wsem = rest
    t, z, y = sc_ref[0], sc_ref[1], sc_ref[3]
    copies = weight_copies(w_ref, held, wsem, chip_blocks(t, chips))
    for c in copies:
        c.start()
    rows, channels = attn_ref.shape
    a = attn_ref[...]
    rank = own_down.shape[1]
    nt = (((1,), (1,)), ((), ()))
    slot = slot_ref[:, : 2 * rank]
    total = jnp.zeros((rows, 2 * rank), F32)
    left = lax.broadcasted_iota(jnp.int32, total.shape, 1) < rank
    pieces = slot_pieces(members, groups, z, y, own_down, same, swapped)
    for (one, one_at), (two, two_at) in zip(pieces[::2], pieces[1::2]):
        part = lax.dot_general(a, jnp.concatenate([one, two], 0), nt, preferred_element_type=F32)
        total += jnp.where(slot == jnp.where(left, one_at, two_at).astype(F32), part, 0.0)
    shr = total[:, :rank] + total[:, rank:]
    shr = jnp.concatenate([shr, jnp.zeros((rows, 128 - rank), F32)], 1).astype(BF16)
    arr = arr_ref[...]
    width = held.shape[2]
    for i, c in enumerate(copies):
        c.wait()
        pack = (pack_send, pack_keep)[i % 2]
        out = jnp.dot(arr, held[i], preferred_element_type=F32).astype(BF16)
        parts = [out[:, c : c + 128] for c in range(0, width, 128)]
        lo, size = (i // 2) * rows, PAD * len(parts)
        pack[lo : lo + size, :128] = jnp.concatenate(parts, 0)
        if size < rows:
            pack[lo + size : lo + rows, :128] = jnp.zeros((rows - size, 128), BF16)
        pack[lo : lo + rows, 128:] = shr


def slot_pieces(members, groups, z, y, own, same, swapped):
    pieces = [(own[g], z * groups + g) for g in range(groups)]
    for k in range(1, members):
        layer = (z ^ k) * groups
        pieces.append((same[k - 1][...], layer + y))
        pieces.append((swapped[k - 1][...], layer + 1 - y))
    return pieces


def final_kernel(members, groups, chips, sc_ref, leave_ref, slot_ref, own_ref, got_ref, own_up, *rest):
    same, swapped = rest[: members - 1], rest[members - 1 : 2 * (members - 1)]
    rest = rest[2 * (members - 1) :]
    packs, rest = rest[:chips], rest[chips:]
    moves, far, out_ref = rest[: chips - 1], rest[chips - 1 : -1], rest[-1]
    z, y = sc_ref[1], sc_ref[3]
    rank = own_up.shape[1]
    shrunk = sum(p[:, 128 : 128 + rank].astype(F32) for p in packs)
    shrunk = shrunk.astype(BF16).astype(F32)
    wide = jnp.concatenate([shrunk, shrunk], 1)
    slot = slot_ref[:, : 2 * rank]
    left = lax.broadcasted_iota(jnp.int32, wide.shape, 1) < rank
    delta = None
    pieces = slot_pieces(members, groups, z, y, own_up, same, swapped)
    for (one, one_at), (two, two_at) in zip(pieces[::2], pieces[1::2]):
        spread = jnp.where(slot == jnp.where(left, one_at, two_at).astype(F32), wide, 0.0).astype(BF16)
        part = jnp.dot(spread, jnp.concatenate([one, two], 0), preferred_element_type=F32)
        delta = part if delta is None else delta + part
    base = own_ref[...].astype(F32) + got_ref[...].astype(F32) + ADAPTER_SCALE * delta
    others = jnp.concatenate(
        [sum(r[...].astype(F32) for r in far[i : i + chips - 1]) for i in range(0, len(far), chips - 1)], 0
    )
    came = sum(r[...].astype(F32) for r in moves)
    row = lax.broadcasted_iota(jnp.int32, base.shape, 0)
    for j in range(leave_ref.shape[1]):
        new = jnp.concatenate([came[c + j : c + j + 1, :] for c in range(0, came.shape[0], PAD)], 1)
        others = jnp.where(row == leave_ref[0, j], new, others)
    out_ref[...] = (base + others).astype(BF16)


def after(value, *others):
    return lax.optimization_barrier((value,) + others)[0]


def on_device(mesh_shape, queries, fresh, pool, table, lengths, adapter_id, storage_slot, leaving, receiving,
              w, down, up):
    members, tensors, groups = mesh_shape["replica"], mesh_shape["tensor"], mesh_shape["groups"]
    chips = tensors // 2
    rows, channels = queries.shape
    heads = channels // HEAD_SIZE
    nblk, bs, _ = pool.shape
    npos = nblk * bs
    cols = w.shape[1] // tensors
    rank = down.shape[2]
    t = lax.axis_index("tensor")
    z = lax.axis_index("replica")
    y = lax.axis_index("groups")
    kv = t * heads // (QUERY_HEADS_HALF // KVH)
    sc = jnp.stack([t, z, kv, y]).astype(jnp.int32)
    idx_t = table.T
    len_row = lengths[None, :]
    id_row = adapter_id[None, :]
    down_t = jnp.swapaxes(down, 1, 2)

    def across(v, k):
        return lax.ppermute(v, "replica", [(i, i ^ k) for i in range(members)])

    def swap(v):
        return lax.ppermute(v, "groups", [(0, 1), (1, 0)])

    def core(v):
        return lax.ppermute(v, "tensor", [(i, i ^ 1) for i in range(tensors)])

    def chip(v, d):
        return lax.ppermute(v, "tensor", [(i, (i + 2 * d) % tensors) for i in range(tensors)])

    def to_chips(v):
        return [chip(v[:, (d - 1) * cols : d * cols] if chips > 2 else v, d) for d in range(1, chips)]

    mine_down = lax.dynamic_index_in_dim(down_t, y, 0, keepdims=False)
    mine_up = lax.dynamic_index_in_dim(up, y, 0, keepdims=False)

    def near(v):
        return {1 << i: across(v, 1 << i) for i in reversed(range(members.bit_length() - 1))}

    def passed(v, have):
        have = {0: v, **have}
        bit = members // 2
        while bit:
            for k in [k for k in have if k % (2 * bit) == 0 and k ^ bit not in have]:
                have[k ^ bit] = across(have[k], bit)
            bit //= 2
        return [have[k] for k in range(1, members)]

    down_near = near(mine_down)
    up_near = near(mine_up)
    sds = jax.ShapeDtypeStruct
    dma = pltpu.SemaphoreType.DMA
    far = (chips - 1) * cols
    sizes = [rows * r // sum(RUNS) for r in RUNS]
    attn, *out = call(
        functools.partial(attend_kernel, chips, members),
        [sds((rows, channels), BF16)] + [sds((n, far), BF16) for n in sizes] * 2
        + [sds((PAD, channels + IDS), BF16)] * members,
        [SMEM, SMEM, SMEM, VMEM, ANY, VMEM, VMEM, VMEM, ANY, ANY],
        [
            pltpu.VMEM((nblk, bs, HEAD_SIZE), BF16),
            pltpu.VMEM((nblk, bs, 2 * HEAD_SIZE), BF16),
            pltpu.VMEM((rows, 2 * HEAD_SIZE), BF16),
            pltpu.VMEM((rows, npos), F32),
            pltpu.VMEM((2, rows, npos), F32),
            pltpu.VMEM((2 * (chips - 1), channels, cols), BF16),
            dma((3,)),
            dma((2 * (chips - 1),)),
        ],
        "attend_and_project",
        (sc, leaving, receiving, queries, fresh, idx_t, len_row, id_row, pool, w),
        LONG,
    )
    runs = len(RUNS)
    sends, keeps, pays = out[:runs], out[runs : 2 * runs], out[2 * runs :]
    sends[0] = after(sends[0], *down_near.values(), *up_near.values())
    totals = []
    for send, keep in zip(sends, keeps):
        totals.append(after(keep, *totals) + core(send))
    x_in = [to_chips(total) for total in totals]
    arrived = [pays[0]] + [across(pays[k], k) for k in range(1, members)]
    down_same = passed(after(mine_down, attn), down_near)
    up_same = passed(after(mine_up, attn), up_near)
    down_swapped = {k: swap(after(v, attn)) for k, v in down_near.items()}
    up_swapped = {k: swap(after(v, attn)) for k, v in up_near.items()}
    early = [*down_same, *down_swapped.values(), *x_in[0]]
    send_own, own, fixed, slot, arr = call(
        functools.partial(own_kernel, members),
        [sds((rows, cols), BF16), sds((rows, cols), BF16), sds((rows, channels), BF16), sds((rows, 128), F32),
         sds((PAD, channels), BF16)],
        [SMEM, SMEM, SMEM, ANY, VMEM, VMEM] + [VMEM] * members,
        [pltpu.VMEM((2, channels, cols), BF16), dma((2,))],
        "project_own_columns",
        (sc, storage_slot, leaving, w, id_row, after(attn, *early), *arrived),
        LONG,
    )
    got_own = core(send_own)
    for k in range(1, members):
        if k not in up_swapped:
            down_swapped[k] = swap(down_same[k - 1])
            up_swapped[k] = swap(up_same[k - 1])
    down_swapped = [down_swapped[k] for k in range(1, members)]
    up_swapped = [up_swapped[k] for k in range(1, members)]
    pack_send, pack_keep = call(
        functools.partial(shrink_kernel, members, groups, chips),
        [sds(((chips - 1) * rows, 256), BF16)] * 2,
        [SMEM, ANY] + [VMEM] * (4 + 2 * (members - 1)),
        [pltpu.VMEM((2 * (chips - 1), channels, cols), BF16), dma((2 * (chips - 1),))],
        "shrink_and_project_arrived",
        (sc, w, after(fixed, *up_same, up_swapped[members // 2 - 1], *x_in[1]), slot, arr, down_t, *down_same,
         *down_swapped),
        LONG,
    )
    pack = pack_keep + core(pack_send)
    packs = [pack[:rows]] + [chip(pack[(d - 1) * rows : d * rows], d) for d in range(1, chips)]

    tile = cols // 4
    col = lambda n: pl.BlockSpec((n, tile), lambda i: (0, i))
    still = lambda *shape: pl.BlockSpec(shape, lambda i: (0,) * len(shape))
    strip = pl.BlockSpec((PAD * tile // 128, 128), lambda i: (i, 0))
    return pl.pallas_call(
        functools.partial(final_kernel, members, groups, chips),
        grid=(cols // tile,),
        out_shape=sds((rows, cols), BF16),
        in_specs=[SMEM, SMEM, still(rows, 128), col(rows), col(rows),
                  pl.BlockSpec((groups, rank, tile), lambda i: (0, 0, i))]
        + [col(rank)] * (2 * (members - 1)) + [still(rows, 256)] * chips + [strip] * (chips - 1)
        + [col(n) for n in sizes for _ in range(chips - 1)],
        out_specs=col(rows),
        compiler_params=pltpu.CompilerParams(vmem_limit_bytes=VMEM_LIMIT),
        cost_estimate=cost(5),
        name="combine",
    )(sc, leaving, slot, own, got_own, up, *up_same, *up_swapped, *packs, *packs[1:], *[v for x in x_in for v in x])


def solution(mesh):
    return jax.shard_map(
        functools.partial(on_device, dict(mesh.shape)),
        mesh=mesh,
        in_specs=(
            P(("groups", "replica"), "tensor"),
            P(("groups", "replica"), None),
            P(("groups", "replica"), None, None),
            P(("groups", "replica"), None),
            P(("groups", "replica")),
            P(("groups", "replica")),
            P(),
            P(("groups", "replica"), None),
            P(("groups", "replica")),
            P("tensor", None),
            P("replica", "tensor", None),
            P("replica", None, "tensor"),
        ),
        out_specs=P(("groups", "replica"), "tensor"),
        check_vma=False,
    )
```

time: 111 us -> 82.4 us (0.74)
  waiting for transfers between devices: 37.3 us -> 13.2 us
  Pallas kernels: 44.5 us -> 31.4 us
  other arithmetic: 1.25 us -> 6.25 us
  starting transfers between devices: 22.9 us -> 25.3 us
    pallas_call x7 -> x3, Pallas kernels: 38.5 us -> 26.1 us  [call(): pl.pallas_call(body, out_shape=out_shape, in_specs=in_specs, out_specs=[V...]
    ppermute x3 -> x4, waiting for transfers between devices: 12.2 us -> 0.01 us  [chip(): lax.ppermute(v, 'tensor', [(i, (i + 2 * d) % tensors) for i in range(tens...]
    ppermute x9, waiting for transfers between devices: 9.16 us -> 1.17 us  [across(): return lax.ppermute(v, 'replica', [(i, i ^ k) for i in range(members)])]
    add x0 -> x4, other arithmetic: none -> 5.63 us  [the longest x3 4.68 us: on_device(): totals.append(after(keep, *totals) + core(send))]
    ppermute x6, waiting for transfers between devices: 15.9 us -> 10.5 us  [swap(): return lax.ppermute(v, 'groups', [(0, 1), (1, 0)])]
    squeeze x1, local copies, waits for them, and re-layouts: 0.02 us -> 1.67 us  [on_device(): mine_up = lax.dynamic_index_in_dim(up, y, 0, keepdims=False)]
    ppermute x4 -> x5, waiting for transfers between devices: 0.01 us -> 1.55 us  [core(): return lax.ppermute(v, 'tensor', [(i, i ^ 1) for i in range(tensors)])]
    unnamed x44 -> x18, local copies, waits for them, and re-layouts: 2.84 us -> 1.52 us
  transfers between devices with their start and end apart: 22 -> 24, of which waited for: 9 -> 7; matrix products, arithmetic and copies ran while one was open for 1% -> 10% of each run, Pallas kernels for 35% -> 32%
where the time goes in v2:
time: 82.4 us; the launch traced here: 82 us
  Pallas kernels  31.4 us (38%)
  starting transfers between devices  25.3 us (31%)
  waiting for transfers between devices  13.2 us (16%)
  other arithmetic  6.25 us (8%)
  local copies, waits for them, and re-layouts  4.77 us (6%)
  between operations  0.95 us (1%)
    pallas_call x3, Pallas kernels, call(): pl.pallas_call(body, out_shape=out_shape, in_specs=in_specs, out_specs=[V...  26.1 us
    ppermute x9, starting transfers between devices, across(): return lax.ppermute(v, 'replica', [(i, i ^ k) for i in range(members)])  13.4 us
    ppermute x6, waiting for transfers between devices, swap(): return lax.ppermute(v, 'groups', [(0, 1), (1, 0)])  10.5 us
    ppermute x6, starting transfers between devices, swap(): return lax.ppermute(v, 'groups', [(0, 1), (1, 0)])  6.51 us
    pallas_call x1, Pallas kernels, on_device(): pl.pallas_call(functools.partial(final_kernel, members, groups, chips), g...  5.39 us
    add x3, other arithmetic, on_device(): totals.append(after(keep, *totals) + core(send))  4.68 us
    ppermute x4, starting transfers between devices, chip(): lax.ppermute(v, 'tensor', [(i, (i + 2 * d) % tensors) for i in range(tens...  4.32 us
    squeeze x1, local copies, waits for them, and re-layouts, on_device(): mine_up = lax.dynamic_index_in_dim(up, y, 0, keepdims=False)  1.67 us
  transfers between devices with their start and end apart: 24, of which 7 were waited for; matrix products, arithmetic and copies ran while one was open for 10% of the time, Pallas kernels for 32%

profile of v2, /device:TPU:0, one launch (start us, length us, event | category | flops | bytes accessed | tf_op | source)
XLA Modules:
  0.0 82.0 jit_solution(2239596612537921518)
XLA Ops:
  0.0 1.7 %dynamic-slice_bitcast_fusion = bf16[64,2048]{1,0:T(8,128)(2,1)} fusion(bf16[2,64,2048]{2,1,0:T(8,128)(2,1)} %own_up.1, s32[]{:T(128)S(6)} %select_n.12), kind=kLoop, calls=%fused_computation | loop fusion | bytes 524292 | tf_op jit(solution)/shard_map/jit(dynamic_index_in_dim)/squeeze | solution.py:330
  1.7 4.0 %collective-permute-start.5 = (bf16[64,2048]{1,0:T(8,128)(2,1)}, bf16[64,2048]{1,0:T(8,128)(2,1)}, u32[]{:S(2)}, u32[]{:S(2)}) collective-permute-start(bf16[64,2048]{1,0:T(8,128)(2,1)} %dynamic-slice_bitcast_fusion), channel_id=1, source_target_pairs={{0,8},{4,12},{8,0},{12,4},{1,9},{5,13},{9,1},{13,5},{2,10},{6,14},... | collective-permute-start | bytes 786440 | tf_op jit(solution)/shard_map/ppermute | solution.py:315
  5.7 1.6 %collective-permute-start.6 = (bf16[64,2048]{1,0:T(8,128)(2,1)}, bf16[64,2048]{1,0:T(8,128)(2,1)}, u32[]{:S(2)}, u32[]{:S(2)}) collective-permute-start(bf16[64,2048]{1,0:T(8,128)(2,1)} %dynamic-slice_bitcast_fusion), channel_id=1, source_target_pairs={{0,4},{4,0},{8,12},{12,8},{1,5},{5,1},{9,13},{13,9},{2,6},{6,2},{1... | collective-permute-start | bytes 786440 | tf_op jit(solution)/shard_map/ppermute | solution.py:315
  7.3 1.6 %dynamic-slice_bitcast_fusion.1 = bf16[64,1024]{1,0:T(8,128)(2,1)} fusion(bf16[2,1024,64]{1,2,0:T(8,128)(2,1)} %param.22, s32[]{:T(128)S(6)} %select_n.12), kind=kLoop, calls=%fused_computation.1 | loop fusion | bytes 262148 | tf_op jit(solution)/shard_map/jit(dynamic_index_in_dim)/squeeze | solution.py:329
  10.6 12.1 %attend_and_project.1 = (bf16[256,1024]{1,0:T(8,128)(2,1)}, bf16[80,2048]{1,0:T(8,128)(2,1)}, bf16[80,2048]{1,0:T(8,128)(2,1)}, bf16[96,2048]{1,0:T(8,128)(2,1)}...) custom-call(s32[4]{0:T(128)} %pad_add_fusion.sc_ref, ...), custom_call_target="tpu_custom_call" | custom-call | flops 230000001024 | bytes 1024 | tf_op jit(solution)/shard_map/attend_and_project/pallas_call | solution.py:32
  22.7 1.0 %collective-permute-done.1.rest_1_ = bf16[64,1024]{1,0:T(8,128)(2,1)} collective-permute-done((bf16[64,1024]{1,0:T(8,128)(2,1)}, bf16[64,1024]{1,0:T(8,128)(2,1)}, u32[]{:S(2)}, u32[]{:S(2)}) %collective-permute-start.1) | collective-permute-done | bytes 131104 | tf_op jit(solution)/shard_map/ppermute | solution.py:315
  24.5 1.3 %collective-permute-done.7 = bf16[80,2048]{1,0:T(8,128)(2,1)S(1)} collective-permute-done((bf16[80,2048]{1,0:T(8,128)(2,1)}, bf16[80,2048]{1,0:T(8,128)(2,1)S(1)}, u32[]{:S(2)}, u32[]{:S(2)}) %collective-permute-start.7) | collective-permute-done | bytes 327712 | tf_op jit(solution)/shard_map/ppermute | solution.py:321
  25.7 1.1 %add.20 = bf16[80,2048]{1,0:T(8,128)(2,1)S(1)} add(bf16[80,2048]{1,0:T(8,128)(2,1)} %get-tuple-element.35, bf16[80,2048]{1,0:T(8,128)(2,1)S(1)} %collective-permute-done.7) | non-fusion elementwise | flops 163840 | bytes 983040 | tf_op jit(solution)/shard_map/add | solution.py:374
  26.8 1.6 %collective-permute-start.8 = (bf16[80,2048]{1,0:T(8,128)(2,1)S(1)}, bf16[80,2048]{1,0:T(8,128)(2,1)S(1)}, u32[]{:S(2)}, u32[]{:S(2)}) collective-permute-start(bf16[80,2048]{1,0:T(8,128)(2,1)S(1)} %add.20), channel_id=1, source_target_pairs={{0,2},{1,3},{2,0},{3,1},{4,6},{5,7},{6,4},{7,5},{8,10},{9,11},{10,... | collective-permute-start | bytes 983048 | tf_op jit(solution)/shard_map/ppermute | solution.py:324
  28.4 1.5 %collective-permute-start.3 = (bf16[64,1024]{1,0:T(8,128)(2,1)}, bf16[64,1024]{1,0:T(8,128)(2,1)S(1)}, u32[]{:S(2)}, u32[]{:S(2)}) collective-permute-start(bf16[64,1024]{1,0:T(8,128)(2,1)} %collective-permute-done.1.rest_1_), channel_id=1, source_target_pairs={{0,16},{16,0},{1,17},{17,1},{2,18},{18,2},{3,19},{19,3},{4,20},{20... | collective-permute-start | bytes 393224 | tf_op jit(solution)/shard_map/ppermute | solution.py:318
  30.4 4.6 %collective-permute-done.3.rest_4_ = bf16[64,1024]{1,0:T(8,128)(2,1)S(1)} collective-permute-done((bf16[64,1024]{1,0:T(8,128)(2,1)}, bf16[64,1024]{1,0:T(8,128)(2,1)S(1)}, u32[]{:S(2)}, u32[]{:S(2)}) %collective-permute-start.3) | collective-permute-done | bytes 131104 | tf_op jit(solution)/shard_map/ppermute | solution.py:318
  35.0 1.4 %collective-permute-start.2 = (bf16[64,1024]{1,0:T(8,128)(2,1)}, bf16[64,1024]{1,0:T(8,128)(2,1)}, u32[]{:S(2)}, u32[]{:S(2)}) collective-permute-start(bf16[64,1024]{1,0:T(8,128)(2,1)} %collective-permute-done.1.rest_1_), channel_id=1, source_target_pairs={{0,4},{4,0},{8,12},{12,8},{1,5},{5,1},{9,13},{13,9},{2,6},{6,2},{1... | collective-permute-start | bytes 393224 | tf_op jit(solution)/shard_map/ppermute | solution.py:315
  36.7 2.2 %collective-permute-start.10 = (bf16[16,1152]{1,0:T(8,128)(2,1)}, bf16[16,1152]{1,0:T(8,128)(2,1)S(1)}, u32[]{:S(2)}, u32[]{:S(2)}) collective-permute-start(bf16[16,1152]{1,0:T(8,128)(2,1)} %get-tuple-element.41), channel_id=1, source_target_pairs={{0,8},{4,12},{8,0},{12,4},{1,9},{5,13},{9,1},{13,5},{2,10},{6,14},... | collective-permute-start | bytes 110600 | tf_op jit(solution)/shard_map/ppermute | solution.py:315
  38.9 1.6 %collective-permute-start.11 = (bf16[16,1152]{1,0:T(8,128)(2,1)}, bf16[16,1152]{1,0:T(8,128)(2,1)S(1)}, u32[]{:S(2)}, u32[]{:S(2)}) collective-permute-start(bf16[16,1152]{1,0:T(8,128)(2,1)} %get-tuple-element.42), channel_id=1, source_target_pairs={{0,12},{4,8},{8,4},{12,0},{1,13},{5,9},{9,5},{13,1},{2,14},{6,10},... | collective-permute-start | bytes 110600 | tf_op jit(solution)/shard_map/ppermute | solution.py:315
  40.6 1.8 %add.21 = bf16[80,2048]{1,0:T(8,128)(2,1)} add(bf16[80,2048]{1,0:T(8,128)(2,1)} %get-tuple-element.50, bf16[80,2048]{1,0:T(8,128)(2,1)S(1)} %collective-permute-done.17) | non-fusion elementwise | flops 163840 | bytes 983040 | tf_op jit(solution)/shard_map/add | solution.py:374
  42.4 1.9 %add.23 = bf16[96,2048]{1,0:T(8,128)(2,1)} add(bf16[96,2048]{1,0:T(8,128)(2,1)} %get-tuple-element.57, bf16[96,2048]{1,0:T(8,128)(2,1)S(1)} %collective-permute-done.22) | non-fusion elementwise | flops 196608 | bytes 1179648 | tf_op jit(solution)/shard_map/add | solution.py:374
  44.3 1.5 %collective-permute-start.15 = (bf16[64,2048]{1,0:T(8,128)(2,1)}, bf16[64,2048]{1,0:T(8,128)(2,1)}, u32[]{:S(2)}, u32[]{:S(2)}) collective-permute-start(bf16[64,2048]{1,0:T(8,128)(2,1)} %collective-permute-done.5.rest_1_), channel_id=1, source_target_pairs={{0,16},{16,0},{1,17},{17,1},{2,18},{18,2},{3,19},{19,3},{4,20},{20... | collective-permute-start | bytes 786440 | tf_op jit(solution)/shard_map/ppermute | solution.py:318
  47.1 1.9 %collective-permute-start.13 = (bf16[64,2048]{1,0:T(8,128)(2,1)}, bf16[64,2048]{1,0:T(8,128)(2,1)}, u32[]{:S(2)}, u32[]{:S(2)}) collective-permute-start(bf16[64,2048]{1,0:T(8,128)(2,1)} %collective-permute-done.5.rest_1_), channel_id=1, source_target_pairs={{0,4},{4,0},{8,12},{12,8},{1,5},{5,1},{9,13},{13,9},{2,6},{6,2},{1... | collective-permute-start | bytes 786440 | tf_op jit(solution)/shard_map/ppermute | solution.py:315
  49.0 1.5 %collective-permute-start.19 = (bf16[64,1024]{1,0:T(8,128)(2,1)}, bf16[64,1024]{1,0:T(8,128)(2,1)}, u32[]{:S(2)}, u32[]{:S(2)}) collective-permute-start(bf16[64,1024]{1,0:T(8,128)(2,1)} %collective-permute-done.2.rest_2_), channel_id=1, source_target_pairs={{0,16},{16,0},{1,17},{17,1},{2,18},{18,2},{3,19},{19,3},{4,20},{20... | collective-permute-start | bytes 393224 | tf_op jit(solution)/shard_map/ppermute | solution.py:318
  51.1 7.2 %project_own_columns.1 = (bf16[256,2048]{1,0:T(8,128)(2,1)}, bf16[256,2048]{1,0:T(8,128)(2,1)}, bf16[256,1024]{1,0:T(8,128)(2,1)}, f32[256,128]{1,0:T(8,128)}, bf16[16,1024]{1,0:T(8,128)(2,1)}) custom-call(s32[4]{0:T(128)} %pad_add_fusion.sc_ref, s32[8]{0:T(128)} %slots_ref.1, s32[1,2]{1,0:T(1,128)} %leave_ref.5, bf16[1024,8192]{1,0:T(8,128)(2,1)} %w_ref.5, ...), custom_call_target="tpu_custom_call" | custom-call | flops 230000001024 | bytes 1024 | tf_op jit(solution)/shard_map/project_own_columns/pallas_call | solution.py:32
  58.3 1.5 %collective-permute-start.23 = (bf16[96,2048]{1,0:T(8,128)(2,1)}, bf16[96,2048]{1,0:T(8,128)(2,1)}, u32[]{:S(2)}, u32[]{:S(2)}) collective-permute-start(bf16[96,2048]{1,0:T(8,128)(2,1)} %add.23), channel_id=1, source_target_pairs={{0,2},{1,3},{2,0},{3,1},{4,6},{5,7},{6,4},{7,5},{8,10},{9,11},{10,... | collective-permute-start | bytes 1179656 | tf_op jit(solution)/shard_map/ppermute | solution.py:324
  59.8 6.8 %shrink_and_project_arrived.1 = (bf16[256,256]{1,0:T(8,128)(2,1)}, bf16[256,256]{1,0:T(8,128)(2,1)}) custom-call(s32[4]{0:T(128)} %pad_add_fusion.sc_ref, bf16[1024,8192]{1,0:T(8,128)(2,1)} %w_ref.5, bf16[256,1024]{1,0:T(8,128)(2,1)} %get-tuple-element.52.attn_ref, f32[256,128]{1,0:T(8,128)} %get-tuple-element.43.slot_ref, ...), custom_call_target="tpu_custom_call" | custom-call | flops 230000001024 | bytes 1024 | tf_op jit(solution)/shard_map/shrink_and_project_arrived/pallas_call | solution.py:32
  70.0 5.7 %collective-permute-done.16.rest_5_ = bf16[64,2048]{1,0:T(8,128)(2,1)S(1)} collective-permute-done((bf16[64,2048]{1,0:T(8,128)(2,1)}, bf16[64,2048]{1,0:T(8,128)(2,1)S(1)}, u32[]{:S(2)}, u32[]{:S(2)}) %collective-permute-start.16) | collective-permute-done | bytes 262176 | tf_op jit(solution)/shard_map/ppermute | solution.py:318
  76.4 5.4 %combine.1 = bf16[256,2048]{1,0:T(8,128)(2,1)} custom-call(s32[4]{0:T(128)} %pad_add_fusion.sc_ref, s32[1,2]{1,0:T(1,128)} %leave_ref.5, f32[256,128]{1,0:T(8,128)} %get-tuple-element.43.slot_ref, bf16[256,2048]{1,0:T(8,128)(2,1)} %get-tuple-element.44.own_ref, bf16[256,2048]{1,0:T(8,128)(2,1)} %collective-permute-done.12.got_ref, ...), custom_call_target="tpu_custom_call" | custom-call | flops 5750000128 | bytes 1024 | tf_op jit(solution)/shard_map/combine/pallas_call | solution.py:416
  (53 shorter events, 8.7 us)
Async XLA Ops:
  1.7 22.2 %collective-permute-start.5 = (bf16[64,2048]{1,0:T(8,128)(2,1)}, bf16[64,2048]{1,0:T(8,128)(2,1)}, u32[]{:S(2)}, u32[]{:S(2)}) collective-permute-start(bf16[64,2048]{1,0:T(8,128)(2,1)} %dynamic-slice_bitcast_fusion), channel_id=1, source_target_pairs={{0,8},{4,12},{8,0},{12,4},{1,9},{5,13},{9,1},{13,5},{2,10},{6,14},... | collective-permute-start | bytes 786440 | tf_op jit(solution)/shard_map/ppermute | solution.py:315
  5.7 18.2 %collective-permute-start.6 = (bf16[64,2048]{1,0:T(8,128)(2,1)}, bf16[64,2048]{1,0:T(8,128)(2,1)}, u32[]{:S(2)}, u32[]{:S(2)}) collective-permute-start(bf16[64,2048]{1,0:T(8,128)(2,1)} %dynamic-slice_bitcast_fusion), channel_id=1, source_target_pairs={{0,4},{4,0},{8,12},{12,8},{1,5},{5,1},{9,13},{13,9},{2,6},{6,2},{1... | collective-permute-start | bytes 786440 | tf_op jit(solution)/shard_map/ppermute | solution.py:315
  8.9 14.9 %collective-permute-start.1 = (bf16[64,1024]{1,0:T(8,128)(2,1)}, bf16[64,1024]{1,0:T(8,128)(2,1)}, u32[]{:S(2)}, u32[]{:S(2)}) collective-permute-start(bf16[64,1024]{1,0:T(8,128)(2,1)} %dynamic-slice_bitcast_fusion.1), channel_id=1, source_target_pairs={{0,8},{4,12},{8,0},{12,4},{1,9},{5,13},{9,1},{13,5},{2,10},{6,14},... | collective-permute-start | bytes 393224 | tf_op jit(solution)/shard_map/ppermute | solution.py:315
  9.2 14.7 %collective-permute-start = (bf16[64,1024]{1,0:T(8,128)(2,1)}, bf16[64,1024]{1,0:T(8,128)(2,1)}, u32[]{:S(2)}, u32[]{:S(2)}) collective-permute-start(bf16[64,1024]{1,0:T(8,128)(2,1)} %dynamic-slice_bitcast_fusion.1), channel_id=1, source_target_pairs={{0,4},{4,0},{8,12},{12,8},{1,5},{5,1},{9,13},{13,9},{2,6},{6,2},{1... | collective-permute-start | bytes 393224 | tf_op jit(solution)/shard_map/ppermute | solution.py:315
  23.9 1.8 %collective-permute-start.7 = (bf16[80,2048]{1,0:T(8,128)(2,1)}, bf16[80,2048]{1,0:T(8,128)(2,1)S(1)}, u32[]{:S(2)}, u32[]{:S(2)}) collective-permute-start(bf16[80,2048]{1,0:T(8,128)(2,1)} %get-tuple-element.37), channel_id=1, source_target_pairs={{0,1},{1,0},{2,3},{3,2},{4,5},{5,4},{6,7},{7,6},{8,9},{9,8},{10,11... | collective-permute-start | bytes 983048 | tf_op jit(solution)/shard_map/ppermute | solution.py:321
  23.9 16.6 %collective-permute-start.22 = (bf16[96,2048]{1,0:T(8,128)(2,1)}, bf16[96,2048]{1,0:T(8,128)(2,1)S(1)}, u32[]{:S(2)}, u32[]{:S(2)}) collective-permute-start(bf16[96,2048]{1,0:T(8,128)(2,1)} %get-tuple-element.58), channel_id=1, source_target_pairs={{0,1},{1,0},{2,3},{3,2},{4,5},{5,4},{6,7},{7,6},{8,9},{9,8},{10,11... | collective-permute-start | bytes 1179656 | tf_op jit(solution)/shard_map/ppermute | solution.py:321
  24.4 14.5 %collective-permute-start.17 = (bf16[80,2048]{1,0:T(8,128)(2,1)}, bf16[80,2048]{1,0:T(8,128)(2,1)S(1)}, u32[]{:S(2)}, u32[]{:S(2)}) collective-permute-start(bf16[80,2048]{1,0:T(8,128)(2,1)} %get-tuple-element.51), channel_id=1, source_target_pairs={{0,1},{1,0},{2,3},{3,2},{4,5},{5,4},{6,7},{7,6},{8,9},{9,8},{10,11... | collective-permute-start | bytes 983048 | tf_op jit(solution)/shard_map/ppermute | solution.py:321
  26.8 19.0 %collective-permute-start.8 = (bf16[80,2048]{1,0:T(8,128)(2,1)S(1)}, bf16[80,2048]{1,0:T(8,128)(2,1)S(1)}, u32[]{:S(2)}, u32[]{:S(2)}) collective-permute-start(bf16[80,2048]{1,0:T(8,128)(2,1)S(1)} %add.20), channel_id=1, source_target_pairs={{0,2},{1,3},{2,0},{3,1},{4,6},{5,7},{6,4},{7,5},{8,10},{9,11},{10,... | collective-permute-start | bytes 983048 | tf_op jit(solution)/shard_map/ppermute | solution.py:324
  28.4 6.6 %collective-permute-start.3 = (bf16[64,1024]{1,0:T(8,128)(2,1)}, bf16[64,1024]{1,0:T(8,128)(2,1)S(1)}, u32[]{:S(2)}, u32[]{:S(2)}) collective-permute-start(bf16[64,1024]{1,0:T(8,128)(2,1)} %collective-permute-done.1.rest_1_), channel_id=1, source_target_pairs={{0,16},{16,0},{1,17},{17,1},{2,18},{18,2},{3,19},{19,3},{4,20},{20... | collective-permute-start | bytes 393224 | tf_op jit(solution)/shard_map/ppermute | solution.py:318
  29.9 6.8 %collective-permute-start.4 = (bf16[64,1024]{1,0:T(8,128)(2,1)}, bf16[64,1024]{1,0:T(8,128)(2,1)S(1)}, u32[]{:S(2)}, u32[]{:S(2)}) collective-permute-start(bf16[64,1024]{1,0:T(8,128)(2,1)} %collective-permute-done.rest_0_), channel_id=1, source_target_pairs={{0,16},{16,0},{1,17},{17,1},{2,18},{18,2},{3,19},{19,3},{4,20},{20... | collective-permute-start | bytes 393224 | tf_op jit(solution)/shard_map/ppermute | solution.py:318
  35.0 9.3 %collective-permute-start.2 = (bf16[64,1024]{1,0:T(8,128)(2,1)}, bf16[64,1024]{1,0:T(8,128)(2,1)}, u32[]{:S(2)}, u32[]{:S(2)}) collective-permute-start(bf16[64,1024]{1,0:T(8,128)(2,1)} %collective-permute-done.1.rest_1_), channel_id=1, source_target_pairs={{0,4},{4,0},{8,12},{12,8},{1,5},{5,1},{9,13},{13,9},{2,6},{6,2},{1... | collective-permute-start | bytes 393224 | tf_op jit(solution)/shard_map/ppermute | solution.py:315
  36.7 10.4 %collective-permute-start.10 = (bf16[16,1152]{1,0:T(8,128)(2,1)}, bf16[16,1152]{1,0:T(8,128)(2,1)S(1)}, u32[]{:S(2)}, u32[]{:S(2)}) collective-permute-start(bf16[16,1152]{1,0:T(8,128)(2,1)} %get-tuple-element.41), channel_id=1, source_target_pairs={{0,8},{4,12},{8,0},{12,4},{1,9},{5,13},{9,1},{13,5},{2,10},{6,14},... | collective-permute-start | bytes 110600 | tf_op jit(solution)/shard_map/ppermute | solution.py:315
  38.9 10.1 %collective-permute-start.11 = (bf16[16,1152]{1,0:T(8,128)(2,1)}, bf16[16,1152]{1,0:T(8,128)(2,1)S(1)}, u32[]{:S(2)}, u32[]{:S(2)}) collective-permute-start(bf16[16,1152]{1,0:T(8,128)(2,1)} %get-tuple-element.42), channel_id=1, source_target_pairs={{0,12},{4,8},{8,4},{12,0},{1,13},{5,9},{9,5},{13,1},{2,14},{6,10},... | collective-permute-start | bytes 110600 | tf_op jit(solution)/shard_map/ppermute | solution.py:315
  40.5 10.0 %collective-permute-start.9 = (bf16[16,1152]{1,0:T(8,128)(2,1)}, bf16[16,1152]{1,0:T(8,128)(2,1)S(1)}, u32[]{:S(2)}, u32[]{:S(2)}) collective-permute-start(bf16[16,1152]{1,0:T(8,128)(2,1)} %get-tuple-element.40), channel_id=1, source_target_pairs={{0,4},{4,0},{8,12},{12,8},{1,5},{5,1},{9,13},{13,9},{2,6},{6,2},{1... | collective-permute-start | bytes 110600 | tf_op jit(solution)/shard_map/ppermute | solution.py:315
  44.3 14.0 %collective-permute-start.15 = (bf16[64,2048]{1,0:T(8,128)(2,1)}, bf16[64,2048]{1,0:T(8,128)(2,1)}, u32[]{:S(2)}, u32[]{:S(2)}) collective-permute-start(bf16[64,2048]{1,0:T(8,128)(2,1)} %collective-permute-done.5.rest_1_), channel_id=1, source_target_pairs={{0,16},{16,0},{1,17},{17,1},{2,18},{18,2},{3,19},{19,3},{4,20},{20... | collective-permute-start | bytes 786440 | tf_op jit(solution)/shard_map/ppermute | solution.py:318
  46.5 23.5 %collective-permute-start.14 = (bf16[64,2048]{1,0:T(8,128)(2,1)}, bf16[64,2048]{1,0:T(8,128)(2,1)}, u32[]{:S(2)}, u32[]{:S(2)}) collective-permute-start(bf16[64,2048]{1,0:T(8,128)(2,1)} %collective-permute-done.6.rest_0_), channel_id=1, source_target_pairs={{0,16},{16,0},{1,17},{17,1},{2,18},{18,2},{3,19},{19,3},{4,20},{20... | collective-permute-start | bytes 786440 | tf_op jit(solution)/shard_map/ppermute | solution.py:318
  47.1 12.8 %collective-permute-start.13 = (bf16[64,2048]{1,0:T(8,128)(2,1)}, bf16[64,2048]{1,0:T(8,128)(2,1)}, u32[]{:S(2)}, u32[]{:S(2)}) collective-permute-start(bf16[64,2048]{1,0:T(8,128)(2,1)} %collective-permute-done.5.rest_1_), channel_id=1, source_target_pairs={{0,4},{4,0},{8,12},{12,8},{1,5},{5,1},{9,13},{13,9},{2,6},{6,2},{1... | collective-permute-start | bytes 786440 | tf_op jit(solution)/shard_map/ppermute | solution.py:315
  49.0 10.9 %collective-permute-start.19 = (bf16[64,1024]{1,0:T(8,128)(2,1)}, bf16[64,1024]{1,0:T(8,128)(2,1)}, u32[]{:S(2)}, u32[]{:S(2)}) collective-permute-start(bf16[64,1024]{1,0:T(8,128)(2,1)} %collective-permute-done.2.rest_2_), channel_id=1, source_target_pairs={{0,16},{16,0},{1,17},{17,1},{2,18},{18,2},{3,19},{19,3},{4,20},{20... | collective-permute-start | bytes 393224 | tf_op jit(solution)/shard_map/ppermute | solution.py:318
  50.5 9.3 %collective-permute-start.18 = (bf16[80,2048]{1,0:T(8,128)(2,1)}, bf16[80,2048]{1,0:T(8,128)(2,1)}, u32[]{:S(2)}, u32[]{:S(2)}) collective-permute-start(bf16[80,2048]{1,0:T(8,128)(2,1)} %add.21), channel_id=1, source_target_pairs={{0,2},{1,3},{2,0},{3,1},{4,6},{5,7},{6,4},{7,5},{8,10},{9,11},{10,... | collective-permute-start | bytes 983048 | tf_op jit(solution)/shard_map/ppermute | solution.py:324
  58.3 17.4 %collective-permute-start.23 = (bf16[96,2048]{1,0:T(8,128)(2,1)}, bf16[96,2048]{1,0:T(8,128)(2,1)}, u32[]{:S(2)}, u32[]{:S(2)}) collective-permute-start(bf16[96,2048]{1,0:T(8,128)(2,1)} %add.23), channel_id=1, source_target_pairs={{0,2},{1,3},{2,0},{3,1},{4,6},{5,7},{6,4},{7,5},{8,10},{9,11},{10,... | collective-permute-start | bytes 1179656 | tf_op jit(solution)/shard_map/ppermute | solution.py:324
  59.8 15.9 %collective-permute-start.12 = (bf16[256,2048]{1,0:T(8,128)(2,1)}, bf16[256,2048]{1,0:T(8,128)(2,1)}, u32[]{:S(2)}, u32[]{:S(2)}) collective-permute-start(bf16[256,2048]{1,0:T(8,128)(2,1)} %get-tuple-element.45), channel_id=1, source_target_pairs={{0,1},{1,0},{2,3},{3,2},{4,5},{5,4},{6,7},{7,6},{8,9},{9,8},{10,11... | collective-permute-start | bytes 3145736 | tf_op jit(solution)/shard_map/ppermute | solution.py:321
  66.6 1.8 %collective-permute-start.20 = (bf16[256,256]{1,0:T(8,128)(2,1)}, bf16[256,256]{1,0:T(8,128)(2,1)S(1)}, u32[]{:S(2)}, u32[]{:S(2)}) collective-permute-start(bf16[256,256]{1,0:T(8,128)(2,1)} %get-tuple-element.55), channel_id=1, source_target_pairs={{0,1},{1,0},{2,3},{3,2},{4,5},{5,4},{6,7},{7,6},{8,9},{9,8},{10,11... | collective-permute-start | bytes 393224 | tf_op jit(solution)/shard_map/ppermute | solution.py:321
  67.2 8.5 %collective-permute-start.16 = (bf16[64,2048]{1,0:T(8,128)(2,1)}, bf16[64,2048]{1,0:T(8,128)(2,1)S(1)}, u32[]{:S(2)}, u32[]{:S(2)}) collective-permute-start(bf16[64,2048]{1,0:T(8,128)(2,1)} %collective-permute-done.13.rest_2_), channel_id=1, source_target_pairs={{0,16},{16,0},{1,17},{17,1},{2,18},{18,2},{3,19},{19,3},{4,20},{20... | collective-permute-start | bytes 786440 | tf_op jit(solution)/shard_map/ppermute | solution.py:318
  69.3 6.4 %collective-permute-start.21 = (bf16[256,256]{1,0:T(8,128)(2,1)S(1)}, bf16[256,256]{1,0:T(8,128)(2,1)S(1)}, u32[]{:S(2)}, u32[]{:S(2)}) collective-permute-start(bf16[256,256]{1,0:T(8,128)(2,1)S(1)} %add.22.rest_6_), channel_id=1, source_target_pairs={{0,2},{1,3},{2,0},{3,1},{4,6},{5,7},{6,4},{7,5},{8,10},{9,11},{10,... | collective-permute-start | bytes 393224 | tf_op jit(solution)/shard_map/ppermute | solution.py:324
  (9 other events, 24.5 us)

commit v3 on v2

--- a/solution.py
+++ b/solution.py
@@ -12,7 +12,7 @@
 KVH = 4
 HEAD_SIZE = 128
 ADAPTER_SCALE = 2.0
-RUNS = (5, 5, 6)
+RUNS = (1,)
 LONG = 200
 PAD = 16
 IDS = 128
@@ -133,13 +133,15 @@
     return out
 
 
-def attend_kernel(chips, members, sc_ref, leave_ref, recv_ref, q_ref, fresh_ref, idx_ref, len_ref, id_ref, pool_ref,
+def attend_kernel(chips, members, leave_ref, recv_ref, q_ref, fresh_ref, idx_ref, len_ref, id_ref, pool_ref,
                   w_ref, attn_ref, *rest):
     sends, keeps, rest = rest[: len(RUNS)], rest[len(RUNS) : 2 * len(RUNS)], rest[2 * len(RUNS) :]
-    pays, (k_ref, v_ref, fresh, bias, s, held, psem, wsem) = rest[:members], rest[members:]
-    t, z, kv = sc_ref[0], sc_ref[1], sc_ref[2]
+    half = members // 2
+    evens, odd, (k_ref, v_ref, fresh, bias, s, held, psem, wsem) = rest[:half], rest[half], rest[half + 1 :]
+    t, z = lax.axis_index("tensor"), lax.axis_index("replica")
     D = HEAD_SIZE
     rows, channels = attn_ref.shape
+    kv = t * (channels // D) // (QUERY_HEADS_HALF // KVH)
     at = pl.multiple_of(kv * 2 * D, 2 * D)
     own_copy = pltpu.make_async_copy(fresh_ref.at[:, pl.ds(at, 2 * D)], fresh, psem.at[2])
     own_copy.start()
@@ -179,21 +181,24 @@
     id_col = lax.dot_general(pick, ids, nt, preferred_element_type=F32)
     left = jnp.concatenate([left, id_col], 1).astype(BF16)
     for k in range(members):
-        pays[k][...] = jnp.where(recv_ref[0] == (z ^ k), left, jnp.zeros_like(left))
-
-
-def own_kernel(members, sc_ref, slots_ref, leave_ref, w_ref, id_ref, attn_ref, *rest):
-    pays, (send_ref, own_ref, fixed, slot_ref, arr_ref, held, wsem) = rest[:members], rest[members:]
-    t = sc_ref[0]
-    copies = weight_copies(w_ref, held, wsem, [t + 1 - 2 * (t % 2), t])
+        pay = jnp.where(recv_ref[0] == (z ^ k), left, jnp.zeros_like(left))
+        if k % 2:
+            odd[PAD * (k // 2) : PAD * (k // 2 + 1), :] = pay
+        else:
+            evens[k // 2][...] = pay
+
+
+def own_kernel(chips, members, groups, slots_ref, leave_ref, w_ref, id_ref, attn_ref, *rest):
+    arr_ref, own_down, rest = rest[0], rest[1], rest[2:]
+    same, swapped, rest = rest[: members - 1], rest[members - 1 : 2 * (members - 1)], rest[2 * (members - 1) :]
+    send1, send2, own_ref, pack_send, pack_keep, slot_ref, fixed, held, wsem = rest
+    t, z, y = lax.axis_index("tensor"), lax.axis_index("replica"), lax.axis_index("groups")
+    copies = weight_copies(w_ref, held, wsem, [t + 1 - 2 * (t % 2), t] + chip_blocks(t, chips))
     for c in copies:
         c.start()
     rows, channels = fixed.shape
     moved = leave_ref.shape[1]
-    arr = pays[0][...]
-    for p in pays[1:]:
-        arr = arr + p[...]
-    arr_ref[...] = arr[:, :channels]
+    arr = arr_ref[...]
     row = lax.broadcasted_iota(jnp.int32, (rows, channels), 0)
     whole = attn_ref[...].astype(F32)
     for j in range(moved):
@@ -209,23 +214,9 @@
         slot = jnp.where(ids == i, slots_ref[i].astype(F32), slot)
     slot_ref[...] = slot
     a = fixed[...]
-    for i, (c, ref) in enumerate(zip(copies, (send_ref, own_ref))):
-        c.wait()
-        ref[...] = jnp.dot(a, held[i], preferred_element_type=F32).astype(BF16)
-
-
-def shrink_kernel(members, groups, chips, sc_ref, w_ref, attn_ref, slot_ref, arr_ref, own_down, *rest):
-    same, swapped, rest = rest[: members - 1], rest[members - 1 : 2 * (members - 1)], rest[2 * (members - 1) :]
-    pack_send, pack_keep, held, wsem = rest
-    t, z, y = sc_ref[0], sc_ref[1], sc_ref[3]
-    copies = weight_copies(w_ref, held, wsem, chip_blocks(t, chips))
-    for c in copies:
-        c.start()
-    rows, channels = attn_ref.shape
-    a = attn_ref[...]
     rank = own_down.shape[1]
     nt = (((1,), (1,)), ((), ()))
-    slot = slot_ref[:, : 2 * rank]
+    slot = slot[:, : 2 * rank]
     total = jnp.zeros((rows, 2 * rank), F32)
     left = lax.broadcasted_iota(jnp.int32, total.shape, 1) < rank
     pieces = slot_pieces(members, groups, z, y, own_down, same, swapped)
@@ -234,18 +225,29 @@
         total += jnp.where(slot == jnp.where(left, one_at, two_at).astype(F32), part, 0.0)
     shr = total[:, :rank] + total[:, rank:]
     shr = jnp.concatenate([shr, jnp.zeros((rows, 128 - rank), F32)], 1).astype(BF16)
-    arr = arr_ref[...]
+    half = rows // 2
+    copies[0].wait()
+    send1[...] = jnp.dot(a[:half], held[0], preferred_element_type=F32).astype(BF16)
+    send2[...] = jnp.dot(a[half:], held[0], preferred_element_type=F32).astype(BF16)
+    copies[1].wait()
+    own_ref[...] = jnp.dot(a, held[1], preferred_element_type=F32).astype(BF16)
     width = held.shape[2]
-    for i, c in enumerate(copies):
+    for i, c in enumerate(copies[2:]):
         c.wait()
         pack = (pack_send, pack_keep)[i % 2]
-        out = jnp.dot(arr, held[i], preferred_element_type=F32).astype(BF16)
+        out = jnp.dot(arr[:, :channels], held[2 + i], preferred_element_type=F32).astype(BF16)
         parts = [out[:, c : c + 128] for c in range(0, width, 128)]
         lo, size = (i // 2) * rows, PAD * len(parts)
         pack[lo : lo + size, :128] = jnp.concatenate(parts, 0)
         if size < rows:
             pack[lo + size : lo + rows, :128] = jnp.zeros((rows - size, 128), BF16)
         pack[lo : lo + rows, 128:] = shr
+
+
+def slice_kernel(down_ref, up_ref, down_out, up_out):
+    y = lax.axis_index("groups")
+    down_out[...] = down_ref[y]
+    up_out[...] = up_ref[y]
 
 
 def slot_pieces(members, groups, z, y, own, same, swapped):
@@ -257,12 +259,12 @@
     return pieces
 
 
-def final_kernel(members, groups, chips, sc_ref, leave_ref, slot_ref, own_ref, got_ref, own_up, *rest):
+def final_kernel(members, groups, chips, leave_ref, slot_ref, own_ref, got1, got2, own_up, *rest):
     same, swapped = rest[: members - 1], rest[members - 1 : 2 * (members - 1)]
     rest = rest[2 * (members - 1) :]
     packs, rest = rest[:chips], rest[chips:]
     moves, far, out_ref = rest[: chips - 1], rest[chips - 1 : -1], rest[-1]
-    z, y = sc_ref[1], sc_ref[3]
+    z, y = lax.axis_index("replica"), lax.axis_index("groups")
     rank = own_up.shape[1]
     shrunk = sum(p[:, 128 : 128 + rank].astype(F32) for p in packs)
     shrunk = shrunk.astype(BF16).astype(F32)
@@ -275,7 +277,8 @@
         spread = jnp.where(slot == jnp.where(left, one_at, two_at).astype(F32), wide, 0.0).astype(BF16)
         part = jnp.dot(spread, jnp.concatenate([one, two], 0), preferred_element_type=F32)
         delta = part if delta is None else delta + part
-    base = own_ref[...].astype(F32) + got_ref[...].astype(F32) + ADAPTER_SCALE * delta
+    got = jnp.concatenate([got1[...], got2[...]], 0)
+    base = own_ref[...].astype(F32) + got.astype(F32) + ADAPTER_SCALE * delta
     others = jnp.concatenate(
         [sum(r[...].astype(F32) for r in far[i : i + chips - 1]) for i in range(0, len(far), chips - 1)], 0
     )
@@ -296,16 +299,10 @@
     members, tensors, groups = mesh_shape["replica"], mesh_shape["tensor"], mesh_shape["groups"]
     chips = tensors // 2
     rows, channels = queries.shape
-    heads = channels // HEAD_SIZE
     nblk, bs, _ = pool.shape
     npos = nblk * bs
     cols = w.shape[1] // tensors
     rank = down.shape[2]
-    t = lax.axis_index("tensor")
-    z = lax.axis_index("replica")
-    y = lax.axis_index("groups")
-    kv = t * heads // (QUERY_HEADS_HALF // KVH)
-    sc = jnp.stack([t, z, kv, y]).astype(jnp.int32)
     idx_t = table.T
     len_row = lengths[None, :]
     id_row = adapter_id[None, :]
@@ -326,8 +323,15 @@
     def to_chips(v):
         return [chip(v[:, (d - 1) * cols : d * cols] if chips > 2 else v, d) for d in range(1, chips)]
 
-    mine_down = lax.dynamic_index_in_dim(down_t, y, 0, keepdims=False)
-    mine_up = lax.dynamic_index_in_dim(up, y, 0, keepdims=False)
+    mine_down, mine_up = call(
+        slice_kernel,
+        [jax.ShapeDtypeStruct(v.shape[1:], BF16) for v in (down_t, up)],
+        [VMEM, VMEM],
+        [],
+        "slices_of_this_group",
+        (down_t, up),
+        0,
+    )
 
     def near(v):
         return {1 << i: across(v, 1 << i) for i in reversed(range(members.bit_length() - 1))}
@@ -350,8 +354,8 @@
     attn, *out = call(
         functools.partial(attend_kernel, chips, members),
         [sds((rows, channels), BF16)] + [sds((n, far), BF16) for n in sizes] * 2
-        + [sds((PAD, channels + IDS), BF16)] * members,
-        [SMEM, SMEM, SMEM, VMEM, ANY, VMEM, VMEM, VMEM, ANY, ANY],
+        + [sds((PAD, channels + IDS), BF16)] * (members // 2) + [sds((PAD * members // 2, channels + IDS), BF16)],
+        [SMEM, SMEM, VMEM, ANY, VMEM, VMEM, VMEM, ANY, ANY],
         [
             pltpu.VMEM((nblk, bs, HEAD_SIZE), BF16),
             pltpu.VMEM((nblk, bs, 2 * HEAD_SIZE), BF16),
@@ -363,50 +367,47 @@
             dma((2 * (chips - 1),)),
         ],
         "attend_and_project",
-        (sc, leaving, receiving, queries, fresh, idx_t, len_row, id_row, pool, w),
+        (leaving, receiving, queries, fresh, idx_t, len_row, id_row, pool, w),
         LONG,
     )
     runs = len(RUNS)
-    sends, keeps, pays = out[:runs], out[runs : 2 * runs], out[2 * runs :]
+    sends, keeps, pays, odd = out[:runs], out[runs : 2 * runs], out[2 * runs : -1], out[-1]
+    first = across(odd, 1)
     sends[0] = after(sends[0], *down_near.values(), *up_near.values())
-    totals = []
-    for send, keep in zip(sends, keeps):
-        totals.append(after(keep, *totals) + core(send))
+    down_same = passed(mine_down, {k: after(v, attn) for k, v in down_near.items()})
+    down_swapped = {k: swap(after(v, attn)) for k, v in down_near.items()}
+    totals = [
+        after(keep, first, *down_same, *down_swapped.values()) + core(send) for send, keep in zip(sends, keeps)
+    ]
+    pays = [pay + first[PAD * i : PAD * (i + 1)] for i, pay in enumerate(pays)]
+    bit = 2
+    while len(pays) > 1:
+        got = across(jnp.concatenate(pays[1::2], 0), bit)
+        pays = [pay + got[PAD * i : PAD * (i + 1)] for i, pay in enumerate(pays[::2])]
+        bit *= 2
+    arrived = pays
     x_in = [to_chips(total) for total in totals]
-    arrived = [pays[0]] + [across(pays[k], k) for k in range(1, members)]
-    down_same = passed(after(mine_down, attn), down_near)
-    up_same = passed(after(mine_up, attn), up_near)
-    down_swapped = {k: swap(after(v, attn)) for k, v in down_near.items()}
-    up_swapped = {k: swap(after(v, attn)) for k, v in up_near.items()}
-    early = [*down_same, *down_swapped.values(), *x_in[0]]
-    send_own, own, fixed, slot, arr = call(
-        functools.partial(own_kernel, members),
-        [sds((rows, cols), BF16), sds((rows, cols), BF16), sds((rows, channels), BF16), sds((rows, 128), F32),
-         sds((PAD, channels), BF16)],
-        [SMEM, SMEM, SMEM, ANY, VMEM, VMEM] + [VMEM] * members,
-        [pltpu.VMEM((2, channels, cols), BF16), dma((2,))],
-        "project_own_columns",
-        (sc, storage_slot, leaving, w, id_row, after(attn, *early), *arrived),
-        LONG,
-    )
-    got_own = core(send_own)
+    up_same = passed(mine_up, {k: after(v, *arrived) for k, v in up_near.items()})
+    down_swapped = [down_swapped[k + 1] if k + 1 in down_swapped else swap(after(v, *totals)) for k, v in enumerate(down_same)]
+    up_swapped = {k: swap(after(v, *down_swapped, *arrived)) for k, v in up_near.items()}
     for k in range(1, members):
         if k not in up_swapped:
-            down_swapped[k] = swap(down_same[k - 1])
             up_swapped[k] = swap(up_same[k - 1])
-    down_swapped = [down_swapped[k] for k in range(1, members)]
     up_swapped = [up_swapped[k] for k in range(1, members)]
-    pack_send, pack_keep = call(
-        functools.partial(shrink_kernel, members, groups, chips),
-        [sds(((chips - 1) * rows, 256), BF16)] * 2,
-        [SMEM, ANY] + [VMEM] * (4 + 2 * (members - 1)),
-        [pltpu.VMEM((2 * (chips - 1), channels, cols), BF16), dma((2 * (chips - 1),))],
-        "shrink_and_project_arrived",
-        (sc, w, after(fixed, *up_same, up_swapped[members // 2 - 1], *x_in[1]), slot, arr, down_t, *down_same,
+    send_own1, send_own2, own, pack_send, pack_keep, slot = call(
+        functools.partial(own_kernel, chips, members, groups),
+        [sds((rows // 2, cols), BF16)] * 2 + [sds((rows, cols), BF16)] + [sds(((chips - 1) * rows, 256), BF16)] * 2
+        + [sds((rows, 128), F32)],
+        [SMEM, SMEM, ANY, VMEM, VMEM] + [VMEM] * (2 + 2 * (members - 1)),
+        [pltpu.VMEM((rows, channels), BF16), pltpu.VMEM((tensors, channels, cols), BF16), dma((tensors,))],
+        "project_own_columns",
+        (storage_slot, leaving, w, id_row, after(attn, *totals), *arrived, down_t, *down_same,
          *down_swapped),
-        LONG,
-    )
-    pack = pack_keep + core(pack_send)
+        0,
+    )
+    got_own = [core(send_own1), core(send_own2)]
+    pack = pack_keep + core(after(pack_send, *[up_swapped[k - 1] for k in up_near]))
+    pack = after(pack, *x_in[0])
     packs = [pack[:rows]] + [chip(pack[(d - 1) * rows : d * rows], d) for d in range(1, chips)]
 
     tile = cols // 4
@@ -417,7 +418,7 @@
         functools.partial(final_kernel, members, groups, chips),
         grid=(cols // tile,),
         out_shape=sds((rows, cols), BF16),
-        in_specs=[SMEM, SMEM, still(rows, 128), col(rows), col(rows),
+        in_specs=[SMEM, still(rows, 128), col(rows), col(rows // 2), col(rows // 2),
                   pl.BlockSpec((groups, rank, tile), lambda i: (0, 0, i))]
         + [col(rank)] * (2 * (members - 1)) + [still(rows, 256)] * chips + [strip] * (chips - 1)
         + [col(n) for n in sizes for _ in range(chips - 1)],
@@ -425,7 +426,7 @@
         compiler_params=pltpu.CompilerParams(vmem_limit_bytes=VMEM_LIMIT),
         cost_estimate=cost(5),
         name="combine",
-    )(sc, leaving, slot, own, got_own, up, *up_same, *up_swapped, *packs, *packs[1:], *[v for x in x_in for v in x])
+    )(leaving, slot, own, *got_own, up, *up_same, *up_swapped, *packs, *packs[1:], *[v for x in x_in for v in x])
 
 
 def solution(mesh):

time: 82.4 us -> 72.3 us (0.88)
  local copies, waits for them, and re-layouts: 4.77 us -> 0.67 us
  starting transfers between devices: 25.3 us -> 21.5 us
  Pallas kernels: 31.4 us -> 29 us
  waiting for transfers between devices: 13.2 us -> 14.9 us
  other arithmetic: 6.25 us -> 4.78 us
    ppermute x6, waiting for transfers between devices: 10.5 us -> 5.91 us  [swap(): return lax.ppermute(v, 'groups', [(0, 1), (1, 0)])]
    ppermute x9 -> x8, waiting for transfers between devices: 1.17 us -> 4.65 us  [across(): return lax.ppermute(v, 'replica', [(i, i ^ k) for i in range(members)])]
    ppermute x4 -> x2, waiting for transfers between devices: 0.01 us -> 3.41 us  [chip(): lax.ppermute(v, 'tensor', [(i, (i + 2 * d) % tensors) for i in range(tens...]
    squeeze x2 -> x0, local copies, waits for them, and re-layouts: 3.25 us -> none  [the longest x1 1.67 us: on_device(): mine_up = lax.dynamic_index_in_dim(up, y, 0, keepdims=False)]
    pallas_call x3, Pallas kernels: 26.1 us -> 23.4 us  [call(): pl.pallas_call(body, out_shape=out_shape, in_specs=in_specs, out_specs=[V...]
    ppermute x9 -> x8, starting transfers between devices: 13.4 us -> 10.8 us  [across(): return lax.ppermute(v, 'replica', [(i, i ^ k) for i in range(members)])]
    ppermute x4 -> x2, starting transfers between devices: 4.32 us -> 3.05 us  [chip(): lax.ppermute(v, 'tensor', [(i, (i + 2 * d) % tensors) for i in range(tens...]
    unnamed x18 -> x22, local copies, waits for them, and re-layouts: 1.52 us -> 0.67 us
  transfers between devices with their start and end apart: 24 -> 20, of which waited for: 7 -> 11; matrix products, arithmetic and copies ran while one was open for 10% -> 7% of each run, Pallas kernels for 32% -> 30%
where the time goes in v3:
time: 72.3 us; the launch traced here: 71.8 us
  Pallas kernels  29 us (40%)
  starting transfers between devices  21.5 us (30%)
  waiting for transfers between devices  14.9 us (21%)
  other arithmetic  4.78 us (7%)
  between operations  0.95 us (1%)
    pallas_call x3, Pallas kernels, call(): pl.pallas_call(body, out_shape=out_shape, in_specs=in_specs, out_specs=[V...  23.4 us
    ppermute x8, starting transfers between devices, across(): return lax.ppermute(v, 'replica', [(i, i ^ k) for i in range(members)])  10.8 us
    ppermute x6, starting transfers between devices, swap(): return lax.ppermute(v, 'groups', [(0, 1), (1, 0)])  7.04 us
    ppermute x6, waiting for transfers between devices, swap(): return lax.ppermute(v, 'groups', [(0, 1), (1, 0)])  5.91 us
    pallas_call x1, Pallas kernels, on_device(): pl.pallas_call(functools.partial(final_kernel, members, groups, chips), g...  5.54 us
    ppermute x8, waiting for transfers between devices, across(): return lax.ppermute(v, 'replica', [(i, i ^ k) for i in range(members)])  4.65 us
    ppermute x2, waiting for transfers between devices, chip(): lax.ppermute(v, 'tensor', [(i, (i + 2 * d) % tensors) for i in range(tens...  3.41 us
    ppermute x2, starting transfers between devices, chip(): lax.ppermute(v, 'tensor', [(i, (i + 2 * d) % tensors) for i in range(tens...  3.05 us
  transfers between devices with their start and end apart: 20, of which 11 were waited for; matrix products, arithmetic and copies ran while one was open for 7% of the time, Pallas kernels for 30%

profile of v3, /device:TPU:0, one launch (start us, length us, event | category | flops | bytes accessed | tf_op | source)
XLA Modules:
  0.0 71.8 jit_solution(11973984328781684858)
XLA Ops:
  0.0 1.9 %slices_of_this_group.1 = (bf16[64,1024]{1,0:T(8,128)(2,1)}, bf16[64,2048]{1,0:T(8,128)(2,1)}) custom-call(bf16[2,64,1024]{2,1,0:T(8,128)(2,1)} %bitcast.4, bf16[2,64,2048]{2,1,0:T(8,128)(2,1)} %own_up.1), custom_call_target="tpu_custom_call" | custom-call | bytes 1024 | tf_op jit(solution)/shard_map/slices_of_this_group/pallas_call | solution.py:32
  1.9 4.0 %collective-permute-start.2 = (bf16[64,1024]{1,0:T(8,128)(2,1)}, bf16[64,1024]{1,0:T(8,128)(2,1)}, u32[]{:S(2)}, u32[]{:S(2)}) collective-permute-start(bf16[64,1024]{1,0:T(8,128)(2,1)} %get-tuple-element.34), channel_id=1, source_target_pairs={{0,8},{4,12},{8,0},{12,4},{1,9},{5,13},{9,1},{13,5},{2,10},{6,14},... | collective-permute-start | bytes 393224 | tf_op jit(solution)/shard_map/ppermute | solution.py:312
  6.0 1.6 %collective-permute-start.1 = (bf16[64,1024]{1,0:T(8,128)(2,1)}, bf16[64,1024]{1,0:T(8,128)(2,1)}, u32[]{:S(2)}, u32[]{:S(2)}) collective-permute-start(bf16[64,1024]{1,0:T(8,128)(2,1)} %get-tuple-element.34), channel_id=1, source_target_pairs={{0,4},{4,0},{8,12},{12,8},{1,5},{5,1},{9,13},{13,9},{2,6},{6,2},{1... | collective-permute-start | bytes 393224 | tf_op jit(solution)/shard_map/ppermute | solution.py:312
  8.6 12.2 %attend_and_project.1 = (bf16[256,1024]{1,0:T(8,128)(2,1)}, bf16[256,2048]{1,0:T(8,128)(2,1)}, bf16[256,2048]{1,0:T(8,128)(2,1)}, bf16[16,1152]{1,0:T(8,128)(2,1...) custom-call(s32[1,2]{1,0:T(1,128)} %leave_ref.5, s32[1]{0:T(128)S(6)} %copy.13.recv_ref, bf16[256,1024]{1,0:T(8,128)(2,1)} %q_ref.1, ...), custom_call_target="tpu_custom_call" | custom-call | flops 230000001024 | bytes 1024 | tf_op jit(solution)/shard_map/attend_and_project/pallas_call | solution.py:32
  20.8 3.1 %collective-permute-done.6.rest_1_ = bf16[64,2048]{1,0:T(8,128)(2,1)} collective-permute-done((bf16[64,2048]{1,0:T(8,128)(2,1)}, bf16[64,2048]{1,0:T(8,128)(2,1)}, u32[]{:S(2)}, u32[]{:S(2)}) %collective-permute-start.6) | collective-permute-done | bytes 262176 | tf_op jit(solution)/shard_map/ppermute | solution.py:312
  24.1 1.5 %collective-permute-start = (bf16[32,1152]{1,0:T(8,128)(2,1)}, bf16[32,1152]{1,0:T(8,128)(2,1)S(1)}, u32[]{:S(2)}, u32[]{:S(2)}) collective-permute-start(bf16[32,1152]{1,0:T(8,128)(2,1)} %get-tuple-element.33), channel_id=1, source_target_pairs={{0,4},{4,0},{8,12},{12,8},{1,5},{5,1},{9,13},{13,9},{2,6},{6,2},{1... | collective-permute-start | bytes 221192 | tf_op jit(solution)/shard_map/ppermute | solution.py:312
  25.6 1.5 %collective-permute-start.4 = (bf16[64,1024]{1,0:T(8,128)(2,1)}, bf16[64,1024]{1,0:T(8,128)(2,1)S(1)}, u32[]{:S(2)}, u32[]{:S(2)}) collective-permute-start(bf16[64,1024]{1,0:T(8,128)(2,1)} %collective-permute-done.2.rest_3_), channel_id=1, source_target_pairs={{0,16},{16,0},{1,17},{17,1},{2,18},{18,2},{3,19},{19,3},{4,20},{20... | collective-permute-start | bytes 393224 | tf_op jit(solution)/shard_map/ppermute | solution.py:315
  29.8 2.1 %collective-permute-start.9 = (bf16[16,1152]{1,0:T(8,128)(2,1)S(1)}, bf16[16,1152]{1,0:T(8,128)(2,1)S(1)}, u32[]{:S(2)}, u32[]{:S(2)}) collective-permute-start(bf16[16,1152]{1,0:T(8,128)(2,1)S(1)} %slice_add_fusion), channel_id=1, source_target_pairs={{0,8},{4,12},{8,0},{12,4},{1,9},{5,13},{9,1},{13,5},{2,10},{6,14},... | collective-permute-start | bytes 110600 | tf_op jit(solution)/shard_map/ppermute | solution.py:312
  32.7 1.6 %collective-permute-done.5.rest_5_ = bf16[64,1024]{1,0:T(8,128)(2,1)S(1)} collective-permute-done((bf16[64,1024]{1,0:T(8,128)(2,1)}, bf16[64,1024]{1,0:T(8,128)(2,1)S(1)}, u32[]{:S(2)}, u32[]{:S(2)}) %collective-permute-start.5) | collective-permute-done | bytes 131104 | tf_op jit(solution)/shard_map/ppermute | solution.py:315
  34.3 1.7 %add.15 = bf16[256,2048]{1,0:T(8,128)(2,1)S(1)} add(bf16[256,2048]{1,0:T(8,128)(2,1)} %get-tuple-element.37, bf16[256,2048]{1,0:T(8,128)(2,1)S(1)} %collective-permute-done.8) | non-fusion elementwise | flops 524288 | bytes 3145728 | tf_op jit(solution)/shard_map/add | solution.py:380
  35.9 1.6 %collective-permute-start.18 = (bf16[256,2048]{1,0:T(8,128)(2,1)S(1)}, bf16[256,2048]{1,0:T(8,128)(2,1)S(1)}, u32[]{:S(2)}, u32[]{:S(2)}) collective-permute-start(bf16[256,2048]{1,0:T(8,128)(2,1)S(1)} %add.15), channel_id=1, source_target_pairs={{0,2},{1,3},{2,0},{3,1},{4,6},{5,7},{6,4},{7,5},{8,10},{9,11},{10,... | collective-permute-start | bytes 3145736 | tf_op jit(solution)/shard_map/ppermute | solution.py:321
  37.5 1.5 %collective-permute-start.10 = (bf16[64,1024]{1,0:T(8,128)(2,1)S(1)}, bf16[64,1024]{1,0:T(8,128)(2,1)S(1)}, u32[]{:S(2)}, u32[]{:S(2)}) collective-permute-start(bf16[64,1024]{1,0:T(8,128)(2,1)S(1)} %collective-permute-done.3.rest_4_), channel_id=1, source_target_pairs={{0,16},{16,0},{1,17},{17,1},{2,18},{18,2},{3,19},{19,3},{4,20},{20... | collective-permute-start | bytes 393224 | tf_op jit(solution)/shard_map/ppermute | solution.py:315
  39.0 1.4 %fusion.rest_0_ = bf16[16,1152]{1,0:T(8,128)(2,1)} fusion(bf16[16,1152]{1,0:T(8,128)(2,1)S(1)} %collective-permute-done.9, bf16[16,1152]{1,0:T(8,128)(2,1)} %get-tuple-element.42, bf16[32,1152]{1,0:T(8,128)(2,1)S(1)} %collective-permute-done), kind=kLoop, calls=%fused_computation.2 | loop fusion | flops 36864 | bytes 147456 | tf_op jit(solution)/shard_map/add | solution.py:386
  40.4 2.0 %collective-permute-done.10.rest_7_ = bf16[64,1024]{1,0:T(8,128)(2,1)S(1)} collective-permute-done((bf16[64,1024]{1,0:T(8,128)(2,1)S(1)}, bf16[64,1024]{1,0:T(8,128)(2,1)S(1)}, u32[]{:S(2)}, u32[]{:S(2)}) %collective-permute-start.10) | collective-permute-done | bytes 131104 | tf_op jit(solution)/shard_map/ppermute | solution.py:315
  42.5 1.5 %collective-permute-start.15 = (bf16[64,2048]{1,0:T(8,128)(2,1)}, bf16[64,2048]{1,0:T(8,128)(2,1)S(1)}, u32[]{:S(2)}, u32[]{:S(2)}) collective-permute-start(bf16[64,2048]{1,0:T(8,128)(2,1)} %collective-permute-done.6.rest_1_), channel_id=1, source_target_pairs={{0,16},{16,0},{1,17},{17,1},{2,18},{18,2},{3,19},{19,3},{4,20},{20... | collective-permute-start | bytes 786440 | tf_op jit(solution)/shard_map/ppermute | solution.py:315
  45.1 9.3 %project_own_columns.1 = (bf16[128,2048]{1,0:T(8,128)(2,1)}, bf16[128,2048]{1,0:T(8,128)(2,1)}, bf16[256,2048]{1,0:T(8,128)(2,1)}, bf16[256,256]{1,0:T(8,128)(2,...) custom-call(s32[8]{0:T(128)} %slots_ref.1, s32[1,2]{1,0:T(1,128)} %leave_ref.5, bf16[1024,8192]{1,0:T(8,128)(2,1)} %w_ref.3, ...), custom_call_target="tpu_custom_call" | custom-call | bytes 1024 | tf_op jit(solution)/shard_map/project_own_columns/pallas_call | solution.py:32
  55.1 1.5 %collective-permute-start.16 = (bf16[64,2048]{1,0:T(8,128)(2,1)}, bf16[64,2048]{1,0:T(8,128)(2,1)S(1)}, u32[]{:S(2)}, u32[]{:S(2)}) collective-permute-start(bf16[64,2048]{1,0:T(8,128)(2,1)} %collective-permute-done.13.rest_2_), channel_id=1, source_target_pairs={{0,16},{16,0},{1,17},{17,1},{2,18},{18,2},{3,19},{19,3},{4,20},{20... | collective-permute-start | bytes 786440 | tf_op jit(solution)/shard_map/ppermute | solution.py:315
  56.6 0.9 %collective-permute-done.17 = bf16[256,256]{1,0:T(8,128)(2,1)S(1)} collective-permute-done((bf16[256,256]{1,0:T(8,128)(2,1)}, bf16[256,256]{1,0:T(8,128)(2,1)S(1)}, u32[]{:S(2)}, u32[]{:S(2)}) %collective-permute-start.17) | collective-permute-done | bytes 131104 | tf_op jit(solution)/shard_map/ppermute | solution.py:318
  57.6 0.9 %add.19.rest_6_ = bf16[256,256]{1,0:T(8,128)(2,1)S(1)} add(bf16[256,256]{1,0:T(8,128)(2,1)} %get-tuple-element.53, bf16[256,256]{1,0:T(8,128)(2,1)S(1)} %collective-permute-done.17) | non-fusion elementwise | flops 65536 | bytes 393216 | tf_op jit(solution)/shard_map/add | solution.py:409
  58.5 2.0 %collective-permute-done.18.rest_9_ = bf16[256,2048]{1,0:T(8,128)(2,1)S(1)} collective-permute-done((bf16[256,2048]{1,0:T(8,128)(2,1)S(1)}, bf16[256,2048]{1,0:T(8,128)(2,1)S(1)}, u32[]{:S(2)}, u32[]{:S(2)}) %collective-permute-start.18) | collective-permute-done | bytes 1048608 | tf_op jit(solution)/shard_map/ppermute | solution.py:321
  60.5 1.5 %collective-permute-start.19 = (bf16[256,256]{1,0:T(8,128)(2,1)S(1)}, bf16[256,256]{1,0:T(8,128)(2,1)S(1)}, u32[]{:S(2)}, u32[]{:S(2)}) collective-permute-start(bf16[256,256]{1,0:T(8,128)(2,1)S(1)} %add.19.rest_6_), channel_id=1, source_target_pairs={{0,2},{1,3},{2,0},{3,1},{4,6},{5,7},{6,4},{7,5},{8,10},{9,11},{10,... | collective-permute-start | bytes 393224 | tf_op jit(solution)/shard_map/ppermute | solution.py:321
  62.0 2.0 %collective-permute-done.16.rest_5_ = bf16[64,2048]{1,0:T(8,128)(2,1)S(1)} collective-permute-done((bf16[64,2048]{1,0:T(8,128)(2,1)}, bf16[64,2048]{1,0:T(8,128)(2,1)S(1)}, u32[]{:S(2)}, u32[]{:S(2)}) %collective-permute-start.16) | collective-permute-done | bytes 262176 | tf_op jit(solution)/shard_map/ppermute | solution.py:315
  64.0 1.4 %collective-permute-done.19.rest_7_.rest_8_ = bf16[256,256]{1,0:T(8,128)(2,1)S(1)} collective-permute-done((bf16[256,256]{1,0:T(8,128)(2,1)S(1)}, bf16[256,256]{1,0:T(8,128)(2,1)S(1)}, u32[]{:S(2)}, u32[]{:S(2)}) %collective-permute-start.19) | collective-permute-done | bytes 131104 | tf_op jit(solution)/shard_map/ppermute | solution.py:321
  66.1 5.5 %combine.1 = bf16[256,2048]{1,0:T(8,128)(2,1)} custom-call(s32[1,2]{1,0:T(1,128)} %leave_ref.5, f32[256,128]{1,0:T(8,128)} %get-tuple-element.45.slot_ref, bf16[256,2048]{1,0:T(8,128)(2,1)} %get-tuple-element.46.own_ref, bf16[128,2048]{1,0:T(8,128)(2,1)} %copy-done.6, bf16[128,2048]{1,0:T(8,128)(2,1)} %copy-done.7, bf16[2,64,2048]{2,1,0:T(8,128)(2,1)} %own_up.1, ...), custom_call_target="tpu_custom_call" | custom-call | flops 5750000128 | bytes 1024 | tf_op jit(solution)/shard_map/combine/pallas_call | solution.py:417
  (46 shorter events, 6.6 us)
Async XLA Ops:
  1.9 18.9 %collective-permute-start.2 = (bf16[64,1024]{1,0:T(8,128)(2,1)}, bf16[64,1024]{1,0:T(8,128)(2,1)}, u32[]{:S(2)}, u32[]{:S(2)}) collective-permute-start(bf16[64,1024]{1,0:T(8,128)(2,1)} %get-tuple-element.34), channel_id=1, source_target_pairs={{0,8},{4,12},{8,0},{12,4},{1,9},{5,13},{9,1},{13,5},{2,10},{6,14},... | collective-permute-start | bytes 393224 | tf_op jit(solution)/shard_map/ppermute | solution.py:312
  6.0 14.9 %collective-permute-start.1 = (bf16[64,1024]{1,0:T(8,128)(2,1)}, bf16[64,1024]{1,0:T(8,128)(2,1)}, u32[]{:S(2)}, u32[]{:S(2)}) collective-permute-start(bf16[64,1024]{1,0:T(8,128)(2,1)} %get-tuple-element.34), channel_id=1, source_target_pairs={{0,4},{4,0},{8,12},{12,8},{1,5},{5,1},{9,13},{13,9},{2,6},{6,2},{1... | collective-permute-start | bytes 393224 | tf_op jit(solution)/shard_map/ppermute | solution.py:312
  7.5 16.4 %collective-permute-start.6 = (bf16[64,2048]{1,0:T(8,128)(2,1)}, bf16[64,2048]{1,0:T(8,128)(2,1)}, u32[]{:S(2)}, u32[]{:S(2)}) collective-permute-start(bf16[64,2048]{1,0:T(8,128)(2,1)} %get-tuple-element.39), channel_id=1, source_target_pairs={{0,8},{4,12},{8,0},{12,4},{1,9},{5,13},{9,1},{13,5},{2,10},{6,14},... | collective-permute-start | bytes 786440 | tf_op jit(solution)/shard_map/ppermute | solution.py:312
  7.9 16.2 %collective-permute-start.7 = (bf16[64,2048]{1,0:T(8,128)(2,1)}, bf16[64,2048]{1,0:T(8,128)(2,1)}, u32[]{:S(2)}, u32[]{:S(2)}) collective-permute-start(bf16[64,2048]{1,0:T(8,128)(2,1)} %get-tuple-element.39), channel_id=1, source_target_pairs={{0,4},{4,0},{8,12},{12,8},{1,5},{5,1},{9,13},{13,9},{2,6},{6,2},{1... | collective-permute-start | bytes 786440 | tf_op jit(solution)/shard_map/ppermute | solution.py:312
  24.1 10.2 %collective-permute-start.8 = (bf16[256,2048]{1,0:T(8,128)(2,1)}, bf16[256,2048]{1,0:T(8,128)(2,1)S(1)}, u32[]{:S(2)}, u32[]{:S(2)}) collective-permute-start(bf16[256,2048]{1,0:T(8,128)(2,1)} %get-tuple-element.40), channel_id=1, source_target_pairs={{0,1},{1,0},{2,3},{3,2},{4,5},{5,4},{6,7},{7,6},{8,9},{9,8},{10,11... | collective-permute-start | bytes 3145736 | tf_op jit(solution)/shard_map/ppermute | solution.py:318
  24.1 4.9 %collective-permute-start = (bf16[32,1152]{1,0:T(8,128)(2,1)}, bf16[32,1152]{1,0:T(8,128)(2,1)S(1)}, u32[]{:S(2)}, u32[]{:S(2)}) collective-permute-start(bf16[32,1152]{1,0:T(8,128)(2,1)} %get-tuple-element.33), channel_id=1, source_target_pairs={{0,4},{4,0},{8,12},{12,8},{1,5},{5,1},{9,13},{13,9},{2,6},{6,2},{1... | collective-permute-start | bytes 221192 | tf_op jit(solution)/shard_map/ppermute | solution.py:312
  25.6 6.5 %collective-permute-start.4 = (bf16[64,1024]{1,0:T(8,128)(2,1)}, bf16[64,1024]{1,0:T(8,128)(2,1)S(1)}, u32[]{:S(2)}, u32[]{:S(2)}) collective-permute-start(bf16[64,1024]{1,0:T(8,128)(2,1)} %collective-permute-done.2.rest_3_), channel_id=1, source_target_pairs={{0,16},{16,0},{1,17},{17,1},{2,18},{18,2},{3,19},{19,3},{4,20},{20... | collective-permute-start | bytes 393224 | tf_op jit(solution)/shard_map/ppermute | solution.py:315
  27.1 5.6 %collective-permute-start.3 = (bf16[64,1024]{1,0:T(8,128)(2,1)}, bf16[64,1024]{1,0:T(8,128)(2,1)S(1)}, u32[]{:S(2)}, u32[]{:S(2)}) collective-permute-start(bf16[64,1024]{1,0:T(8,128)(2,1)} %collective-permute-done.2.rest_3_), channel_id=1, source_target_pairs={{0,4},{4,0},{8,12},{12,8},{1,5},{5,1},{9,13},{13,9},{2,6},{6,2},{1... | collective-permute-start | bytes 393224 | tf_op jit(solution)/shard_map/ppermute | solution.py:312
  27.7 6.5 %collective-permute-start.5 = (bf16[64,1024]{1,0:T(8,128)(2,1)}, bf16[64,1024]{1,0:T(8,128)(2,1)S(1)}, u32[]{:S(2)}, u32[]{:S(2)}) collective-permute-start(bf16[64,1024]{1,0:T(8,128)(2,1)} %collective-permute-done.1.rest_2_), channel_id=1, source_target_pairs={{0,16},{16,0},{1,17},{17,1},{2,18},{18,2},{3,19},{19,3},{4,20},{20... | collective-permute-start | bytes 393224 | tf_op jit(solution)/shard_map/ppermute | solution.py:315
  29.8 9.2 %collective-permute-start.9 = (bf16[16,1152]{1,0:T(8,128)(2,1)S(1)}, bf16[16,1152]{1,0:T(8,128)(2,1)S(1)}, u32[]{:S(2)}, u32[]{:S(2)}) collective-permute-start(bf16[16,1152]{1,0:T(8,128)(2,1)S(1)} %slice_add_fusion), channel_id=1, source_target_pairs={{0,8},{4,12},{8,0},{12,4},{1,9},{5,13},{9,1},{13,5},{2,10},{6,14},... | collective-permute-start | bytes 110600 | tf_op jit(solution)/shard_map/ppermute | solution.py:312
  32.2 12.9 %copy-start = (bf16[64,1024]{1,0:T(8,128)(2,1)}, bf16[64,1024]{1,0:T(8,128)(2,1)S(1)}, u32[]{:S(2)}) copy-start(bf16[64,1024]{1,0:T(8,128)(2,1)S(1)} %collective-permute-done.4.rest_6_) | copy-start | bytes 393220
  32.7 12.4 %copy-start.1 = (bf16[64,1024]{1,0:T(8,128)(2,1)}, bf16[64,1024]{1,0:T(8,128)(2,1)S(1)}, u32[]{:S(2)}) copy-start(bf16[64,1024]{1,0:T(8,128)(2,1)S(1)} %collective-permute-done.3.rest_4_) | copy-start | bytes 393220
  34.3 10.8 %copy-start.2 = (bf16[64,1024]{1,0:T(8,128)(2,1)}, bf16[64,1024]{1,0:T(8,128)(2,1)S(1)}, u32[]{:S(2)}) copy-start(bf16[64,1024]{1,0:T(8,128)(2,1)S(1)} %collective-permute-done.5.rest_5_) | copy-start | bytes 393220
  35.9 24.5 %collective-permute-start.18 = (bf16[256,2048]{1,0:T(8,128)(2,1)S(1)}, bf16[256,2048]{1,0:T(8,128)(2,1)S(1)}, u32[]{:S(2)}, u32[]{:S(2)}) collective-permute-start(bf16[256,2048]{1,0:T(8,128)(2,1)S(1)} %add.15), channel_id=1, source_target_pairs={{0,2},{1,3},{2,0},{3,1},{4,6},{5,7},{6,4},{7,5},{8,10},{9,11},{10,... | collective-permute-start | bytes 3145736 | tf_op jit(solution)/shard_map/ppermute | solution.py:321
  37.5 5.0 %collective-permute-start.10 = (bf16[64,1024]{1,0:T(8,128)(2,1)S(1)}, bf16[64,1024]{1,0:T(8,128)(2,1)S(1)}, u32[]{:S(2)}, u32[]{:S(2)}) collective-permute-start(bf16[64,1024]{1,0:T(8,128)(2,1)S(1)} %collective-permute-done.3.rest_4_), channel_id=1, source_target_pairs={{0,16},{16,0},{1,17},{17,1},{2,18},{18,2},{3,19},{19,3},{4,20},{20... | collective-permute-start | bytes 393224 | tf_op jit(solution)/shard_map/ppermute | solution.py:315
  42.5 12.1 %collective-permute-start.15 = (bf16[64,2048]{1,0:T(8,128)(2,1)}, bf16[64,2048]{1,0:T(8,128)(2,1)S(1)}, u32[]{:S(2)}, u32[]{:S(2)}) collective-permute-start(bf16[64,2048]{1,0:T(8,128)(2,1)} %collective-permute-done.6.rest_1_), channel_id=1, source_target_pairs={{0,16},{16,0},{1,17},{17,1},{2,18},{18,2},{3,19},{19,3},{4,20},{20... | collective-permute-start | bytes 786440 | tf_op jit(solution)/shard_map/ppermute | solution.py:315
  44.0 11.0 %collective-permute-start.14 = (bf16[64,2048]{1,0:T(8,128)(2,1)}, bf16[64,2048]{1,0:T(8,128)(2,1)}, u32[]{:S(2)}, u32[]{:S(2)}) collective-permute-start(bf16[64,2048]{1,0:T(8,128)(2,1)} %collective-permute-done.7.rest_0_), channel_id=1, source_target_pairs={{0,16},{16,0},{1,17},{17,1},{2,18},{18,2},{3,19},{19,3},{4,20},{20... | collective-permute-start | bytes 786440 | tf_op jit(solution)/shard_map/ppermute | solution.py:315
  44.5 10.6 %collective-permute-start.13 = (bf16[64,2048]{1,0:T(8,128)(2,1)}, bf16[64,2048]{1,0:T(8,128)(2,1)}, u32[]{:S(2)}, u32[]{:S(2)}) collective-permute-start(bf16[64,2048]{1,0:T(8,128)(2,1)} %collective-permute-done.6.rest_1_), channel_id=1, source_target_pairs={{0,4},{4,0},{8,12},{12,8},{1,5},{5,1},{9,13},{13,9},{2,6},{6,2},{1... | collective-permute-start | bytes 786440 | tf_op jit(solution)/shard_map/ppermute | solution.py:312
  54.4 9.5 %collective-permute-start.11 = (bf16[128,2048]{1,0:T(8,128)(2,1)}, bf16[128,2048]{1,0:T(8,128)(2,1)S(1)}, u32[]{:S(2)}, u32[]{:S(2)}) collective-permute-start(bf16[128,2048]{1,0:T(8,128)(2,1)} %get-tuple-element.47), channel_id=1, source_target_pairs={{0,1},{1,0},{2,3},{3,2},{4,5},{5,4},{6,7},{7,6},{8,9},{9,8},{10,11... | collective-permute-start | bytes 1572872 | tf_op jit(solution)/shard_map/ppermute | solution.py:318
  54.5 10.9 %copy-start.8 = (bf16[64,2048]{1,0:T(8,128)(2,1)}, bf16[64,2048]{1,0:T(8,128)(2,1)S(1)}, u32[]{:S(2)}) copy-start(bf16[64,2048]{1,0:T(8,128)(2,1)S(1)} %collective-permute-done.15.rest_4_) | copy-start | bytes 786436
  54.5 9.4 %collective-permute-start.12 = (bf16[128,2048]{1,0:T(8,128)(2,1)}, bf16[128,2048]{1,0:T(8,128)(2,1)S(1)}, u32[]{:S(2)}, u32[]{:S(2)}) collective-permute-start(bf16[128,2048]{1,0:T(8,128)(2,1)} %get-tuple-element.48), channel_id=1, source_target_pairs={{0,1},{1,0},{2,3},{3,2},{4,5},{5,4},{6,7},{7,6},{8,9},{9,8},{10,11... | collective-permute-start | bytes 1572872 | tf_op jit(solution)/shard_map/ppermute | solution.py:318
  55.0 2.5 %collective-permute-start.17 = (bf16[256,256]{1,0:T(8,128)(2,1)}, bf16[256,256]{1,0:T(8,128)(2,1)S(1)}, u32[]{:S(2)}, u32[]{:S(2)}) collective-permute-start(bf16[256,256]{1,0:T(8,128)(2,1)} %get-tuple-element.55), channel_id=1, source_target_pairs={{0,1},{1,0},{2,3},{3,2},{4,5},{5,4},{6,7},{7,6},{8,9},{9,8},{10,11... | collective-permute-start | bytes 393224 | tf_op jit(solution)/shard_map/ppermute | solution.py:318
  55.1 8.9 %collective-permute-start.16 = (bf16[64,2048]{1,0:T(8,128)(2,1)}, bf16[64,2048]{1,0:T(8,128)(2,1)S(1)}, u32[]{:S(2)}, u32[]{:S(2)}) collective-permute-start(bf16[64,2048]{1,0:T(8,128)(2,1)} %collective-permute-done.13.rest_2_), channel_id=1, source_target_pairs={{0,16},{16,0},{1,17},{17,1},{2,18},{18,2},{3,19},{19,3},{4,20},{20... | collective-permute-start | bytes 786440 | tf_op jit(solution)/shard_map/ppermute | solution.py:315
  60.5 5.0 %collective-permute-start.19 = (bf16[256,256]{1,0:T(8,128)(2,1)S(1)}, bf16[256,256]{1,0:T(8,128)(2,1)S(1)}, u32[]{:S(2)}, u32[]{:S(2)}) collective-permute-start(bf16[256,256]{1,0:T(8,128)(2,1)S(1)} %add.19.rest_6_), channel_id=1, source_target_pairs={{0,2},{1,3},{2,0},{3,1},{4,6},{5,7},{6,4},{7,5},{8,10},{9,11},{10,... | collective-permute-start | bytes 393224 | tf_op jit(solution)/shard_map/ppermute | solution.py:321
  (7 other events, 19.7 us)

commit v4 on v3

--- a/solution.py
+++ b/solution.py
@@ -45,7 +45,7 @@
     return jnp.broadcast_to(lane_row, (128, lane_row.shape[1])).T
 
 
-def attend(q_of, own_of, idx, lens, pool_ref, at, k_ref, v_ref, sems, bias_ref, s_ref, heads, store):
+def attend(q_of, own_of, idx, lens, pool_ref, at, k_ref, v_ref, sems, bias_ref, s_ref, heads, store, begin):
     rows = idx.shape[1]
     D = HEAD_SIZE
     nblk, bs, _ = pool_ref.shape
@@ -86,14 +86,16 @@
     own = own_of().astype(F32)
     own_k, own_v = own[:, :D], own[:, D:]
     k_copy.wait()
-    v_copy.wait()
     keys = k_ref[...].reshape(npos, D)
-    values = v_ref[...].reshape(npos, 2 * D)
     nt = (((1,), (1,)), ((), ()))
     before = None
     width = 1024
     for h in range(heads + 1):
         top = acc = None
+        if h == 1:
+            v_copy.wait()
+            begin()
+            values = v_ref[...].reshape(npos, 2 * D)
         for w in range(0, npos, width):
             if h < heads:
                 s = lax.dot_general(q_of(h), keys[w : w + width], nt, preferred_element_type=F32)
@@ -148,16 +150,18 @@
     copies = weight_copies(w_ref, held, wsem, chip_blocks(t, chips))
 
     def own_of():
+        own_copy.wait()
+        return fresh[...]
+
+    def begin():
         for c in copies:
             c.start()
-        own_copy.wait()
-        return fresh[...]
 
     def store(h, out):
         attn_ref[:, h * D : (h + 1) * D] = out
 
     attend(lambda h: q_ref[:, h * D : (h + 1) * D], own_of, idx_ref[...].astype(F32),
-           len_ref[...].astype(F32), pool_ref, at, k_ref, v_ref, psem, bias, s, channels // D, store)
+           len_ref[...].astype(F32), pool_ref, at, k_ref, v_ref, psem, bias, s, channels // D, store, begin)
     a = attn_ref[...]
     width = held.shape[2]
     for i, c in enumerate(copies):
@@ -376,13 +380,11 @@
     sends[0] = after(sends[0], *down_near.values(), *up_near.values())
     down_same = passed(mine_down, {k: after(v, attn) for k, v in down_near.items()})
     down_swapped = {k: swap(after(v, attn)) for k, v in down_near.items()}
-    totals = [
-        after(keep, first, *down_same, *down_swapped.values()) + core(send) for send, keep in zip(sends, keeps)
-    ]
+    totals = [after(keep, first) + core(send) for send, keep in zip(sends, keeps)]
     pays = [pay + first[PAD * i : PAD * (i + 1)] for i, pay in enumerate(pays)]
     bit = 2
     while len(pays) > 1:
-        got = across(jnp.concatenate(pays[1::2], 0), bit)
+        got = after(across(after(jnp.concatenate(pays[1::2], 0), *totals), bit), *down_same, *down_swapped.values())
         pays = [pay + got[PAD * i : PAD * (i + 1)] for i, pay in enumerate(pays[::2])]
         bit *= 2
     arrived = pays
@@ -410,7 +412,7 @@
     pack = after(pack, *x_in[0])
     packs = [pack[:rows]] + [chip(pack[(d - 1) * rows : d * rows], d) for d in range(1, chips)]
 
-    tile = cols // 4
+    tile = cols // 2
     col = lambda n: pl.BlockSpec((n, tile), lambda i: (0, i))
     still = lambda *shape: pl.BlockSpec(shape, lambda i: (0,) * len(shape))
     strip = pl.BlockSpec((PAD * tile // 128, 128), lambda i: (i, 0))

time: 72.3 us -> 69.7 us (0.964)
  waiting for transfers between devices: 14.9 us -> 10.9 us
  starting transfers between devices: 21.5 us -> 23.3 us
    ppermute x2, waiting for transfers between devices: 3.41 us -> 0.74 us  [chip(): lax.ppermute(v, 'tensor', [(i, (i + 2 * d) % tensors) for i in range(tens...]
    ppermute x8, starting transfers between devices: 10.8 us -> 12.6 us  [across(): return lax.ppermute(v, 'replica', [(i, i ^ k) for i in range(members)])]
  transfers between devices with their start and end apart: 20 -> 20, of which waited for: 11 -> 8; matrix products, arithmetic and copies ran while one was open for 7% -> 7% of each run, Pallas kernels for 30% -> 31%
where the time goes in v4:
time: 69.7 us; the launch traced here: 69.3 us
  Pallas kernels  28.3 us (41%)
  starting transfers between devices  23.3 us (33%)
  waiting for transfers between devices  10.9 us (16%)
  other arithmetic  4.78 us (7%)
  local copies, waits for them, and re-layouts  1.02 us (1%)
  between operations  0.94 us (1%)
    pallas_call x3, Pallas kernels, call(): pl.pallas_call(body, out_shape=out_shape, in_specs=in_specs, out_specs=[V...  23.5 us
    ppermute x8, starting transfers between devices, across(): return lax.ppermute(v, 'replica', [(i, i ^ k) for i in range(members)])  12.6 us
    ppermute x6, starting transfers between devices, swap(): return lax.ppermute(v, 'groups', [(0, 1), (1, 0)])  7.15 us
    ppermute x6, waiting for transfers between devices, swap(): return lax.ppermute(v, 'groups', [(0, 1), (1, 0)])  5.35 us
    pallas_call x1, Pallas kernels, on_device(): pl.pallas_call(functools.partial(final_kernel, members, groups, chips), g...  4.82 us
    ppermute x8, waiting for transfers between devices, across(): return lax.ppermute(v, 'replica', [(i, i ^ k) for i in range(members)])  4.03 us
    ppermute x2, starting transfers between devices, chip(): lax.ppermute(v, 'tensor', [(i, (i + 2 * d) % tensors) for i in range(tens...  2.98 us
    add x1, other arithmetic, on_device(): after(keep, first) + core(send)  1.61 us
  transfers between devices with their start and end apart: 20, of which 8 were waited for; matrix products, arithmetic and copies ran while one was open for 7% of the time, Pallas kernels for 31%

profile of v4, /device:TPU:0, one launch (start us, length us, event | category | flops | bytes accessed | tf_op | source)
XLA Modules:
  0.0 69.3 jit_solution(8244948718580414224)
XLA Ops:
  0.0 1.9 %slices_of_this_group.1 = (bf16[64,1024]{1,0:T(8,128)(2,1)}, bf16[64,2048]{1,0:T(8,128)(2,1)}) custom-call(bf16[2,64,1024]{2,1,0:T(8,128)(2,1)} %bitcast.4, bf16[2,64,2048]{2,1,0:T(8,128)(2,1)} %own_up.1), custom_call_target="tpu_custom_call" | custom-call | bytes 1024 | tf_op jit(solution)/shard_map/slices_of_this_group/pallas_call | solution.py:32
  1.9 4.0 %collective-permute-start.3 = (bf16[64,2048]{1,0:T(8,128)(2,1)}, bf16[64,2048]{1,0:T(8,128)(2,1)}, u32[]{:S(2)}, u32[]{:S(2)}) collective-permute-start(bf16[64,2048]{1,0:T(8,128)(2,1)} %get-tuple-element.39), channel_id=1, source_target_pairs={{0,8},{4,12},{8,0},{12,4},{1,9},{5,13},{9,1},{13,5},{2,10},{6,14},... | collective-permute-start | bytes 786440 | tf_op jit(solution)/shard_map/ppermute | solution.py:316
  6.0 1.6 %collective-permute-start.4 = (bf16[64,2048]{1,0:T(8,128)(2,1)}, bf16[64,2048]{1,0:T(8,128)(2,1)}, u32[]{:S(2)}, u32[]{:S(2)}) collective-permute-start(bf16[64,2048]{1,0:T(8,128)(2,1)} %get-tuple-element.39), channel_id=1, source_target_pairs={{0,4},{4,0},{8,12},{12,8},{1,5},{5,1},{9,13},{13,9},{2,6},{6,2},{1... | collective-permute-start | bytes 786440 | tf_op jit(solution)/shard_map/ppermute | solution.py:316
  8.6 12.2 %attend_and_project.1 = (bf16[256,1024]{1,0:T(8,128)(2,1)}, bf16[256,2048]{1,0:T(8,128)(2,1)}, bf16[256,2048]{1,0:T(8,128)(2,1)}, bf16[16,1152]{1,0:T(8,128)(2,1...) custom-call(s32[1,2]{1,0:T(1,128)} %leave_ref.5, s32[1]{0:T(128)S(6)} %copy.13.recv_ref, bf16[256,1024]{1,0:T(8,128)(2,1)} %q_ref.1, ...), custom_call_target="tpu_custom_call" | custom-call | flops 230000001024 | bytes 1024 | tf_op jit(solution)/shard_map/attend_and_project/pallas_call | solution.py:32
  20.9 3.1 %collective-permute-done.1.rest_3_ = bf16[64,1024]{1,0:T(8,128)(2,1)} collective-permute-done((bf16[64,1024]{1,0:T(8,128)(2,1)}, bf16[64,1024]{1,0:T(8,128)(2,1)}, u32[]{:S(2)}, u32[]{:S(2)}) %collective-permute-start.1) | collective-permute-done | bytes 131104 | tf_op jit(solution)/shard_map/ppermute | solution.py:316
  24.1 1.6 %collective-permute-start = (bf16[32,1152]{1,0:T(8,128)(2,1)}, bf16[32,1152]{1,0:T(8,128)(2,1)S(1)}, u32[]{:S(2)}, u32[]{:S(2)}) collective-permute-start(bf16[32,1152]{1,0:T(8,128)(2,1)} %get-tuple-element.35), channel_id=1, source_target_pairs={{0,4},{4,0},{8,12},{12,8},{1,5},{5,1},{9,13},{13,9},{2,6},{6,2},{1... | collective-permute-start | bytes 221192 | tf_op jit(solution)/shard_map/ppermute | solution.py:316
  25.7 1.5 %collective-permute-start.8 = (bf16[64,1024]{1,0:T(8,128)(2,1)}, bf16[64,1024]{1,0:T(8,128)(2,1)S(1)}, u32[]{:S(2)}, u32[]{:S(2)}) collective-permute-start(bf16[64,1024]{1,0:T(8,128)(2,1)} %collective-permute-done.1.rest_3_), channel_id=1, source_target_pairs={{0,16},{16,0},{1,17},{17,1},{2,18},{18,2},{3,19},{19,3},{4,20},{20... | collective-permute-start | bytes 393224 | tf_op jit(solution)/shard_map/ppermute | solution.py:319
  28.2 0.8 %collective-permute-done = bf16[32,1152]{1,0:T(8,128)(2,1)S(1)} collective-permute-done((bf16[32,1152]{1,0:T(8,128)(2,1)}, bf16[32,1152]{1,0:T(8,128)(2,1)S(1)}, u32[]{:S(2)}, u32[]{:S(2)}) %collective-permute-start) | collective-permute-done | bytes 73760 | tf_op jit(solution)/shard_map/ppermute | solution.py:316
  29.0 0.8 %slice_add_fusion = bf16[16,1152]{1,0:T(8,128)(2,1)S(1)} fusion(bf16[16,1152]{1,0:T(8,128)(2,1)} %get-tuple-element.43, bf16[32,1152]{1,0:T(8,128)(2,1)S(1)} %collective-permute-done), kind=kLoop, calls=%fused_computation | loop fusion | flops 18432 | bytes 110592 | tf_op jit(solution)/shard_map/add | solution.py:384
  29.8 1.6 %add.15 = bf16[256,2048]{1,0:T(8,128)(2,1)S(1)} add(bf16[256,2048]{1,0:T(8,128)(2,1)} %get-tuple-element.36, bf16[256,2048]{1,0:T(8,128)(2,1)S(1)} %collective-permute-done.5) | non-fusion elementwise | flops 524288 | bytes 3145728 | tf_op jit(solution)/shard_map/add | solution.py:383
  31.4 2.2 %collective-permute-start.6 = (bf16[16,1152]{1,0:T(8,128)(2,1)S(1)}, bf16[16,1152]{1,0:T(8,128)(2,1)S(1)}, u32[]{:S(2)}, u32[]{:S(2)}) collective-permute-start(bf16[16,1152]{1,0:T(8,128)(2,1)S(1)} %slice_add_fusion), channel_id=1, source_target_pairs={{0,8},{4,12},{8,0},{12,4},{1,9},{5,13},{9,1},{13,5},{2,10},{6,14},... | collective-permute-start | bytes 110600 | tf_op jit(solution)/shard_map/ppermute | solution.py:316
  33.7 1.5 %collective-permute-start.18 = (bf16[256,2048]{1,0:T(8,128)(2,1)S(1)}, bf16[256,2048]{1,0:T(8,128)(2,1)S(1)}, u32[]{:S(2)}, u32[]{:S(2)}) collective-permute-start(bf16[256,2048]{1,0:T(8,128)(2,1)S(1)} %add.15), channel_id=1, source_target_pairs={{0,2},{1,3},{2,0},{3,1},{4,6},{5,7},{6,4},{7,5},{8,10},{9,11},{10,... | collective-permute-start | bytes 3145736 | tf_op jit(solution)/shard_map/ppermute | solution.py:325
  35.2 1.5 %collective-permute-start.10 = (bf16[64,1024]{1,0:T(8,128)(2,1)S(1)}, bf16[64,1024]{1,0:T(8,128)(2,1)S(1)}, u32[]{:S(2)}, u32[]{:S(2)}) collective-permute-start(bf16[64,1024]{1,0:T(8,128)(2,1)S(1)} %collective-permute-done.7.rest_4_), channel_id=1, source_target_pairs={{0,16},{16,0},{1,17},{17,1},{2,18},{18,2},{3,19},{19,3},{4,20},{20... | collective-permute-start | bytes 393224 | tf_op jit(solution)/shard_map/ppermute | solution.py:319
  36.7 1.4 %fusion.rest_0_ = bf16[16,1152]{1,0:T(8,128)(2,1)} fusion(bf16[16,1152]{1,0:T(8,128)(2,1)S(1)} %collective-permute-done.6, bf16[16,1152]{1,0:T(8,128)(2,1)} %get-tuple-element.42, bf16[32,1152]{1,0:T(8,128)(2,1)S(1)} %collective-permute-done), kind=kLoop, calls=%fused_computation.2 | loop fusion | flops 36864 | bytes 147456 | tf_op jit(solution)/shard_map/add | solution.py:388
  38.2 2.0 %collective-permute-done.10.rest_7_ = bf16[64,1024]{1,0:T(8,128)(2,1)S(1)} collective-permute-done((bf16[64,1024]{1,0:T(8,128)(2,1)S(1)}, bf16[64,1024]{1,0:T(8,128)(2,1)S(1)}, u32[]{:S(2)}, u32[]{:S(2)}) %collective-permute-start.10) | collective-permute-done | bytes 131104 | tf_op jit(solution)/shard_map/ppermute | solution.py:319
  40.1 1.5 %collective-permute-start.15 = (bf16[64,2048]{1,0:T(8,128)(2,1)}, bf16[64,2048]{1,0:T(8,128)(2,1)S(1)}, u32[]{:S(2)}, u32[]{:S(2)}) collective-permute-start(bf16[64,2048]{1,0:T(8,128)(2,1)} %collective-permute-done.3.rest_1_), channel_id=1, source_target_pairs={{0,16},{16,0},{1,17},{17,1},{2,18},{18,2},{3,19},{19,3},{4,20},{20... | collective-permute-start | bytes 786440 | tf_op jit(solution)/shard_map/ppermute | solution.py:319
  42.2 2.1 %collective-permute-start.13 = (bf16[64,2048]{1,0:T(8,128)(2,1)}, bf16[64,2048]{1,0:T(8,128)(2,1)}, u32[]{:S(2)}, u32[]{:S(2)}) collective-permute-start(bf16[64,2048]{1,0:T(8,128)(2,1)} %collective-permute-done.3.rest_1_), channel_id=1, source_target_pairs={{0,4},{4,0},{8,12},{12,8},{1,5},{5,1},{9,13},{13,9},{2,6},{6,2},{1... | collective-permute-start | bytes 786440 | tf_op jit(solution)/shard_map/ppermute | solution.py:316
  44.3 9.3 %project_own_columns.1 = (bf16[128,2048]{1,0:T(8,128)(2,1)}, bf16[128,2048]{1,0:T(8,128)(2,1)}, bf16[256,2048]{1,0:T(8,128)(2,1)}, bf16[256,256]{1,0:T(8,128)(2,...) custom-call(s32[8]{0:T(128)} %slots_ref.1, s32[1,2]{1,0:T(1,128)} %leave_ref.5, bf16[1024,8192]{1,0:T(8,128)(2,1)} %w_ref.3, ...), custom_call_target="tpu_custom_call" | custom-call | bytes 1024 | tf_op jit(solution)/shard_map/project_own_columns/pallas_call | solution.py:32
  54.3 1.6 %collective-permute-start.16 = (bf16[64,2048]{1,0:T(8,128)(2,1)}, bf16[64,2048]{1,0:T(8,128)(2,1)S(1)}, u32[]{:S(2)}, u32[]{:S(2)}) collective-permute-start(bf16[64,2048]{1,0:T(8,128)(2,1)} %collective-permute-done.13.rest_2_), channel_id=1, source_target_pairs={{0,16},{16,0},{1,17},{17,1},{2,18},{18,2},{3,19},{19,3},{4,20},{20... | collective-permute-start | bytes 786440 | tf_op jit(solution)/shard_map/ppermute | solution.py:319
  55.9 0.8 %collective-permute-done.17 = bf16[256,256]{1,0:T(8,128)(2,1)S(1)} collective-permute-done((bf16[256,256]{1,0:T(8,128)(2,1)}, bf16[256,256]{1,0:T(8,128)(2,1)S(1)}, u32[]{:S(2)}, u32[]{:S(2)}) %collective-permute-start.17) | collective-permute-done | bytes 131104 | tf_op jit(solution)/shard_map/ppermute | solution.py:322
  56.7 0.9 %add.19.rest_6_ = bf16[256,256]{1,0:T(8,128)(2,1)S(1)} add(bf16[256,256]{1,0:T(8,128)(2,1)} %get-tuple-element.57, bf16[256,256]{1,0:T(8,128)(2,1)S(1)} %collective-permute-done.17) | non-fusion elementwise | flops 65536 | bytes 393216 | tf_op jit(solution)/shard_map/add | solution.py:411
  58.3 1.5 %collective-permute-start.19 = (bf16[256,256]{1,0:T(8,128)(2,1)S(1)}, bf16[256,256]{1,0:T(8,128)(2,1)S(1)}, u32[]{:S(2)}, u32[]{:S(2)}) collective-permute-start(bf16[256,256]{1,0:T(8,128)(2,1)S(1)} %add.19.rest_6_), channel_id=1, source_target_pairs={{0,2},{1,3},{2,0},{3,1},{4,6},{5,7},{6,4},{7,5},{8,10},{9,11},{10,... | collective-permute-start | bytes 393224 | tf_op jit(solution)/shard_map/ppermute | solution.py:325
  59.8 3.4 %collective-permute-done.16.rest_5_ = bf16[64,2048]{1,0:T(8,128)(2,1)S(1)} collective-permute-done((bf16[64,2048]{1,0:T(8,128)(2,1)}, bf16[64,2048]{1,0:T(8,128)(2,1)S(1)}, u32[]{:S(2)}, u32[]{:S(2)}) %collective-permute-start.16) | collective-permute-done | bytes 262176 | tf_op jit(solution)/shard_map/ppermute | solution.py:319
  64.3 4.8 %combine.1 = bf16[256,2048]{1,0:T(8,128)(2,1)} custom-call(s32[1,2]{1,0:T(1,128)} %leave_ref.5, f32[256,128]{1,0:T(8,128)} %get-tuple-element.49.slot_ref, bf16[256,2048]{1,0:T(8,128)(2,1)} %get-tuple-element.50.own_ref, bf16[128,2048]{1,0:T(8,128)(2,1)} %copy-done.6, bf16[128,2048]{1,0:T(8,128)(2,1)} %copy-done.7, bf16[2,64,2048]{2,1,0:T(8,128)(2,1)} %own_up.1, ...), custom_call_target="tpu_custom_call" | custom-call | flops 5750000128 | bytes 1024 | tf_op jit(solution)/shard_map/combine/pallas_call | solution.py:419
  (46 shorter events, 4.6 us)
Async XLA Ops:
  1.9 22.2 %collective-permute-start.3 = (bf16[64,2048]{1,0:T(8,128)(2,1)}, bf16[64,2048]{1,0:T(8,128)(2,1)}, u32[]{:S(2)}, u32[]{:S(2)}) collective-permute-start(bf16[64,2048]{1,0:T(8,128)(2,1)} %get-tuple-element.39), channel_id=1, source_target_pairs={{0,8},{4,12},{8,0},{12,4},{1,9},{5,13},{9,1},{13,5},{2,10},{6,14},... | collective-permute-start | bytes 786440 | tf_op jit(solution)/shard_map/ppermute | solution.py:316
  6.0 18.2 %collective-permute-start.4 = (bf16[64,2048]{1,0:T(8,128)(2,1)}, bf16[64,2048]{1,0:T(8,128)(2,1)}, u32[]{:S(2)}, u32[]{:S(2)}) collective-permute-start(bf16[64,2048]{1,0:T(8,128)(2,1)} %get-tuple-element.39), channel_id=1, source_target_pairs={{0,4},{4,0},{8,12},{12,8},{1,5},{5,1},{9,13},{13,9},{2,6},{6,2},{1... | collective-permute-start | bytes 786440 | tf_op jit(solution)/shard_map/ppermute | solution.py:316
  7.5 16.4 %collective-permute-start.1 = (bf16[64,1024]{1,0:T(8,128)(2,1)}, bf16[64,1024]{1,0:T(8,128)(2,1)}, u32[]{:S(2)}, u32[]{:S(2)}) collective-permute-start(bf16[64,1024]{1,0:T(8,128)(2,1)} %get-tuple-element.38), channel_id=1, source_target_pairs={{0,8},{4,12},{8,0},{12,4},{1,9},{5,13},{9,1},{13,5},{2,10},{6,14},... | collective-permute-start | bytes 393224 | tf_op jit(solution)/shard_map/ppermute | solution.py:316
  7.9 16.2 %collective-permute-start.2 = (bf16[64,1024]{1,0:T(8,128)(2,1)}, bf16[64,1024]{1,0:T(8,128)(2,1)}, u32[]{:S(2)}, u32[]{:S(2)}) collective-permute-start(bf16[64,1024]{1,0:T(8,128)(2,1)} %get-tuple-element.38), channel_id=1, source_target_pairs={{0,4},{4,0},{8,12},{12,8},{1,5},{5,1},{9,13},{13,9},{2,6},{6,2},{1... | collective-permute-start | bytes 393224 | tf_op jit(solution)/shard_map/ppermute | solution.py:316
  24.1 5.7 %collective-permute-start.5 = (bf16[256,2048]{1,0:T(8,128)(2,1)}, bf16[256,2048]{1,0:T(8,128)(2,1)S(1)}, u32[]{:S(2)}, u32[]{:S(2)}) collective-permute-start(bf16[256,2048]{1,0:T(8,128)(2,1)} %get-tuple-element.40), channel_id=1, source_target_pairs={{0,1},{1,0},{2,3},{3,2},{4,5},{5,4},{6,7},{7,6},{8,9},{9,8},{10,11... | collective-permute-start | bytes 3145736 | tf_op jit(solution)/shard_map/ppermute | solution.py:322
  24.1 4.9 %collective-permute-start = (bf16[32,1152]{1,0:T(8,128)(2,1)}, bf16[32,1152]{1,0:T(8,128)(2,1)S(1)}, u32[]{:S(2)}, u32[]{:S(2)}) collective-permute-start(bf16[32,1152]{1,0:T(8,128)(2,1)} %get-tuple-element.35), channel_id=1, source_target_pairs={{0,4},{4,0},{8,12},{12,8},{1,5},{5,1},{9,13},{13,9},{2,6},{6,2},{1... | collective-permute-start | bytes 221192 | tf_op jit(solution)/shard_map/ppermute | solution.py:316
  25.7 11.0 %collective-permute-start.8 = (bf16[64,1024]{1,0:T(8,128)(2,1)}, bf16[64,1024]{1,0:T(8,128)(2,1)S(1)}, u32[]{:S(2)}, u32[]{:S(2)}) collective-permute-start(bf16[64,1024]{1,0:T(8,128)(2,1)} %collective-permute-done.1.rest_3_), channel_id=1, source_target_pairs={{0,16},{16,0},{1,17},{17,1},{2,18},{18,2},{3,19},{19,3},{4,20},{20... | collective-permute-start | bytes 393224 | tf_op jit(solution)/shard_map/ppermute | solution.py:319
  27.2 8.0 %collective-permute-start.7 = (bf16[64,1024]{1,0:T(8,128)(2,1)}, bf16[64,1024]{1,0:T(8,128)(2,1)S(1)}, u32[]{:S(2)}, u32[]{:S(2)}) collective-permute-start(bf16[64,1024]{1,0:T(8,128)(2,1)} %collective-permute-done.1.rest_3_), channel_id=1, source_target_pairs={{0,4},{4,0},{8,12},{12,8},{1,5},{5,1},{9,13},{13,9},{2,6},{6,2},{1... | collective-permute-start | bytes 393224 | tf_op jit(solution)/shard_map/ppermute | solution.py:316
  27.8 8.9 %collective-permute-start.9 = (bf16[64,1024]{1,0:T(8,128)(2,1)}, bf16[64,1024]{1,0:T(8,128)(2,1)S(1)}, u32[]{:S(2)}, u32[]{:S(2)}) collective-permute-start(bf16[64,1024]{1,0:T(8,128)(2,1)} %collective-permute-done.2.rest_2_), channel_id=1, source_target_pairs={{0,16},{16,0},{1,17},{17,1},{2,18},{18,2},{3,19},{19,3},{4,20},{20... | collective-permute-start | bytes 393224 | tf_op jit(solution)/shard_map/ppermute | solution.py:319
  31.4 5.3 %collective-permute-start.6 = (bf16[16,1152]{1,0:T(8,128)(2,1)S(1)}, bf16[16,1152]{1,0:T(8,128)(2,1)S(1)}, u32[]{:S(2)}, u32[]{:S(2)}) collective-permute-start(bf16[16,1152]{1,0:T(8,128)(2,1)S(1)} %slice_add_fusion), channel_id=1, source_target_pairs={{0,8},{4,12},{8,0},{12,4},{1,9},{5,13},{9,1},{13,5},{2,10},{6,14},... | collective-permute-start | bytes 110600 | tf_op jit(solution)/shard_map/ppermute | solution.py:316
  33.7 24.6 %collective-permute-start.18 = (bf16[256,2048]{1,0:T(8,128)(2,1)S(1)}, bf16[256,2048]{1,0:T(8,128)(2,1)S(1)}, u32[]{:S(2)}, u32[]{:S(2)}) collective-permute-start(bf16[256,2048]{1,0:T(8,128)(2,1)S(1)} %add.15), channel_id=1, source_target_pairs={{0,2},{1,3},{2,0},{3,1},{4,6},{5,7},{6,4},{7,5},{8,10},{9,11},{10,... | collective-permute-start | bytes 3145736 | tf_op jit(solution)/shard_map/ppermute | solution.py:325
  35.2 9.1 %copy-start.1 = (bf16[64,1024]{1,0:T(8,128)(2,1)}, bf16[64,1024]{1,0:T(8,128)(2,1)S(1)}, u32[]{:S(2)}) copy-start(bf16[64,1024]{1,0:T(8,128)(2,1)S(1)} %collective-permute-done.7.rest_4_) | copy-start | bytes 393220
  35.2 5.0 %collective-permute-start.10 = (bf16[64,1024]{1,0:T(8,128)(2,1)S(1)}, bf16[64,1024]{1,0:T(8,128)(2,1)S(1)}, u32[]{:S(2)}, u32[]{:S(2)}) collective-permute-start(bf16[64,1024]{1,0:T(8,128)(2,1)S(1)} %collective-permute-done.7.rest_4_), channel_id=1, source_target_pairs={{0,16},{16,0},{1,17},{17,1},{2,18},{18,2},{3,19},{19,3},{4,20},{20... | collective-permute-start | bytes 393224 | tf_op jit(solution)/shard_map/ppermute | solution.py:319
  36.7 7.6 %copy-start = (bf16[64,1024]{1,0:T(8,128)(2,1)}, bf16[64,1024]{1,0:T(8,128)(2,1)S(1)}, u32[]{:S(2)}) copy-start(bf16[64,1024]{1,0:T(8,128)(2,1)S(1)} %collective-permute-done.8.rest_6_) | copy-start | bytes 393220
  36.7 7.6 %copy-start.2 = (bf16[64,1024]{1,0:T(8,128)(2,1)}, bf16[64,1024]{1,0:T(8,128)(2,1)S(1)}, u32[]{:S(2)}) copy-start(bf16[64,1024]{1,0:T(8,128)(2,1)S(1)} %collective-permute-done.9.rest_5_) | copy-start | bytes 393220
  40.1 13.6 %collective-permute-start.15 = (bf16[64,2048]{1,0:T(8,128)(2,1)}, bf16[64,2048]{1,0:T(8,128)(2,1)S(1)}, u32[]{:S(2)}, u32[]{:S(2)}) collective-permute-start(bf16[64,2048]{1,0:T(8,128)(2,1)} %collective-permute-done.3.rest_1_), channel_id=1, source_target_pairs={{0,16},{16,0},{1,17},{17,1},{2,18},{18,2},{3,19},{19,3},{4,20},{20... | collective-permute-start | bytes 786440 | tf_op jit(solution)/shard_map/ppermute | solution.py:319
  41.6 12.6 %collective-permute-start.14 = (bf16[64,2048]{1,0:T(8,128)(2,1)}, bf16[64,2048]{1,0:T(8,128)(2,1)}, u32[]{:S(2)}, u32[]{:S(2)}) collective-permute-start(bf16[64,2048]{1,0:T(8,128)(2,1)} %collective-permute-done.4.rest_0_), channel_id=1, source_target_pairs={{0,16},{16,0},{1,17},{17,1},{2,18},{18,2},{3,19},{19,3},{4,20},{20... | collective-permute-start | bytes 786440 | tf_op jit(solution)/shard_map/ppermute | solution.py:319
  42.2 12.1 %collective-permute-start.13 = (bf16[64,2048]{1,0:T(8,128)(2,1)}, bf16[64,2048]{1,0:T(8,128)(2,1)}, u32[]{:S(2)}, u32[]{:S(2)}) collective-permute-start(bf16[64,2048]{1,0:T(8,128)(2,1)} %collective-permute-done.3.rest_1_), channel_id=1, source_target_pairs={{0,4},{4,0},{8,12},{12,8},{1,5},{5,1},{9,13},{13,9},{2,6},{6,2},{1... | collective-permute-start | bytes 786440 | tf_op jit(solution)/shard_map/ppermute | solution.py:316
  53.6 9.5 %collective-permute-start.11 = (bf16[128,2048]{1,0:T(8,128)(2,1)}, bf16[128,2048]{1,0:T(8,128)(2,1)S(1)}, u32[]{:S(2)}, u32[]{:S(2)}) collective-permute-start(bf16[128,2048]{1,0:T(8,128)(2,1)} %get-tuple-element.51), channel_id=1, source_target_pairs={{0,1},{1,0},{2,3},{3,2},{4,5},{5,4},{6,7},{7,6},{8,9},{9,8},{10,11... | collective-permute-start | bytes 1572872 | tf_op jit(solution)/shard_map/ppermute | solution.py:322
  53.7 9.6 %copy-start.8 = (bf16[64,2048]{1,0:T(8,128)(2,1)}, bf16[64,2048]{1,0:T(8,128)(2,1)S(1)}, u32[]{:S(2)}) copy-start(bf16[64,2048]{1,0:T(8,128)(2,1)S(1)} %collective-permute-done.15.rest_4_) | copy-start | bytes 786436
  53.7 9.4 %collective-permute-start.12 = (bf16[128,2048]{1,0:T(8,128)(2,1)}, bf16[128,2048]{1,0:T(8,128)(2,1)S(1)}, u32[]{:S(2)}, u32[]{:S(2)}) collective-permute-start(bf16[128,2048]{1,0:T(8,128)(2,1)} %get-tuple-element.52), channel_id=1, source_target_pairs={{0,1},{1,0},{2,3},{3,2},{4,5},{5,4},{6,7},{7,6},{8,9},{9,8},{10,11... | collective-permute-start | bytes 1572872 | tf_op jit(solution)/shard_map/ppermute | solution.py:322
  54.2 2.5 %collective-permute-start.17 = (bf16[256,256]{1,0:T(8,128)(2,1)}, bf16[256,256]{1,0:T(8,128)(2,1)S(1)}, u32[]{:S(2)}, u32[]{:S(2)}) collective-permute-start(bf16[256,256]{1,0:T(8,128)(2,1)} %get-tuple-element.59), channel_id=1, source_target_pairs={{0,1},{1,0},{2,3},{3,2},{4,5},{5,4},{6,7},{7,6},{8,9},{9,8},{10,11... | collective-permute-start | bytes 393224 | tf_op jit(solution)/shard_map/ppermute | solution.py:322
  54.3 8.9 %collective-permute-start.16 = (bf16[64,2048]{1,0:T(8,128)(2,1)}, bf16[64,2048]{1,0:T(8,128)(2,1)S(1)}, u32[]{:S(2)}, u32[]{:S(2)}) collective-permute-start(bf16[64,2048]{1,0:T(8,128)(2,1)} %collective-permute-done.13.rest_2_), channel_id=1, source_target_pairs={{0,16},{16,0},{1,17},{17,1},{2,18},{18,2},{3,19},{19,3},{4,20},{20... | collective-permute-start | bytes 786440 | tf_op jit(solution)/shard_map/ppermute | solution.py:319
  58.3 5.0 %collective-permute-start.19 = (bf16[256,256]{1,0:T(8,128)(2,1)S(1)}, bf16[256,256]{1,0:T(8,128)(2,1)S(1)}, u32[]{:S(2)}, u32[]{:S(2)}) collective-permute-start(bf16[256,256]{1,0:T(8,128)(2,1)S(1)} %add.19.rest_6_), channel_id=1, source_target_pairs={{0,2},{1,3},{2,0},{3,1},{4,6},{5,7},{6,4},{7,5},{8,10},{9,11},{10,... | collective-permute-start | bytes 393224 | tf_op jit(solution)/shard_map/ppermute | solution.py:325
  (7 other events, 18.5 us)
